TPU v7x, 32 devices: a whole 2x2x4 slice. The times are simulated.
32 devices in a mesh: grp: 2 (over y), samp: 4 (over z), snp: 4 (over x, core).
Axes of the slice: x: 2, y: 2, z: 4, core: 2. Of those that a mesh axis runs over, the one named last changes fastest.
Arguments:
- genotypes: int32 [2048, 8192], P(('grp', 'samp'), 'snp'), parts along dimension 0, may hold values from 0 to 2730, as said below
- basis_cols: bfloat16 [16384, 256], P(('grp', 'snp')), parts along dimension 0, may hold values from -0.0625 to 0.0625
Outputs:
- y_block: float32 [8, 4, 512, 256], P(('grp', 'snp'), 'samp'), parts along dimension 0
- r_factor: float32 [512, 256], P('grp'), parts along dimension 0
- q_next: float32 [8, 4, 512, 256], P(('grp', 'snp'), 'samp'), parts along dimension 0
There are 2 independent parts, one for each index of `grp`. A program takes and returns all parts, laid end to end along the dimension named above; each array names one. Nothing has to cross between parts.
Inputs may be any that keep to these rules, and one draw needn't show every extreme that they name: `genotypes`: each word packs 6 dosages of 0, 1 or 2 in pairs of bits: bits 2 t and 2 t + 1 of word (w, p) hold the dosage of sample 6 w + t at SNP p, t from 0 to 5; bits 12 and up are zero.
All inputs are finite; a program needn't handle non-finite values.
Results may differ from a plain program's by a relative error of at most 0.0025.
Values may be sent and summed in bfloat16 or wider, within the bound.
No kernel may reach another device: no remote copies, remote signals or barrier semaphores. Data moves between devices by JAX's collectives and lax.ppermute only.
A program may use at most 64 MiB of HBM per device.

v0:
```python
import jax
import jax.numpy as jnp
from jax import lax
from jax.sharding import PartitionSpec as P


def unpack_counts(genotypes):
    planes = [
        jnp.bitwise_and(jnp.right_shift(genotypes, 2 * shift_pos), 3) for shift_pos in range(6)
    ]
    local_counts = planes[0].sum(axis=0)
    for plane_item in planes[1:]:
        local_counts = local_counts + plane_item.sum(axis=0)
    dosage = jnp.stack([plane_item.astype(jnp.bfloat16) for plane_item in planes], axis=1)
    dosage = dosage.reshape(genotypes.shape[0] * 6, genotypes.shape[1])
    return (dosage, local_counts)


def per_device(genotypes, basis_cols):
    dosage, local_counts = unpack_counts(genotypes)
    sample_rows, snp_cols = dosage.shape
    width = basis_cols.shape[1]
    totals = lax.psum(local_counts, "samp")
    samples = sample_rows * lax.axis_size("samp")
    allele_mean = totals.astype(jnp.float32) / jnp.float32(samples)
    center = jnp.dot(allele_mean, basis_cols.astype(jnp.float32), precision=lax.Precision.HIGHEST)
    inv_root = jnp.float32(1.0) / jnp.sqrt(jnp.float32(samples))
    contract_rows = (((0,), (0,)), ((), ()))
    product_term = jnp.dot(dosage, basis_cols, preferred_element_type=jnp.float32) - center[None, :]
    score_rows = lax.psum(product_term, "snp").astype(jnp.bfloat16)
    y_local = lax.psum_scatter(
        lax.dot_general(dosage, score_rows, contract_rows, preferred_element_type=jnp.float32)
        * inv_root,
        "samp",
        scatter_dimension=0,
        tiled=True,
    )
    snp_total = snp_cols * lax.axis_size("snp")
    local_gram = jnp.dot(y_local.T, y_local, precision=lax.Precision.HIGHEST) / jnp.float32(
        snp_total
    )
    gram_sum = lax.psum(local_gram, ("samp", "snp"))
    lower_factor = jnp.linalg.cholesky(gram_sum)
    q_next = lax.linalg.triangular_solve(
        lower_factor, y_local, left_side=False, lower=True, transpose_a=True
    )
    layout = (1, 1, y_local.shape[0], width)
    return (y_local.reshape(layout), lower_factor.T, q_next.reshape(layout))


def solution(mesh):
    return jax.shard_map(
        per_device,
        mesh=mesh,
        in_specs=(P(("grp", "samp"), "snp"), P(("grp", "snp"), None)),
        out_specs=(
            P(("grp", "snp"), "samp", None, None),
            P("grp", None),
            P(("grp", "snp"), "samp", None, None),
        ),
        check_vma=False,
    )
```

profile of v0, /device:TPU:0, one launch (start us, length us, event | category | flops | bytes accessed | tf_op | source)
XLA Modules:
  0.0 290.9 jit_solution(1570081549035918999)
XLA Ops:
  7.2 0.0 copy-start
  7.2 0.0 copy-start.1
  7.2 0.0 reduce-scatter.2.cloned.1.call-start
  7.2 2.0 fusion.23
  9.2 0.3 copy-done.1
  9.5 1.2 fusion.2
  10.7 0.3 fusion.21
  11.0 0.3 fusion.19
  11.3 0.3 fusion.17
  11.5 0.3 fusion.15
  11.8 0.3 fusion.13
  12.1 6.9 %copy.9 = bf16[256,6,2048]{2,1,0:T(8,128)(2,1)} copy(bf16[256,6,2048]{2,0,1:T(8,128)(2,1)S(1)} %fusion.13) | data formatting | bytes 12582912 | tf_op jit(solution)/shard_map/stack | solution.py:14
  18.9 11.1 %reshape.33 = bf16[1536,2048]{1,0:T(8,128)(2,1)} reshape(bf16[256,6,2048]{2,1,0:T(8,128)(2,1)} %copy.9) | data formatting | bytes 12582912 | tf_op jit(solution)/shard_map/reshape | solution.py:15
  30.0 10.0 %psum.21 = s32[2048]{0:T(1024)S(1)} all-reduce(s32[2048]{0:T(1024)S(1)} %add_add_fusion), channel_id=1, replica_groups=mesh['grp'=2,'samp'=4,'snp'=4] {'samp'}, use_global_device_ids=true, to_apply=%region_6.0 | all-reduce | flops 2048 | bytes 16384 | tf_op jit(solution)/shard_map/psum | solution.py:23
  40.0 0.0 copy-done
  40.0 0.5 fusion.36
  40.5 4.6 %convolution_subtract_fusion = f32[1536,256]{1,0:T(8,128)S(1)} fusion(bf16[1536,2048]{1,0:T(8,128)(2,1)} %reshape.33, bf16[2048,256]{1,0:T(8,128)(2,1)S(1)} %copy-done, f32[256]{0:T(256)S(1)} %bitcast.72), kind=kOutput, calls=%fused_computation.3 | convolution fusion | flops 1611005952 | bytes 8913920 | tf_op jit(solution)/shard_map/dot_general | solution.py:29
  45.1 32.6 %all-reduce.5 = bf16[1536,256]{1,0:T(8,128)(2,1)S(1)} all-reduce(f32[1536,256]{1,0:T(8,128)S(1)} %convolution_subtract_fusion), channel_id=1, replica_groups=mesh['grp'=2,'samp'=4,'snp'=4] {'snp'}, use_global_device_ids=true, to_apply=%region_7.0 | all-reduce | flops 393216 | bytes 2359296 | tf_op jit(solution)/shard_map/psum | solution.py:30
  77.7 6.0 %convolution_multiply_fusion = f32[2048,256]{1,0:T(8,128)} fusion(bf16[1536,2048]{1,0:T(8,128)(2,1)} %reshape.33, bf16[1536,256]{1,0:T(8,128)(2,1)S(1)} %all-reduce.5), kind=kOutput, calls=%fused_computation.2 | convolution fusion | flops 1611137024 | bytes 9175040 | tf_op jit(solution)/shard_map/dot_general | solution.py:32
  83.8 0.0 reduce-scatter.2.cloned.1.call-update
  83.8 0.0 all-reduce.4.cloned.1.call-start
  83.9 42.6 %reduce-scatter.2.cloned.1.call-done = f32[512,256]{1,0:T(8,128)} async-done(((f32[2048,256]{1,0:T(8,128)}), f32[512,256]{1,0:T(8,128)}) %reduce-scatter.2.cloned.1.call-update) | async-done | bytes 524304 | tf_op jit(solution)/shard_map/reduce_scatter | solution.py:31
  126.5 2.9 convolution_multiply_fusion.1
  129.4 0.0 all-reduce.4.cloned.1.call-update
  129.4 89.5 %all-reduce.4.cloned.1.call-done = f32[256,256]{0,1:T(8,128)} async-done(((f32[256,256]{0,1:T(8,128)}), f32[256,256]{0,1:T(8,128)}) %all-reduce.4.cloned.1.call-update) | async-done | bytes 262160 | tf_op jit(solution)/shard_map/psum | solution.py:42
  218.9 1.1 copy.11
  220.0 0.0 copy-start.2
  220.0 1.0 fusion.27
  221.1 11.7 %cholesky.50 = f32[128,128]{1,0:T(8,128)S(1)} custom-call(f32[128,128]{1,0:T(8,128)S(1)} %cholesky.118), custom_call_target="Cholesky" | custom-call | tf_op jit(solution)/shard_map/jit(cholesky)/cholesky | solution.py:43
  232.9 9.8 %custom-call.14 = f32[1,128,128]{1,2,0:T(8,128)S(1)} custom-call(f32[1,128,128]{2,1,0:T(8,128)S(1)} %get-tuple-element.38), custom_call_target="InvertDiagBlocksLowerTriangular" | custom-call | tf_op jit(solution)/shard_map/jit(cholesky)/cholesky | solution.py:43
  242.7 0.2 constant_dynamic-update-slice_fusion.1
  242.9 0.3 convolution_subtract_fusion.2
  243.2 11.7 %cholesky.105 = f32[128,128]{1,0:T(8,128)S(1)} custom-call(f32[128,128]{1,0:T(8,128)S(1)} %convolution_subtract_fusion.2), custom_call_target="Cholesky" | custom-call | tf_op jit(solution)/shard_map/jit(cholesky)/cholesky | solution.py:43
  254.9 0.6 compare_reduce_fusion
  256.9 0.8 copy.12
  257.7 0.1 triangular_solve.43
  257.8 4.1 %while.1 = (s32[]{:T(128)}, f32[256,256]{1,0:T(8,128)S(1)}, s32[2,2]{1,0:T(2,128)S(1)}, f32[2,128,128]{2,1,0:T(8,128)S(1)}, s32[]{:T(128)}) while((s32[]{:T(128)}, f32[256,256]{1,0:T(8,128)S(1)}, s32[2,2]{1,0:T(2,128)S(1)}, f32[2,128,128]{2,1,0:T(8,128)S(1)}, s32[]{:T(128)}) %tuple.35), condition=%wide.while_cond, body=%wide.while_body.sunk | while | flops 2 | bytes 131189 | solution.py:44
  257.8 0.6 fusion.50
  258.4 1.4 bitcast_dynamic-update-slice_fusion.2
  259.9 0.6 fusion.50
  260.5 1.4 bitcast_dynamic-update-slice_fusion.2
  261.9 19.7 %custom-call.15 = f32[2,128,128]{1,2,0:T(8,128)S(1)} custom-call(f32[2,128,128]{2,1,0:T(8,128)S(1)} %get-tuple-element.10), custom_call_target="InvertDiagBlocksLowerTriangular" | custom-call | tf_op jit(solution)/shard_map/triangular_solve | solution.py:44
  281.6 0.0 copy-done.2
  281.6 0.4 fusion.25
  282.0 0.6 convolution_subtract_fusion.1
  282.6 0.4 fusion.30
  283.1 1.0 copy.13
  (12 shorter events, 0.2 us)
Async XLA Ops:
  7.2 32.9 %copy-start = (bf16[2048,256]{1,0:T(8,128)(2,1)S(1)}, bf16[2048,256]{1,0:T(8,128)(2,1)}, u32[]{:S(2)}) copy-start(bf16[2048,256]{1,0:T(8,128)(2,1)} %param.3) | copy-start | bytes 3145732
  7.2 2.3 copy-start.1
  7.2 119.3 %reduce-scatter.2.cloned.1.call-start = ((), (), s32[]{:S(2)}) async-start(), calls=%async_computation.1 | async-start | bytes 2621440 | tf_op jit(solution)/shard_map/reduce_scatter | solution.py:31
  83.8 135.1 %all-reduce.4.cloned.1.call-start = ((), (), s32[]{:S(2)}) async-start(), calls=%async_computation.2 | async-start | bytes 524288 | tf_op jit(solution)/shard_map/psum | solution.py:42
  220.0 61.6 %copy-start.2 = (f32[512,256]{1,0:T(8,128)S(1)}, f32[512,256]{1,0:T(8,128)}, u32[]{:S(2)}) copy-start(f32[512,256]{1,0:T(8,128)} %reduce-scatter.2.cloned.1.call-done) | copy-start | bytes 1572868
Sparse Core Ops, SparseCore 0:
  83.9 42.5 reduce-scatter.1
  130.8 88.0 all-reduce.3
where the time goes:
time: 292 us; the launch traced here: 291 us
  waiting for transfers between devices  132 us (45%)
  other arithmetic  59.3 us (20%)
  blocking collectives  42.6 us (15%)
  local copies, waits for them, and re-layouts  25.3 us (9%)
  matrix products  15.9 us (5%)
  between operations  15.6 us (5%)
    psum x1, waiting for transfers between devices, per_device(): gram_sum = lax.psum(local_gram, ('samp', 'snp'))  89.5 us
    reduce_scatter x1, waiting for transfers between devices, per_device(): lax.psum_scatter(lax.dot_general(dosage, score_rows, contract_rows, prefe...  42.6 us
    another operation x6, other arithmetic, per_device(): lower_factor = jnp.linalg.cholesky(gram_sum)  33.9 us
    psum x1, blocking collectives, per_device(): score_rows = lax.psum(product_term, 'snp').astype(jnp.bfloat16)  32.6 us
    another operation x3, other arithmetic, per_device(): lax.linalg.triangular_solve(lower_factor, y_local, left_side=False, lower...  19.7 us
    reshape x1, local copies, waits for them, and re-layouts, unpack_counts(): dosage = dosage.reshape(genotypes.shape[0] * 6, genotypes.shape[1])  11.1 us
    psum x1, blocking collectives, per_device(): totals = lax.psum(local_counts, 'samp')  10 us
    another operation x1, local copies, waits for them, and re-layouts, unpack_counts(): jnp.stack([plane_item.astype(jnp.bfloat16) for plane_item in planes], axi...  6.86 us
  transfers between devices with their start and end apart: 2, of which 2 were waited for; matrix products, arithmetic and copies ran while one was open for 0% of the time, Pallas kernels for 0%

commit v1 on v0

v1 whole, which is shorter than its diff:
```python
import functools

import jax
import jax.numpy as jnp
from jax import lax
from jax.experimental import pallas as pl
from jax.experimental.pallas import tpu as pltpu
from jax.sharding import PartitionSpec as P

PLANES = 6
STEPS = 64.0
TOP = 32767.0
HIGH = lax.Precision.HIGHEST
VMEM_BYTES = 40 * 1024 * 1024


def params(**more):
    return pltpu.CompilerParams(vmem_limit_bytes=VMEM_BYTES, **more)


def planes_of(words):
    return [
        jnp.bitwise_and(jnp.right_shift(words, 2 * t), 3).astype(jnp.float32).astype(jnp.bfloat16)
        for t in range(PLANES)
    ]


def project_kernel(pick, words, basis, out, sums):
    blocks, _, depth, _ = out.shape
    total = jnp.zeros(sums.shape, jnp.float32)
    for t, plane in enumerate(planes_of(words[...])):
        product = jnp.dot(plane, basis[...], preferred_element_type=jnp.float32)
        for b in range(blocks):
            out[b, t] = product[b * depth : (b + 1) * depth]
        total = total + product.reshape(-1, 8, product.shape[1]).sum(axis=0)
    sums[...] = total


def project(words, basis, pick, blocks):
    count, snps = words.shape
    width = basis.shape[1]
    half = count // 2
    depth = half // blocks
    return pl.pallas_call(
        project_kernel,
        grid_spec=pltpu.PrefetchScalarGridSpec(
            num_scalar_prefetch=1,
            grid=(1,),
            in_specs=[
                pl.BlockSpec((half, snps), lambda i, pick: (pick[0], 0)),
                pl.BlockSpec((snps, width), lambda i, pick: (0, 0)),
            ],
            out_specs=[
                pl.BlockSpec((blocks, PLANES, depth, width), lambda i, pick: (0, 0, 0, 0)),
                pl.BlockSpec((8, width), lambda i, pick: (0, 0)),
            ],
        ),
        out_shape=[
            jax.ShapeDtypeStruct((blocks, PLANES, depth, width), jnp.float32),
            jax.ShapeDtypeStruct((8, width), jnp.float32),
        ],
        compiler_params=params(),
        name="project",
        cost_estimate=pl.CostEstimate(
            flops=2 * half * PLANES * snps * width,
            bytes_accessed=4 * half * snps + 2 * snps * width + 4 * half * PLANES * width,
            transcendentals=0,
        ),
    )(pick, words, basis)


def bit_reverse(index, bits):
    out = 0
    for b in range(bits):
        out |= ((index >> b) & 1) << (bits - 1 - b)
    return out


def back_project(words, scores, scale):
    blocks = scores.shape[0]
    bits = blocks.bit_length() - 1
    total = None
    for t, plane in enumerate(planes_of(words)):
        rows = jnp.concatenate([scores[bit_reverse(b, bits), t] for b in range(blocks)], axis=0)
        term = lax.dot_general(
            rows, plane, (((0,), (0,)), ((), ())), preferred_element_type=jnp.float32
        )
        total = term if total is None else total + term
    return (total * scale).T


def sent_kernel(scale, pick, words, scores, out):
    value = back_project(words[...], scores, scale)
    rows = value.shape[0]
    top = jnp.maximum(jnp.max(jnp.abs(value), axis=0, keepdims=True), 1e-30)
    level = jnp.ceil(STEPS * jnp.log2(top / TOP)) + 1.0
    unit = jnp.exp2(level * (1.0 / STEPS))
    coded = jnp.clip(jnp.round(value * (1.0 / unit)), -TOP, TOP)
    out[:rows] = coded.astype(jnp.int32).astype(jnp.int16)
    out[rows:] = jnp.broadcast_to(level, (16, level.shape[1])).astype(jnp.int32).astype(jnp.int16)


def kept_kernel(scale, pick, words, scores, out):
    out[...] = back_project(words[...], scores, scale)


def chunk_of_y(words, scores, pick, rows, scale, sent):
    count, snps = words.shape
    width = scores.shape[-1]
    shape = (rows + 16, width) if sent else (rows, width)
    dtype = jnp.int16 if sent else jnp.float32
    return pl.pallas_call(
        functools.partial(sent_kernel if sent else kept_kernel, scale),
        grid_spec=pltpu.PrefetchScalarGridSpec(
            num_scalar_prefetch=1,
            grid=(1,),
            in_specs=[
                pl.BlockSpec((count, rows), lambda i, pick: (0, pick[0])),
                pl.BlockSpec(scores.shape, lambda i, pick: (0, 0, 0, 0)),
            ],
            out_specs=pl.BlockSpec(shape, lambda i, pick: (0, 0)),
        ),
        out_shape=jax.ShapeDtypeStruct(shape, dtype),
        compiler_params=params(),
        name="chunk_sent" if sent else "chunk_kept",
        cost_estimate=pl.CostEstimate(
            flops=2 * count * PLANES * rows * width,
            bytes_accessed=4 * count * rows + 2 * scores.size + 4 * rows * width,
            transcendentals=0,
        ),
    )(pick, words, scores)


def collect_kernel(scale, *refs):
    kept, out, gram = refs[0], refs[-2], refs[-1]
    rows = kept.shape[0]
    total = kept[...]
    for ref in refs[1:-2]:
        level = ref[rows : rows + 16].astype(jnp.int32).astype(jnp.float32)[:1]
        unit = jnp.exp2(level * (1.0 / STEPS))
        total = total + ref[:rows].astype(jnp.int32).astype(jnp.float32) * unit
    out[...] = total
    gram[...] = scale * lax.dot_general(
        total, total, (((0,), (0,)), ((), ())), precision=HIGH, preferred_element_type=jnp.float32
    )


def collect(kept, received, scale):
    width = kept.shape[1]
    return pl.pallas_call(
        functools.partial(collect_kernel, scale),
        out_shape=[
            jax.ShapeDtypeStruct(kept.shape, jnp.float32),
            jax.ShapeDtypeStruct((width, width), jnp.float32),
        ],
        compiler_params=params(),
        name="collect",
    )(kept, *received)


def swap(array, axis, mask):
    size = lax.axis_size(axis)
    return lax.ppermute(array, axis, [(i, i ^ mask) for i in range(size)])


def halve(array, axis, mask):
    bit = (lax.axis_index(axis) & mask) // mask
    mine = lax.dynamic_index_in_dim(array, bit, 0, keepdims=False)
    other = lax.dynamic_index_in_dim(array, 1 - bit, 0, keepdims=False)
    return mine, swap(other, axis, mask)


def gram_total(gram):
    width = gram.shape[0]
    n_snp, n_samp = lax.axis_size("snp"), lax.axis_size("samp")
    if n_snp != 4 or n_samp != 4:
        return lax.psum(gram, ("samp", "snp"))
    mine, got = halve(gram.reshape(2, width // 2, width), "snp", 1)
    part = mine + got
    mine, got = halve(part.reshape(2, width // 4, width), "snp", 2)
    part = mine + got
    part = ((part + swap(part, "samp", 1)) + (swap(part, "samp", 2) + swap(part, "samp", 3)))
    x_bit = (lax.axis_index("snp") // 2) == 0
    c_bit = (lax.axis_index("snp") % 2) == 0
    got = swap(part, "snp", 2)
    part = jnp.concatenate([jnp.where(x_bit, part, got), jnp.where(x_bit, got, part)], axis=0)
    got = swap(part, "snp", 1)
    return jnp.concatenate([jnp.where(c_bit, part, got), jnp.where(c_bit, got, part)], axis=0)


def per_device(genotypes, basis_cols):
    n_snp, n_samp = lax.axis_size("snp"), lax.axis_size("samp")
    bits = n_snp.bit_length() - 1
    words, snps = genotypes.shape
    width = basis_cols.shape[1]
    samples = words * PLANES * n_samp
    inv_root = float(1.0 / samples**0.5)
    blocks = n_snp // 2
    depth = words // n_snp
    me = lax.axis_index("snp")
    low = (me & 1).astype(jnp.int32)

    other, other_sums = project(genotypes, basis_cols, (1 - low)[None], blocks)
    got = swap(other, "snp", 1)
    mine, mine_sums = project(genotypes, basis_cols, low[None], blocks)
    part = mine + got
    sums = mine_sums + other_sums
    for b in range(1, bits):
        shape = (2, part.shape[0] // 2) + part.shape[1:]
        keep, got = halve(part.reshape(shape), "snp", 1 << b)
        part = keep + got
    if n_snp * n_samp <= 16:
        every = jnp.broadcast_to(sums[None], (n_snp * n_samp,) + sums.shape)
        center = lax.all_to_all(every, ("samp", "snp"), 0, 0, tiled=True).sum(axis=(0, 1))
    else:
        center = lax.psum(sums, ("samp", "snp")).sum(axis=0)
    center = center / jnp.float32(samples)
    rows = (part.reshape(PLANES * depth, width) - center[None, :]).astype(jnp.bfloat16)
    scores = lax.all_gather(rows, "snp").reshape(n_snp, PLANES, depth, width)

    chunk = snps // n_samp
    z = lax.axis_index("samp").astype(jnp.int32)
    total_snps = snps * n_snp
    if n_samp <= 4 and chunk % 128 == 0:
        received = []
        for mask in range(n_samp - 1, 0, -1):
            coded = chunk_of_y(genotypes, scores, (z ^ mask)[None], chunk, inv_root, True)
            received.append(swap(coded, "samp", mask))
        kept = chunk_of_y(genotypes, scores, z[None], chunk, inv_root, False)
        y_local, gram = collect(kept, received, 1.0 / total_snps)
    else:
        tile = 512 if snps % 512 == 0 else snps
        parts = [
            chunk_of_y(genotypes, scores, jnp.full((1,), i, jnp.int32), tile, inv_root, False)
            for i in range(snps // tile)
        ]
        y_local = lax.psum_scatter(
            jnp.concatenate(parts, axis=0), "samp", scatter_dimension=0, tiled=True
        )
        y_local, gram = collect(y_local, [], 1.0 / total_snps)
    gram_sum = gram_total(gram)
    lower_factor = jnp.linalg.cholesky(gram_sum)
    q_next = lax.linalg.triangular_solve(
        lower_factor, y_local, left_side=False, lower=True, transpose_a=True
    )
    layout = (1, 1, y_local.shape[0], width)
    return (y_local.reshape(layout), lower_factor.T, q_next.reshape(layout))


def solution(mesh):
    return jax.shard_map(
        per_device,
        mesh=mesh,
        in_specs=(P(("grp", "samp"), "snp"), P(("grp", "snp"), None)),
        out_specs=(
            P(("grp", "snp"), "samp", None, None),
            P("grp", None),
            P(("grp", "snp"), "samp", None, None),
        ),
        check_vma=False,
    )
```

time: 292 us -> 160 us (0.55)
  waiting for transfers between devices: 132 us -> 48.8 us
  blocking collectives: 42.6 us -> 8.69 us
  starting transfers between devices: 0.08 us -> 20.1 us
  local copies, waits for them, and re-layouts: 25.3 us -> 10.6 us
  matrix products: 15.9 us -> 1.91 us
  between operations: 15.6 us -> 2.28 us
  Pallas kernels: 0 us -> 10.3 us
    psum x1 -> x0, waiting for transfers between devices: 89.5 us -> none  [per_device(): gram_sum = lax.psum(local_gram, ('samp', 'snp'))]
    ppermute x0 -> x12, waiting for transfers between devices: none -> 45 us  [swap(): return lax.ppermute(array, axis, [(i, i ^ mask) for i in range(size)])]
    reduce_scatter x1 -> x0, waiting for transfers between devices: 42.6 us -> none  [per_device(): lax.psum_scatter(lax.dot_general(dosage, score_rows, contract_rows, prefe...]
    psum x2 -> x0, blocking collectives: 42.6 us -> none  [the longest x1 32.6 us: per_device(): score_rows = lax.psum(product_term, 'snp').astype(jnp.bfloat16)]
    dot_general x4 -> x0, matrix products: 14.1 us -> none  [the longest x1 6.05 us: per_device(): lax.dot_general(dosage, score_rows, contract_rows, preferred_element_type...]
    ppermute x0 -> x12, starting transfers between devices: none -> 13.1 us  [swap(): return lax.ppermute(array, axis, [(i, i ^ mask) for i in range(size)])]
    reshape x1 -> x0, local copies, waits for them, and re-layouts: 11.1 us -> none  [unpack_counts(): dosage = dosage.reshape(genotypes.shape[0] * 6, genotypes.shape[1])]
    pallas_call x0 -> x7, Pallas kernels: none -> 10.3 us  [the longest x4 5.36 us: chunk_of_y(): pl.pallas_call(functools.partial(sent_kernel if sent else kept_kernel, sc...]
  transfers between devices with their start and end apart: 2 -> 13, of which waited for: 2 -> 10; matrix products, arithmetic and copies ran while one was open for 0% -> 1% of each run, Pallas kernels for 0% -> 3%
where the time goes in v1:
time: 160 us; the launch traced here: 159 us
  other arithmetic  56.6 us (35%)
  waiting for transfers between devices  48.8 us (30%)
  starting transfers between devices  20.1 us (13%)
  local copies, waits for them, and re-layouts  10.6 us (7%)
  Pallas kernels  10.3 us (6%)
  blocking collectives  8.69 us (5%)
  between operations  2.28 us (1%)
  matrix products  1.91 us (1%)
    ppermute x12, waiting for transfers between devices, swap(): return lax.ppermute(array, axis, [(i, i ^ mask) for i in range(size)])  45 us
    another operation x6, other arithmetic, per_device(): lower_factor = jnp.linalg.cholesky(gram_sum)  34.1 us
    another operation x3, other arithmetic, per_device(): lax.linalg.triangular_solve(lower_factor, y_local, left_side=False, lower...  19.7 us
    ppermute x12, starting transfers between devices, swap(): return lax.ppermute(array, axis, [(i, i ^ mask) for i in range(size)])  13.1 us
    all_gather x1, blocking collectives, per_device(): scores = lax.all_gather(rows, 'snp').reshape(n_snp, PLANES, depth, width)  8.69 us
    all_to_all x1, starting transfers between devices, per_device(): lax.all_to_all(every, ('samp', 'snp'), 0, 0, tiled=True).sum(axis=(0, 1))  7.02 us
    unnamed x12, local copies, waits for them, and re-layouts  5.54 us
    pallas_call x4, Pallas kernels, chunk_of_y(): pl.pallas_call(functools.partial(sent_kernel if sent else kept_kernel, sc...  5.36 us
  transfers between devices with their start and end apart: 13, of which 10 were waited for; matrix products, arithmetic and copies ran while one was open for 1% of the time, Pallas kernels for 3%

profile of v1, /device:TPU:0, one launch (start us, length us, event | category | flops | bytes accessed | tf_op | source)
XLA Modules:
  0.0 159.3 jit_solution(17360116345257905894)
XLA Ops:
  0.6 1.6 copy-done
  2.2 1.2 copy-done.2
  3.5 1.9 %project.3 = (f32[2,6,64,256]{3,2,1,0:T(8,128)}, f32[8,256]{1,0:T(8,128)S(1)}) custom-call(s32[1]{0:T(128)} %bitcast.2.pick, s32[256,2048]{1,0:T(8,128)S(1)} %copy-done, bf16[2048,256]{1,0:T(8,128)(2,1)S(1)} %copy-done.2), custom_call_target="tpu_custom_call" | custom-call | flops 805306368 | bytes 2883584 | tf_op jit(solution)/shard_map/project/pallas_call | solution.py:44
  5.3 0.5 collective-permute-start
  5.8 1.1 project.2
  6.9 0.7 broadcast_in_dim.30
  7.5 7.0 %all-to-all-start = ((f32[16,8,256]{2,1,0:T(8,128)}), f32[16,8,256]{2,1,0:T(8,128)S(1)}, u32[]{:S(2)}, u32[]{:S(2)}) async-start(f32[16,8,256]{2,1,0:T(8,128)} %broadcast_in_dim.30), calls=%async_computation | async-start | bytes 262144 | tf_op jit(solution)/shard_map/all_to_all | solution.py:214
  14.6 1.2 add.72
  15.9 0.9 copy-done.3
  16.8 2.0 %collective-permute-start.1 = (f32[1,6,64,256]{3,2,1,0:T(8,128)S(1)}, f32[1,6,64,256]{3,2,1,0:T(8,128)S(1)}, u32[]{:S(2)}, u32[]{:S(2)}) collective-permute-start(f32[1,6,64,256]{3,2,1,0:T(8,128)S(1)} %constant_dynamic-slice_fusion.3), channel_id=1, source_target_pairs={{0,2},{1,3},{2,0},{3,1},{4,6},{5,7},{6,4},{7,5},{8,10},{9,11},{10,... | collective-permute-start | bytes 1179656 | tf_op jit(solution)/shard_map/ppermute | solution.py:163
  18.7 3.8 %all-to-all-done = f32[16,8,256]{2,1,0:T(8,128)S(1)} async-done(((f32[16,8,256]{2,1,0:T(8,128)}), f32[16,8,256]{2,1,0:T(8,128)S(1)}, u32[]{:S(2)}, u32[]{:S(2)}) %all-to-all-start) | async-done | bytes 131104 | tf_op jit(solution)/shard_map/all_to_all | solution.py:214
  22.6 6.3 %collective-permute-done.1 = f32[1,6,64,256]{3,2,1,0:T(8,128)S(1)} collective-permute-done((f32[1,6,64,256]{3,2,1,0:T(8,128)S(1)}, f32[1,6,64,256]{3,2,1,0:T(8,128)S(1)}, u32[]{:S(2)}, u32[]{:S(2)}) %collective-permute-start.1) | collective-permute-done | bytes 393248 | tf_op jit(solution)/shard_map/ppermute | solution.py:163
  28.9 1.0 dynamic-slice_add_fusion
  29.9 8.7 %all_gather.4 = bf16[4,384,256]{2,1,0:T(8,128)(2,1)S(1)} all-gather(bf16[1,384,256]{2,1,0:T(8,128)(2,1)S(1)} %fusion), channel_id=1, replica_groups=mesh['grp'=2,'samp'=4,'snp'=4] {'snp'}, dimensions={0}, use_global_device_ids=true | all-gather | bytes 983040 | tf_op jit(solution)/shard_map/all_gather | solution.py:219
  38.6 1.5 chunk_sent.3
  40.2 2.9 %collective-permute-start.2 = (s16[528,256]{1,0:T(8,128)(2,1)}, s16[528,256]{1,0:T(8,128)(2,1)S(1)}, u32[]{:S(2)}, u32[]{:S(2)}) collective-permute-start(s16[528,256]{1,0:T(8,128)(2,1)} %chunk_sent.3), channel_id=1, source_target_pairs={{0,12},{4,8},{8,4},{12,0},{1,13},{5,9},{9,5},{13,1},{2,14},{6,10},... | collective-permute-start | bytes 811016 | tf_op jit(solution)/shard_map/ppermute | solution.py:163
  43.1 1.5 chunk_sent.4
  44.6 1.5 chunk_sent.5
  46.2 1.5 collective-permute-start.4
  47.6 0.7 chunk_kept.1.refs_0_
  48.4 3.2 %collective-permute-done.2.refs_1_ = s16[528,256]{1,0:T(8,128)(2,1)S(1)} collective-permute-done((s16[528,256]{1,0:T(8,128)(2,1)}, s16[528,256]{1,0:T(8,128)(2,1)S(1)}, u32[]{:S(2)}, u32[]{:S(2)}) %collective-permute-start.2) | collective-permute-done | bytes 270368 | tf_op jit(solution)/shard_map/ppermute | solution.py:163
  51.6 15.6 %collective-permute-done.3.refs_2_ = s16[528,256]{1,0:T(8,128)(2,1)S(1)} collective-permute-done((s16[528,256]{1,0:T(8,128)(2,1)}, s16[528,256]{1,0:T(8,128)(2,1)S(1)}, u32[]{:S(2)}, u32[]{:S(2)}) %collective-permute-start.3) | collective-permute-done | bytes 270368 | tf_op jit(solution)/shard_map/ppermute | solution.py:163
  67.2 2.0 %collect.1 = (f32[512,256]{1,0:T(8,128)}, f32[256,256]{1,0:T(8,128)S(1)}) custom-call(f32[512,256]{1,0:T(8,128)S(1)} %chunk_kept.1.refs_0_, s16[528,256]{1,0:T(8,128)(2,1)S(1)} %collective-permute-done.2.refs_1_, s16[528,256]{1,0:T(8,128)(2,1)S(1)} %collective-permute-done.3.refs_2_, s16[528,256]{1,0:T(8,128)(2,1)} %collective-permute-done.4.refs_3_), custom_call_target="tpu_custom_call" | custom-call | tf_op jit(solution)/shard_map/collect/pallas_call | solution.py:150
  69.3 1.3 collective-permute-done.5
  70.8 0.8 collective-permute-start.6
  71.7 4.7 %collective-permute-done.6 = f32[64,256]{0,1:T(8,128)S(1)} collective-permute-done((f32[64,256]{0,1:T(8,128)S(1)}, f32[64,256]{0,1:T(8,128)S(1)}, u32[]{:S(2)}, u32[]{:S(2)}) %collective-permute-start.6) | collective-permute-done | bytes 65568 | tf_op jit(solution)/shard_map/ppermute | solution.py:163
  76.5 2.7 %collective-permute-start.8 = (f32[64,256]{0,1:T(8,128)S(1)}, f32[64,256]{0,1:T(8,128)S(1)}, u32[]{:S(2)}, u32[]{:S(2)}) collective-permute-start(f32[64,256]{0,1:T(8,128)S(1)} %bitcast_add_fusion.1), channel_id=1, source_target_pairs={{0,8},{4,12},{8,0},{12,4},{1,9},{5,13},{9,1},{13,5},{2,10},{6,14},... | collective-permute-start | bytes 196616 | tf_op jit(solution)/shard_map/ppermute | solution.py:163
  79.3 1.6 %collective-permute-start.9 = (f32[64,256]{0,1:T(8,128)S(1)}, f32[64,256]{0,1:T(8,128)S(1)}, u32[]{:S(2)}, u32[]{:S(2)}) collective-permute-start(f32[64,256]{0,1:T(8,128)S(1)} %bitcast_add_fusion.1), channel_id=1, source_target_pairs={{0,12},{4,8},{8,4},{12,0},{1,13},{5,9},{9,5},{13,1},{2,14},{6,10},... | collective-permute-start | bytes 196616 | tf_op jit(solution)/shard_map/ppermute | solution.py:163
  80.9 2.2 %collective-permute-done.7 = f32[64,256]{0,1:T(8,128)S(1)} collective-permute-done((f32[64,256]{0,1:T(8,128)S(1)}, f32[64,256]{0,1:T(8,128)S(1)}, u32[]{:S(2)}, u32[]{:S(2)}) %collective-permute-start.7) | collective-permute-done | bytes 65568 | tf_op jit(solution)/shard_map/ppermute | solution.py:163
  83.1 6.2 %collective-permute-done.8 = f32[64,256]{0,1:T(8,128)S(1)} collective-permute-done((f32[64,256]{0,1:T(8,128)S(1)}, f32[64,256]{0,1:T(8,128)S(1)}, u32[]{:S(2)}, u32[]{:S(2)}) %collective-permute-start.8) | collective-permute-done | bytes 65568 | tf_op jit(solution)/shard_map/ppermute | solution.py:163
  89.3 0.8 collective-permute-start.10
  90.1 4.2 %collective-permute-done.10 = f32[64,256]{0,1:T(8,128)S(1)} collective-permute-done((f32[64,256]{0,1:T(8,128)S(1)}, f32[64,256]{0,1:T(8,128)S(1)}, u32[]{:S(2)}, u32[]{:S(2)}) %collective-permute-start.10) | collective-permute-done | bytes 65568 | tf_op jit(solution)/shard_map/ppermute | solution.py:163
  94.6 1.3 collective-permute-done.11
  96.2 11.7 %cholesky.50 = f32[128,128]{1,0:T(8,128)S(1)} custom-call(f32[128,128]{1,0:T(8,128)S(1)} %cholesky.118), custom_call_target="Cholesky" | custom-call | tf_op jit(solution)/shard_map/jit(cholesky)/cholesky | solution.py:242
  108.0 9.8 %custom-call.14 = f32[1,128,128]{1,2,0:T(8,128)S(1)} custom-call(f32[1,128,128]{2,1,0:T(8,128)S(1)} %get-tuple-element.56), custom_call_target="InvertDiagBlocksLowerTriangular" | custom-call | tf_op jit(solution)/shard_map/jit(cholesky)/cholesky | solution.py:242
  118.3 11.9 %cholesky.105 = f32[128,128]{1,0:T(8,128)S(1)} custom-call(f32[128,128]{1,0:T(8,128)S(1)} %convolution_subtract_fusion), custom_call_target="Cholesky" | custom-call | tf_op jit(solution)/shard_map/jit(cholesky)/cholesky | solution.py:242
  130.2 0.6 compare_reduce_fusion
  132.3 4.0 %while.1 = (s32[]{:T(128)}, f32[256,256]{1,0:T(8,128)S(1)}, s32[2,2]{1,0:T(2,128)S(1)}, f32[2,128,128]{2,1,0:T(8,128)S(1)}, s32[]{:T(128)}) while((s32[]{:T(128)}, f32[256,256]{1,0:T(8,128)S(1)}, s32[2,2]{1,0:T(2,128)S(1)}, f32[2,128,128]{2,1,0:T(8,128)S(1)}, s32[]{:T(128)}) %tuple.35), condition=%wide.while_cond, body=%wide.while_body.sunk | while | flops 2 | bytes 131181 | solution.py:243
  132.3 0.6 fusion.19
  132.9 1.4 bitcast_dynamic-update-slice_fusion.2
  134.3 0.6 fusion.19
  134.9 1.4 bitcast_dynamic-update-slice_fusion.2
  136.3 19.7 %custom-call.15 = f32[2,128,128]{1,2,0:T(8,128)S(1)} custom-call(f32[2,128,128]{2,1,0:T(8,128)S(1)} %get-tuple-element.22), custom_call_target="InvertDiagBlocksLowerTriangular" | custom-call | tf_op jit(solution)/shard_map/triangular_solve | solution.py:243
  156.0 0.4 fusion.5
  156.4 0.6 fusion.9
  157.0 0.4 fusion.2
  157.5 1.0 copy.22
  158.5 0.8 copy.21
  (45 shorter events, 1.7 us)
Async XLA Ops:
  0.6 1.6 copy-start
  2.2 1.2 copy-start.2
  3.5 2.3 %copy-start.1 = (s32[256,2048]{1,0:T(8,128)S(1)}, s32[256,2048]{1,0:T(8,128)}, u32[]{:S(2)}) copy-start(s32[256,2048]{1,0:T(8,128)} %words.11) | copy-start | bytes 6291460
  5.3 9.3 %collective-permute-start = (f32[2,6,64,256]{3,2,1,0:T(8,128)}, f32[2,6,64,256]{3,2,1,0:T(8,128)}, u32[]{:S(2)}, u32[]{:S(2)}) collective-permute-start(f32[2,6,64,256]{3,2,1,0:T(8,128)} %get-tuple-element.10), channel_id=1, source_target_pairs={{0,1},{1,0},{2,3},{3,2},{4,5},{5,4},{6,7},{7,6},{8,9},{9,8},{10,11... | collective-permute-start | bytes 2359304 | tf_op jit(solution)/shard_map/ppermute | solution.py:163
  7.5 15.0 %all-to-all-start = ((f32[16,8,256]{2,1,0:T(8,128)}), f32[16,8,256]{2,1,0:T(8,128)S(1)}, u32[]{:S(2)}, u32[]{:S(2)}) async-start(f32[16,8,256]{2,1,0:T(8,128)} %broadcast_in_dim.30), calls=%async_computation | async-start | bytes 262144 | tf_op jit(solution)/shard_map/all_to_all | solution.py:214
  15.8 0.9 copy-start.3
  16.8 12.1 %collective-permute-start.1 = (f32[1,6,64,256]{3,2,1,0:T(8,128)S(1)}, f32[1,6,64,256]{3,2,1,0:T(8,128)S(1)}, u32[]{:S(2)}, u32[]{:S(2)}) collective-permute-start(f32[1,6,64,256]{3,2,1,0:T(8,128)S(1)} %constant_dynamic-slice_fusion.3), channel_id=1, source_target_pairs={{0,2},{1,3},{2,0},{3,1},{4,6},{5,7},{6,4},{7,5},{8,10},{9,11},{10,... | collective-permute-start | bytes 1179656 | tf_op jit(solution)/shard_map/ppermute | solution.py:163
  40.2 11.4 %collective-permute-start.2 = (s16[528,256]{1,0:T(8,128)(2,1)}, s16[528,256]{1,0:T(8,128)(2,1)S(1)}, u32[]{:S(2)}, u32[]{:S(2)}) collective-permute-start(s16[528,256]{1,0:T(8,128)(2,1)} %chunk_sent.3), channel_id=1, source_target_pairs={{0,12},{4,8},{8,4},{12,0},{1,13},{5,9},{9,5},{13,1},{2,14},{6,10},... | collective-permute-start | bytes 811016 | tf_op jit(solution)/shard_map/ppermute | solution.py:163
  44.6 22.6 %collective-permute-start.3 = (s16[528,256]{1,0:T(8,128)(2,1)}, s16[528,256]{1,0:T(8,128)(2,1)S(1)}, u32[]{:S(2)}, u32[]{:S(2)}) collective-permute-start(s16[528,256]{1,0:T(8,128)(2,1)} %chunk_sent.4), channel_id=1, source_target_pairs={{0,8},{4,12},{8,0},{12,4},{1,9},{5,13},{9,1},{13,5},{2,10},{6,14},... | collective-permute-start | bytes 811016 | tf_op jit(solution)/shard_map/ppermute | solution.py:163
  46.2 21.1 %collective-permute-start.4 = (s16[528,256]{1,0:T(8,128)(2,1)}, s16[528,256]{1,0:T(8,128)(2,1)}, u32[]{:S(2)}, u32[]{:S(2)}) collective-permute-start(s16[528,256]{1,0:T(8,128)(2,1)} %chunk_sent.5), channel_id=1, source_target_pairs={{0,4},{4,0},{8,12},{12,8},{1,5},{5,1},{9,13},{13,9},{2,6},{6,2},{1... | collective-permute-start | bytes 811016 | tf_op jit(solution)/shard_map/ppermute | solution.py:163
  69.3 1.4 collective-permute-start.5
  70.8 5.6 %collective-permute-start.6 = (f32[64,256]{0,1:T(8,128)S(1)}, f32[64,256]{0,1:T(8,128)S(1)}, u32[]{:S(2)}, u32[]{:S(2)}) collective-permute-start(f32[64,256]{0,1:T(8,128)S(1)} %bitcast.63), channel_id=1, source_target_pairs={{0,2},{1,3},{2,0},{3,1},{4,6},{5,7},{6,4},{7,5},{8,10},{9,11},{10,... | collective-permute-start | bytes 196616 | tf_op jit(solution)/shard_map/ppermute | solution.py:163
  76.4 6.7 %collective-permute-start.7 = (f32[64,256]{0,1:T(8,128)S(1)}, f32[64,256]{0,1:T(8,128)S(1)}, u32[]{:S(2)}, u32[]{:S(2)}) collective-permute-start(f32[64,256]{0,1:T(8,128)S(1)} %bitcast_add_fusion.1), channel_id=1, source_target_pairs={{0,4},{4,0},{8,12},{12,8},{1,5},{5,1},{9,13},{13,9},{2,6},{6,2},{1... | collective-permute-start | bytes 196616 | tf_op jit(solution)/shard_map/ppermute | solution.py:163
  76.5 12.7 %collective-permute-start.8 = (f32[64,256]{0,1:T(8,128)S(1)}, f32[64,256]{0,1:T(8,128)S(1)}, u32[]{:S(2)}, u32[]{:S(2)}) collective-permute-start(f32[64,256]{0,1:T(8,128)S(1)} %bitcast_add_fusion.1), channel_id=1, source_target_pairs={{0,8},{4,12},{8,0},{12,4},{1,9},{5,13},{9,1},{13,5},{2,10},{6,14},... | collective-permute-start | bytes 196616 | tf_op jit(solution)/shard_map/ppermute | solution.py:163
  79.3 10.0 %collective-permute-start.9 = (f32[64,256]{0,1:T(8,128)S(1)}, f32[64,256]{0,1:T(8,128)S(1)}, u32[]{:S(2)}, u32[]{:S(2)}) collective-permute-start(f32[64,256]{0,1:T(8,128)S(1)} %bitcast_add_fusion.1), channel_id=1, source_target_pairs={{0,12},{4,8},{8,4},{12,0},{1,13},{5,9},{9,5},{13,1},{2,14},{6,10},... | collective-permute-start | bytes 196616 | tf_op jit(solution)/shard_map/ppermute | solution.py:163
  89.3 5.0 %collective-permute-start.10 = (f32[64,256]{0,1:T(8,128)S(1)}, f32[64,256]{0,1:T(8,128)S(1)}, u32[]{:S(2)}, u32[]{:S(2)}) collective-permute-start(f32[64,256]{0,1:T(8,128)S(1)} %add_add_fusion), channel_id=1, source_target_pairs={{0,2},{1,3},{2,0},{3,1},{4,6},{5,7},{6,4},{7,5},{8,10},{9,11},{10,... | collective-permute-start | bytes 196616 | tf_op jit(solution)/shard_map/ppermute | solution.py:163
  94.5 1.4 collective-permute-start.11
  96.0 59.9 %copy-start.4 = (f32[512,256]{1,0:T(8,128)S(1)}, f32[512,256]{1,0:T(8,128)}, u32[]{:S(2)}) copy-start(f32[512,256]{1,0:T(8,128)} %get-tuple-element.13) | copy-start | bytes 1572868

commit v2 on v1

--- a/solution.py
+++ b/solution.py
@@ -10,6 +10,7 @@
 PLANES = 6
 STEPS = 64.0
 TOP = 32767.0
+BLOCK, LANES, SUB = 32, 128, 8
 HIGH = lax.Precision.HIGHEST
 VMEM_BYTES = 40 * 1024 * 1024
 
@@ -156,6 +157,114 @@
         compiler_params=params(),
         name="collect",
     )(kept, *received)
+
+
+def pieces(x):
+    high = x.astype(jnp.bfloat16)
+    rest = x - high.astype(jnp.float32)
+    mid = rest.astype(jnp.bfloat16)
+    low = (rest - mid.astype(jnp.float32)).astype(jnp.bfloat16)
+    return high, mid, low
+
+def factor(table, r_out):
+    width = table.shape[0]
+    tiles = width // LANES
+    lane = lax.broadcasted_iota(jnp.int32, (SUB, LANES), 1)
+    sub = lax.broadcasted_iota(jnp.int32, (SUB, LANES), 0)
+    spread = lambda x, k: jnp.broadcast_to(x[k : k + 1], (SUB, LANES))
+    for base in range(0, width, BLOCK):
+        t, off = base // LANES, base % LANES
+        groups = BLOCK // SUB
+        rows = [
+            [
+                table[base + SUB * q : base + SUB * (q + 1), LANES * i : LANES * (i + 1)]
+                for i in range(tiles)
+            ]
+            for q in range(groups)
+        ]
+        for p in range(groups):
+            first = off + SUB * p
+            cols = [
+                [
+                    jnp.broadcast_to(rows[q][t][:, first + m : first + m + 1], (SUB, LANES))
+                    if q >= p
+                    else None
+                    for q in range(groups)
+                ]
+                for m in range(SUB)
+            ]
+            upper = rows[p][t]
+            inside = (lane >= first) & (lane < first + SUB)
+            unit = jnp.where(lane - first == sub, 1.0, 0.0)
+            for q in range(p, groups):
+                rows[q][t] = jnp.where(inside, unit if q == p else 0.0, rows[q][t])
+            pivots = jnp.ones((SUB, LANES), jnp.float32)
+            for k in range(SUB):
+                pivot = spread(cols[k][p], k)
+                inverse = 1.0 / pivot
+                pivots = jnp.where(sub == k, pivot, pivots)
+                step = [None] * groups
+                for q in range(p, groups):
+                    step[q] = (jnp.where(sub > k, cols[k][q], 0.0) if q == p else cols[k][q]) * inverse
+                for m in range(k + 1, SUB):
+                    line = spread(cols[m][p], k)
+                    for q in range(p, groups):
+                        cols[m][q] = cols[m][q] - step[q] * line
+                for i in range(tiles):
+                    line = spread(rows[p][i], k)
+                    for q in range(p, groups):
+                        rows[q][i] = rows[q][i] - step[q] * line
+                upper = upper - step[p] * spread(upper, k)
+            scale = lax.rsqrt(pivots)
+            for i in range(tiles):
+                rows[p][i] = rows[p][i] * scale
+            upper = jnp.where(lane >= first + SUB, rows[p][t], upper * scale)
+            upper = jnp.where(lane >= first + sub, upper, 0.0)
+            place = slice(base + SUB * p, base + SUB * (p + 1))
+            for i in range(tiles):
+                r_out[place, LANES * i : LANES * (i + 1)] = (
+                    upper if i == t else rows[p][i] if i > t else jnp.zeros((SUB, LANES), jnp.float32)
+                )
+        for p in range(groups - 1):
+            rows[p][t] = jnp.where((lane >= off + SUB * (p + 1)) & (lane < off + BLOCK), 0.0, rows[p][t])
+        whole = jnp.concatenate([jnp.concatenate(r, axis=1) for r in rows], axis=0)
+        column = lax.broadcasted_iota(jnp.int32, (BLOCK, width), 1)
+        table[base : base + BLOCK, :] = jnp.where(column < base + BLOCK, whole, 0.0)
+        end = base + BLOCK
+        if end < width:
+            begin = end // LANES * LANES
+            h, m, l = pieces(whole)
+            left = jnp.concatenate([h, h, h, m, m, l], axis=0)[:, begin:]
+            right = jnp.concatenate([h, m, l, h, m, h], axis=0)
+            change = lax.dot_general(left, right, (((0,), (0,)), ((), ())), preferred_element_type=jnp.float32)
+            column = lax.broadcasted_iota(jnp.int32, (width - end, width), 1)
+            keep = jnp.where((column >= base) & (column < end), 0.0, table[end:, :])
+            table[end:, :] = keep - change[end - begin :]
+
+def basis_kernel(gram, y, r_out, q_out, table):
+    table[...] = gram[...]
+    factor(table, r_out)
+    q_out[...] = lax.dot_general(
+        y[...],
+        table[...],
+        (((1,), (1,)), ((), ())),
+        precision=HIGH,
+        preferred_element_type=jnp.float32,
+    )
+
+
+def orthonormalize(gram, y):
+    width = gram.shape[0]
+    return pl.pallas_call(
+        basis_kernel,
+        out_shape=[
+            jax.ShapeDtypeStruct((width, width), jnp.float32),
+            jax.ShapeDtypeStruct(y.shape, jnp.float32),
+        ],
+        scratch_shapes=[pltpu.VMEM((width, width), jnp.float32)],
+        compiler_params=params(),
+        name="orthonormalize",
+    )(gram, y)
 
 
 def swap(array, axis, mask):
@@ -239,12 +348,9 @@
         )
         y_local, gram = collect(y_local, [], 1.0 / total_snps)
     gram_sum = gram_total(gram)
-    lower_factor = jnp.linalg.cholesky(gram_sum)
-    q_next = lax.linalg.triangular_solve(
-        lower_factor, y_local, left_side=False, lower=True, transpose_a=True
-    )
+    r_factor, q_next = orthonormalize(gram_sum, y_local)
     layout = (1, 1, y_local.shape[0], width)
-    return (y_local.reshape(layout), lower_factor.T, q_next.reshape(layout))
+    return (y_local.reshape(layout), r_factor, q_next.reshape(layout))
 
 
 def solution(mesh):

time: 160 us -> 101 us (0.63)
  other arithmetic: 56.6 us -> 2.47 us
  Pallas kernels: 10.3 us -> 19.2 us
  local copies, waits for them, and re-layouts: 10.6 us -> 4.41 us
  waiting for transfers between devices: 48.8 us -> 45.3 us
  matrix products: 1.91 us -> 0 us
    another operation x9 -> x0, other arithmetic: 53.8 us -> none  [the longest x6 34.1 us: per_device(): lower_factor = jnp.linalg.cholesky(gram_sum)]
    pallas_call x0 -> x1, Pallas kernels: none -> 8.91 us  [orthonormalize(): pl.pallas_call(basis_kernel, out_shape=[jax.ShapeDtypeStruct((width, widt...]
    another operation x9 -> x0, local copies, waits for them, and re-layouts: 4.05 us -> none
    ppermute x12, waiting for transfers between devices: 45 us -> 41.5 us  [swap(): return lax.ppermute(array, axis, [(i, i ^ mask) for i in range(size)])]
    another operation x5 -> x0, matrix products: 1.91 us -> none  [the longest x3 1.43 us: per_device(): lax.linalg.triangular_solve(lower_factor, y_local, left_side=False, lower...]
    unnamed x12 -> x10, local copies, waits for them, and re-layouts: 5.54 us -> 3.7 us
  transfers between devices with their start and end apart: 13 -> 13, of which waited for: 10 -> 10; matrix products, arithmetic and copies ran while one was open for 1% -> 2% of each run, Pallas kernels for 3% -> 2%
where the time goes in v2:
time: 101 us
  waiting for transfers between devices  45.3 us (45%)
  starting transfers between devices  20.1 us (20%)
  Pallas kernels  19.2 us (19%)
  blocking collectives  8.69 us (9%)
  local copies, waits for them, and re-layouts  4.41 us (4%)
  other arithmetic  2.47 us (2%)
    ppermute x12, waiting for transfers between devices, swap(): return lax.ppermute(array, axis, [(i, i ^ mask) for i in range(size)])  41.5 us
    ppermute x12, starting transfers between devices, swap(): return lax.ppermute(array, axis, [(i, i ^ mask) for i in range(size)])  13.1 us
    pallas_call x1, Pallas kernels, orthonormalize(): pl.pallas_call(basis_kernel, out_shape=[jax.ShapeDtypeStruct((width, widt...  8.91 us
    all_gather x1, blocking collectives, per_device(): scores = lax.all_gather(rows, 'snp').reshape(n_snp, PLANES, depth, width)  8.69 us
    all_to_all x1, starting transfers between devices, per_device(): lax.all_to_all(every, ('samp', 'snp'), 0, 0, tiled=True).sum(axis=(0, 1))  7.02 us
    pallas_call x4, Pallas kernels, chunk_of_y(): pl.pallas_call(functools.partial(sent_kernel if sent else kept_kernel, sc...  5.36 us
    all_to_all x1, waiting for transfers between devices, per_device(): lax.all_to_all(every, ('samp', 'snp'), 0, 0, tiled=True).sum(axis=(0, 1))  3.79 us
    unnamed x10, local copies, waits for them, and re-layouts  3.7 us
  transfers between devices with their start and end apart: 13, of which 10 were waited for; matrix products, arithmetic and copies ran while one was open for 2% of the time, Pallas kernels for 2%

profile of v2, /device:TPU:0, one launch (start us, length us, event | category | flops | bytes accessed | tf_op | source)
XLA Modules:
  0.0 101.0 jit_solution(1800539015039729956)
XLA Ops:
  0.6 0.0 copy-start
  0.6 1.6 %copy-done = s32[256,2048]{1,0:T(8,128)S(1)} copy-done((s32[256,2048]{1,0:T(8,128)S(1)}, s32[256,2048]{1,0:T(8,128)}, u32[]{:S(2)}) %copy-start) | copy-done | bytes 2097176
  2.2 0.0 copy-start.2
  2.2 1.2 %copy-done.2 = bf16[2048,256]{1,0:T(8,128)(2,1)S(1)} copy-done((bf16[2048,256]{1,0:T(8,128)(2,1)S(1)}, bf16[2048,256]{1,0:T(8,128)(2,1)}, u32[]{:S(2)}) %copy-start.2) | copy-done | bytes 1048600
  3.5 0.0 copy-start.1
  3.5 1.9 %project.3 = (f32[2,6,64,256]{3,2,1,0:T(8,128)}, f32[8,256]{1,0:T(8,128)S(1)}) custom-call(s32[1]{0:T(128)} %bitcast.2.pick, s32[256,2048]{1,0:T(8,128)S(1)} %copy-done, bf16[2048,256]{1,0:T(8,128)(2,1)S(1)} %copy-done.2), custom_call_target="tpu_custom_call" | custom-call | flops 805306368 | bytes 2883584 | tf_op jit(solution)/shard_map/project/pallas_call | solution.py:45
  5.3 0.5 collective-permute-start
  5.8 0.0 copy-done.1
  5.8 1.1 %project.2 = (f32[2,6,64,256]{3,2,1,0:T(8,128)S(1)}, f32[8,256]{1,0:T(8,128)S(1)}) custom-call(s32[1]{0:T(128)} %bitcast.1.pick, s32[256,2048]{1,0:T(8,128)S(1)} %copy-done.1, bf16[2048,256]{1,0:T(8,128)(2,1)S(1)} %copy-done.2), custom_call_target="tpu_custom_call" | custom-call | flops 805306368 | bytes 2883584 | tf_op jit(solution)/shard_map/project/pallas_call | solution.py:45
  6.9 0.7 broadcast_in_dim.28
  7.5 7.0 %all-to-all-start = ((f32[16,8,256]{2,1,0:T(8,128)}), f32[16,8,256]{2,1,0:T(8,128)S(1)}, u32[]{:S(2)}, u32[]{:S(2)}) async-start(f32[16,8,256]{2,1,0:T(8,128)} %broadcast_in_dim.28), calls=%async_computation | async-start | bytes 262144 | tf_op jit(solution)/shard_map/all_to_all | solution.py:323
  14.6 0.0 collective-permute-done
  14.6 1.2 %add.50 = f32[2,6,64,256]{3,2,1,0:T(8,128)S(1)} add(f32[2,6,64,256]{3,2,1,0:T(8,128)S(1)} %get-tuple-element.11, f32[2,6,64,256]{3,2,1,0:T(8,128)} %collective-permute-done) | non-fusion elementwise | flops 196608 | bytes 2359296 | tf_op jit(solution)/shard_map/add | solution.py:315
  15.8 0.0 copy-start.4
  15.9 0.9 copy-done.4
  16.8 2.0 %collective-permute-start.1 = (f32[1,6,64,256]{3,2,1,0:T(8,128)S(1)}, f32[1,6,64,256]{3,2,1,0:T(8,128)S(1)}, u32[]{:S(2)}, u32[]{:S(2)}) collective-permute-start(f32[1,6,64,256]{3,2,1,0:T(8,128)S(1)} %constant_dynamic-slice_fusion), channel_id=1, source_target_pairs={{0,2},{1,3},{2,0},{3,1},{4,6},{5,7},{6,4},{7,5},{8,10},{9,11},{10,... | collective-permute-start | bytes 1179656 | tf_op jit(solution)/shard_map/ppermute | solution.py:272
  18.7 3.8 %all-to-all-done = f32[16,8,256]{2,1,0:T(8,128)S(1)} async-done(((f32[16,8,256]{2,1,0:T(8,128)}), f32[16,8,256]{2,1,0:T(8,128)S(1)}, u32[]{:S(2)}, u32[]{:S(2)}) %all-to-all-start) | async-done | bytes 131104 | tf_op jit(solution)/shard_map/all_to_all | solution.py:323
  22.6 6.3 %collective-permute-done.1 = f32[1,6,64,256]{3,2,1,0:T(8,128)S(1)} collective-permute-done((f32[1,6,64,256]{3,2,1,0:T(8,128)S(1)}, f32[1,6,64,256]{3,2,1,0:T(8,128)S(1)}, u32[]{:S(2)}, u32[]{:S(2)}) %collective-permute-start.1) | collective-permute-done | bytes 393248 | tf_op jit(solution)/shard_map/ppermute | solution.py:272
  28.9 1.0 %dynamic-slice_add_fusion = f32[1,6,64,256]{3,2,1,0:T(8,128)S(1)} fusion(f32[1,6,64,256]{3,2,1,0:T(8,128)S(1)} %collective-permute-done.1, f32[2,6,64,256]{3,2,1,0:T(8,128)} %copy-done.4, s32[]{:T(128)S(6)} %select_n.58), kind=kLoop, calls=%fused_computation.2 | loop fusion | flops 98304 | bytes 1179652 | tf_op jit(solution)/shard_map/add | solution.py:320
  29.9 8.7 %all_gather.4 = bf16[4,384,256]{2,1,0:T(8,128)(2,1)S(1)} all-gather(bf16[1,384,256]{2,1,0:T(8,128)(2,1)S(1)} %fusion), channel_id=1, replica_groups=mesh['grp'=2,'samp'=4,'snp'=4] {'snp'}, dimensions={0}, use_global_device_ids=true | all-gather | bytes 983040 | tf_op jit(solution)/shard_map/all_gather | solution.py:328
  38.6 1.5 %chunk_sent.5 = s16[528,256]{1,0:T(8,128)(2,1)} custom-call(s32[1]{0:T(128)} %bitcast.7.pick, s32[256,2048]{1,0:T(8,128)S(1)} %copy-done.1, bf16[4,6,64,256]{3,2,1,0:T(8,128)(2,1)S(1)} %bitcast.23), custom_call_target="tpu_custom_call" | custom-call | flops 402653184 | bytes 1835008 | tf_op jit(solution)/shard_map/chunk_sent/pallas_call | solution.py:113
  40.2 1.5 %chunk_sent.4 = s16[528,256]{1,0:T(8,128)(2,1)} custom-call(s32[1]{0:T(128)} %bitcast.6.pick, s32[256,2048]{1,0:T(8,128)S(1)} %copy-done.1, bf16[4,6,64,256]{3,2,1,0:T(8,128)(2,1)S(1)} %bitcast.24), custom_call_target="tpu_custom_call" | custom-call | flops 402653184 | bytes 1835008 | tf_op jit(solution)/shard_map/chunk_sent/pallas_call | solution.py:113
  41.7 1.5 %chunk_sent.3 = s16[528,256]{1,0:T(8,128)(2,1)} custom-call(s32[1]{0:T(128)} %bitcast.5.pick, s32[256,2048]{1,0:T(8,128)S(1)} %copy-done.1, bf16[4,6,64,256]{3,2,1,0:T(8,128)(2,1)S(1)} %bitcast.25), custom_call_target="tpu_custom_call" | custom-call | flops 402653184 | bytes 1835008 | tf_op jit(solution)/shard_map/chunk_sent/pallas_call | solution.py:113
  43.3 2.9 %collective-permute-start.2 = (s16[528,256]{1,0:T(8,128)(2,1)}, s16[528,256]{1,0:T(8,128)(2,1)S(1)}, u32[]{:S(2)}, u32[]{:S(2)}) collective-permute-start(s16[528,256]{1,0:T(8,128)(2,1)} %chunk_sent.3), channel_id=1, source_target_pairs={{0,12},{4,8},{8,4},{12,0},{1,13},{5,9},{9,5},{13,1},{2,14},{6,10},... | collective-permute-start | bytes 811016 | tf_op jit(solution)/shard_map/ppermute | solution.py:272
  46.2 0.0 collective-permute-start.3
  46.2 1.5 %collective-permute-start.4 = (s16[528,256]{1,0:T(8,128)(2,1)}, s16[528,256]{1,0:T(8,128)(2,1)}, u32[]{:S(2)}, u32[]{:S(2)}) collective-permute-start(s16[528,256]{1,0:T(8,128)(2,1)} %chunk_sent.5), channel_id=1, source_target_pairs={{0,4},{4,0},{8,12},{12,8},{1,5},{5,1},{9,13},{13,9},{2,6},{6,2},{1... | collective-permute-start | bytes 811016 | tf_op jit(solution)/shard_map/ppermute | solution.py:272
  47.6 0.7 chunk_kept.1.refs_0_
  48.4 6.3 %collective-permute-done.2.refs_1_ = s16[528,256]{1,0:T(8,128)(2,1)S(1)} collective-permute-done((s16[528,256]{1,0:T(8,128)(2,1)}, s16[528,256]{1,0:T(8,128)(2,1)S(1)}, u32[]{:S(2)}, u32[]{:S(2)}) %collective-permute-start.2) | collective-permute-done | bytes 270368 | tf_op jit(solution)/shard_map/ppermute | solution.py:272
  54.7 15.6 %collective-permute-done.3.refs_2_ = s16[528,256]{1,0:T(8,128)(2,1)S(1)} collective-permute-done((s16[528,256]{1,0:T(8,128)(2,1)}, s16[528,256]{1,0:T(8,128)(2,1)S(1)}, u32[]{:S(2)}, u32[]{:S(2)}) %collective-permute-start.3) | collective-permute-done | bytes 270368 | tf_op jit(solution)/shard_map/ppermute | solution.py:272
  70.3 0.0 collective-permute-done.4.refs_3_
  70.3 2.0 %collect.1 = (f32[512,256]{1,0:T(8,128)}, f32[256,256]{1,0:T(8,128)S(1)}) custom-call(f32[512,256]{1,0:T(8,128)S(1)} %chunk_kept.1.refs_0_, s16[528,256]{1,0:T(8,128)(2,1)S(1)} %collective-permute-done.2.refs_1_, s16[528,256]{1,0:T(8,128)(2,1)S(1)} %collective-permute-done.3.refs_2_, s16[528,256]{1,0:T(8,128)(2,1)} %collective-permute-done.4.refs_3_), custom_call_target="tpu_custom_call" | custom-call | tf_op jit(solution)/shard_map/collect/pallas_call | solution.py:151
  72.3 0.0 copy-start.3
  72.3 0.1 collective-permute-start.5
  72.4 1.3 %collective-permute-done.5 = f32[128,256]{1,0:T(8,128)S(1)} collective-permute-done((f32[128,256]{1,0:T(8,128)S(1)}, f32[128,256]{1,0:T(8,128)S(1)}, u32[]{:S(2)}, u32[]{:S(2)}) %collective-permute-start.5) | collective-permute-done | bytes 131104 | tf_op jit(solution)/shard_map/ppermute | solution.py:272
  73.8 0.8 collective-permute-start.6
  74.6 3.5 %collective-permute-done.6 = f32[64,256]{1,0:T(8,128)S(1)} collective-permute-done((f32[64,256]{1,0:T(8,128)S(1)}, f32[64,256]{1,0:T(8,128)S(1)}, u32[]{:S(2)}, u32[]{:S(2)}) %collective-permute-start.6) | collective-permute-done | bytes 65568 | tf_op jit(solution)/shard_map/ppermute | solution.py:272
  78.1 2.3 %collective-permute-start.9 = (f32[64,256]{1,0:T(8,128)S(1)}, f32[64,256]{1,0:T(8,128)S(1)}, u32[]{:S(2)}, u32[]{:S(2)}) collective-permute-start(f32[64,256]{1,0:T(8,128)S(1)} %bitcast_add_fusion.1), channel_id=1, source_target_pairs={{0,12},{4,8},{8,4},{12,0},{1,13},{5,9},{9,5},{13,1},{2,14},{6,10},... | collective-permute-start | bytes 196616 | tf_op jit(solution)/shard_map/ppermute | solution.py:272
  80.4 0.0 collective-permute-start.8
  80.4 2.2 %collective-permute-start.7 = (f32[64,256]{1,0:T(8,128)S(1)}, f32[64,256]{1,0:T(8,128)S(1)}, u32[]{:S(2)}, u32[]{:S(2)}) collective-permute-start(f32[64,256]{1,0:T(8,128)S(1)} %bitcast_add_fusion.1), channel_id=1, source_target_pairs={{0,4},{4,0},{8,12},{12,8},{1,5},{5,1},{9,13},{13,9},{2,6},{6,2},{1... | collective-permute-start | bytes 196616 | tf_op jit(solution)/shard_map/ppermute | solution.py:272
  82.6 2.1 %collective-permute-done.9 = f32[64,256]{1,0:T(8,128)S(1)} collective-permute-done((f32[64,256]{1,0:T(8,128)S(1)}, f32[64,256]{1,0:T(8,128)S(1)}, u32[]{:S(2)}, u32[]{:S(2)}) %collective-permute-start.9) | collective-permute-done | bytes 65568 | tf_op jit(solution)/shard_map/ppermute | solution.py:272
  84.7 1.5 %collective-permute-done.8 = f32[64,256]{1,0:T(8,128)S(1)} collective-permute-done((f32[64,256]{1,0:T(8,128)S(1)}, f32[64,256]{1,0:T(8,128)S(1)}, u32[]{:S(2)}, u32[]{:S(2)}) %collective-permute-start.8) | collective-permute-done | bytes 65568 | tf_op jit(solution)/shard_map/ppermute | solution.py:272
  86.2 0.0 collective-permute-done.7
  86.2 0.8 collective-permute-start.10
  87.1 3.5 %collective-permute-done.10 = f32[64,256]{1,0:T(8,128)S(1)} collective-permute-done((f32[64,256]{1,0:T(8,128)S(1)}, f32[64,256]{1,0:T(8,128)S(1)}, u32[]{:S(2)}, u32[]{:S(2)}) %collective-permute-start.10) | collective-permute-done | bytes 65568 | tf_op jit(solution)/shard_map/ppermute | solution.py:272
  90.6 0.1 collective-permute-start.11
  90.7 1.3 %collective-permute-done.11 = f32[128,256]{1,0:T(8,128)S(1)} collective-permute-done((f32[128,256]{1,0:T(8,128)S(1)}, f32[128,256]{1,0:T(8,128)S(1)}, u32[]{:S(2)}, u32[]{:S(2)}) %collective-permute-start.11) | collective-permute-done | bytes 131104 | tf_op jit(solution)/shard_map/ppermute | solution.py:272
  92.1 0.0 copy-done.3
  92.1 8.9 %orthonormalize.1 = (f32[256,256]{1,0:T(8,128)}, f32[512,256]{1,0:T(8,128)}) custom-call(f32[256,256]{1,0:T(8,128)S(1)} %pad_maximum_fusion.gram, f32[512,256]{1,0:T(8,128)S(1)} %copy-done.3), custom_call_target="tpu_custom_call" | custom-call | tf_op jit(solution)/shard_map/orthonormalize/pallas_call | solution.py:258
  (14 shorter events, 0.2 us)
Async XLA Ops:
  0.6 1.6 %copy-start = (s32[256,2048]{1,0:T(8,128)S(1)}, s32[256,2048]{1,0:T(8,128)}, u32[]{:S(2)}) copy-start(s32[256,2048]{1,0:T(8,128)} %words.11) | copy-start | bytes 6291460
  2.2 1.2 %copy-start.2 = (bf16[2048,256]{1,0:T(8,128)(2,1)S(1)}, bf16[2048,256]{1,0:T(8,128)(2,1)}, u32[]{:S(2)}) copy-start(bf16[2048,256]{1,0:T(8,128)(2,1)} %basis.3) | copy-start | bytes 3145732
  3.5 2.3 %copy-start.1 = (s32[256,2048]{1,0:T(8,128)S(1)}, s32[256,2048]{1,0:T(8,128)}, u32[]{:S(2)}) copy-start(s32[256,2048]{1,0:T(8,128)} %words.11) | copy-start | bytes 6291460
  5.3 9.3 %collective-permute-start = (f32[2,6,64,256]{3,2,1,0:T(8,128)}, f32[2,6,64,256]{3,2,1,0:T(8,128)}, u32[]{:S(2)}, u32[]{:S(2)}) collective-permute-start(f32[2,6,64,256]{3,2,1,0:T(8,128)} %get-tuple-element.12), channel_id=1, source_target_pairs={{0,1},{1,0},{2,3},{3,2},{4,5},{5,4},{6,7},{7,6},{8,9},{9,8},{10,11... | collective-permute-start | bytes 2359304 | tf_op jit(solution)/shard_map/ppermute | solution.py:272
  7.5 15.0 %all-to-all-start = ((f32[16,8,256]{2,1,0:T(8,128)}), f32[16,8,256]{2,1,0:T(8,128)S(1)}, u32[]{:S(2)}, u32[]{:S(2)}) async-start(f32[16,8,256]{2,1,0:T(8,128)} %broadcast_in_dim.28), calls=%async_computation | async-start | bytes 262144 | tf_op jit(solution)/shard_map/all_to_all | solution.py:323
  15.8 0.9 copy-start.4
  16.8 12.1 %collective-permute-start.1 = (f32[1,6,64,256]{3,2,1,0:T(8,128)S(1)}, f32[1,6,64,256]{3,2,1,0:T(8,128)S(1)}, u32[]{:S(2)}, u32[]{:S(2)}) collective-permute-start(f32[1,6,64,256]{3,2,1,0:T(8,128)S(1)} %constant_dynamic-slice_fusion), channel_id=1, source_target_pairs={{0,2},{1,3},{2,0},{3,1},{4,6},{5,7},{6,4},{7,5},{8,10},{9,11},{10,... | collective-permute-start | bytes 1179656 | tf_op jit(solution)/shard_map/ppermute | solution.py:272
  43.3 11.5 %collective-permute-start.2 = (s16[528,256]{1,0:T(8,128)(2,1)}, s16[528,256]{1,0:T(8,128)(2,1)S(1)}, u32[]{:S(2)}, u32[]{:S(2)}) collective-permute-start(s16[528,256]{1,0:T(8,128)(2,1)} %chunk_sent.3), channel_id=1, source_target_pairs={{0,12},{4,8},{8,4},{12,0},{1,13},{5,9},{9,5},{13,1},{2,14},{6,10},... | collective-permute-start | bytes 811016 | tf_op jit(solution)/shard_map/ppermute | solution.py:272
  46.2 24.1 %collective-permute-start.3 = (s16[528,256]{1,0:T(8,128)(2,1)}, s16[528,256]{1,0:T(8,128)(2,1)S(1)}, u32[]{:S(2)}, u32[]{:S(2)}) collective-permute-start(s16[528,256]{1,0:T(8,128)(2,1)} %chunk_sent.4), channel_id=1, source_target_pairs={{0,8},{4,12},{8,0},{12,4},{1,9},{5,13},{9,1},{13,5},{2,10},{6,14},... | collective-permute-start | bytes 811016 | tf_op jit(solution)/shard_map/ppermute | solution.py:272
  46.2 24.1 %collective-permute-start.4 = (s16[528,256]{1,0:T(8,128)(2,1)}, s16[528,256]{1,0:T(8,128)(2,1)}, u32[]{:S(2)}, u32[]{:S(2)}) collective-permute-start(s16[528,256]{1,0:T(8,128)(2,1)} %chunk_sent.5), channel_id=1, source_target_pairs={{0,4},{4,0},{8,12},{12,8},{1,5},{5,1},{9,13},{13,9},{2,6},{6,2},{1... | collective-permute-start | bytes 811016 | tf_op jit(solution)/shard_map/ppermute | solution.py:272
  72.3 19.7 %copy-start.3 = (f32[512,256]{1,0:T(8,128)S(1)}, f32[512,256]{1,0:T(8,128)}, u32[]{:S(2)}) copy-start(f32[512,256]{1,0:T(8,128)} %get-tuple-element.15.y) | copy-start | bytes 1572868
  72.3 1.4 %collective-permute-start.5 = (f32[128,256]{1,0:T(8,128)S(1)}, f32[128,256]{1,0:T(8,128)S(1)}, u32[]{:S(2)}, u32[]{:S(2)}) collective-permute-start(f32[128,256]{1,0:T(8,128)S(1)} %dynamic-slice_bitcast_fusion), channel_id=1, source_target_pairs={{0,1},{1,0},{2,3},{3,2},{4,5},{5,4},{6,7},{7,6},{8,9},{9,8},{10,11... | collective-permute-start | bytes 393224 | tf_op jit(solution)/shard_map/ppermute | solution.py:272
  73.8 4.3 %collective-permute-start.6 = (f32[64,256]{1,0:T(8,128)S(1)}, f32[64,256]{1,0:T(8,128)S(1)}, u32[]{:S(2)}, u32[]{:S(2)}) collective-permute-start(f32[64,256]{1,0:T(8,128)S(1)} %dynamic-slice_bitcast_fusion.1), channel_id=1, source_target_pairs={{0,2},{1,3},{2,0},{3,1},{4,6},{5,7},{6,4},{7,5},{8,10},{9,11},{10,... | collective-permute-start | bytes 196616 | tf_op jit(solution)/shard_map/ppermute | solution.py:272
  78.1 6.6 %collective-permute-start.9 = (f32[64,256]{1,0:T(8,128)S(1)}, f32[64,256]{1,0:T(8,128)S(1)}, u32[]{:S(2)}, u32[]{:S(2)}) collective-permute-start(f32[64,256]{1,0:T(8,128)S(1)} %bitcast_add_fusion.1), channel_id=1, source_target_pairs={{0,12},{4,8},{8,4},{12,0},{1,13},{5,9},{9,5},{13,1},{2,14},{6,10},... | collective-permute-start | bytes 196616 | tf_op jit(solution)/shard_map/ppermute | solution.py:272
  80.4 5.8 %collective-permute-start.8 = (f32[64,256]{1,0:T(8,128)S(1)}, f32[64,256]{1,0:T(8,128)S(1)}, u32[]{:S(2)}, u32[]{:S(2)}) collective-permute-start(f32[64,256]{1,0:T(8,128)S(1)} %bitcast_add_fusion.1), channel_id=1, source_target_pairs={{0,8},{4,12},{8,0},{12,4},{1,9},{5,13},{9,1},{13,5},{2,10},{6,14},... | collective-permute-start | bytes 196616 | tf_op jit(solution)/shard_map/ppermute | solution.py:272
  80.4 5.8 %collective-permute-start.7 = (f32[64,256]{1,0:T(8,128)S(1)}, f32[64,256]{1,0:T(8,128)S(1)}, u32[]{:S(2)}, u32[]{:S(2)}) collective-permute-start(f32[64,256]{1,0:T(8,128)S(1)} %bitcast_add_fusion.1), channel_id=1, source_target_pairs={{0,4},{4,0},{8,12},{12,8},{1,5},{5,1},{9,13},{13,9},{2,6},{6,2},{1... | collective-permute-start | bytes 196616 | tf_op jit(solution)/shard_map/ppermute | solution.py:272
  86.2 4.3 %collective-permute-start.10 = (f32[64,256]{1,0:T(8,128)S(1)}, f32[64,256]{1,0:T(8,128)S(1)}, u32[]{:S(2)}, u32[]{:S(2)}) collective-permute-start(f32[64,256]{1,0:T(8,128)S(1)} %add_add_fusion), channel_id=1, source_target_pairs={{0,2},{1,3},{2,0},{3,1},{4,6},{5,7},{6,4},{7,5},{8,10},{9,11},{10,... | collective-permute-start | bytes 196616 | tf_op jit(solution)/shard_map/ppermute | solution.py:272
  90.6 1.4 %collective-permute-start.11 = (f32[128,256]{1,0:T(8,128)S(1)}, f32[128,256]{1,0:T(8,128)S(1)}, u32[]{:S(2)}, u32[]{:S(2)}) collective-permute-start(f32[128,256]{1,0:T(8,128)S(1)} %pad_maximum_fusion.1), channel_id=1, source_target_pairs={{0,1},{1,0},{2,3},{3,2},{4,5},{5,4},{6,7},{7,6},{8,9},{9,8},{10,11... | collective-permute-start | bytes 393224 | tf_op jit(solution)/shard_map/ppermute | solution.py:272

commit v3 on v2

--- a/solution.py
+++ b/solution.py
@@ -1,4 +1,5 @@
 import functools
+import math
 
 import jax
 import jax.numpy as jnp
@@ -10,8 +11,9 @@
 PLANES = 6
 STEPS = 64.0
 TOP = 32767.0
-BLOCK, LANES, SUB = 32, 128, 8
+BLOCK, LANES, SUB, PAD = 32, 128, 8, 32
 HIGH = lax.Precision.HIGHEST
+PAIRS = 0x333
 VMEM_BYTES = 40 * 1024 * 1024
 
 
@@ -26,48 +28,104 @@
     ]
 
 
-def project_kernel(pick, words, basis, out, sums):
+def half_rows(words, basis, out, place):
+    half = words.shape[0] // 2
     blocks, _, depth, _ = out.shape
-    total = jnp.zeros(sums.shape, jnp.float32)
-    for t, plane in enumerate(planes_of(words[...])):
+    part = words[pl.ds(pl.multiple_of(place * half, half), half)]
+    for t, plane in enumerate(planes_of(part)):
         product = jnp.dot(plane, basis[...], preferred_element_type=jnp.float32)
         for b in range(blocks):
             out[b, t] = product[b * depth : (b + 1) * depth]
-        total = total + product.reshape(-1, 8, product.shape[1]).sum(axis=0)
-    sums[...] = total
-
-
-def project(words, basis, pick, blocks):
+
+
+def low_bit():
+    return jnp.bitwise_and(lax.axis_index("snp"), 1)
+
+
+def counts_of(words):
+    total = None
+    groups = words.shape[0] // 8
+    for first in range(0, groups, 3):
+        held = None
+        for g in range(first, min(first + 3, groups)):
+            word = words[8 * g : 8 * g + 8]
+            pair = (word & PAIRS) + (jnp.right_shift(word, 2) & PAIRS)
+            held = pair if held is None else held + pair
+        held = (held & 15) + (jnp.right_shift(held, 4) & 15) + jnp.right_shift(held, 8)
+        total = held if total is None else total + held
+    return total
+
+
+def other_kernel(words, basis, out, sums):
+    counts = counts_of(words)
+    pieces_ = jnp.concatenate([jnp.right_shift(counts, 4), counts & 15], axis=0)
+    both_ = jnp.dot(
+        pieces_.astype(jnp.float32).astype(jnp.bfloat16),
+        basis[...],
+        preferred_element_type=jnp.float32,
+    )
+    sums[...] = 16.0 * both_[:8] + both_[8:]
+    half_rows(words, basis, out, 1 - low_bit())
+
+
+def mine_kernel(words, basis, out):
+    half_rows(words, basis, out, low_bit())
+
+
+def project(words, basis, blocks, other):
     count, snps = words.shape
     width = basis.shape[1]
     half = count // 2
-    depth = half // blocks
-    return pl.pallas_call(
-        project_kernel,
-        grid_spec=pltpu.PrefetchScalarGridSpec(
-            num_scalar_prefetch=1,
-            grid=(1,),
-            in_specs=[
-                pl.BlockSpec((half, snps), lambda i, pick: (pick[0], 0)),
-                pl.BlockSpec((snps, width), lambda i, pick: (0, 0)),
-            ],
-            out_specs=[
-                pl.BlockSpec((blocks, PLANES, depth, width), lambda i, pick: (0, 0, 0, 0)),
-                pl.BlockSpec((8, width), lambda i, pick: (0, 0)),
-            ],
-        ),
-        out_shape=[
-            jax.ShapeDtypeStruct((blocks, PLANES, depth, width), jnp.float32),
-            jax.ShapeDtypeStruct((8, width), jnp.float32),
-        ],
-        compiler_params=params(),
-        name="project",
+    shapes = [jax.ShapeDtypeStruct((blocks, PLANES, half // blocks, width), jnp.float32)]
+    if other:
+        shapes.append(jax.ShapeDtypeStruct((8, width), jnp.float32))
+    return pl.pallas_call(
+        other_kernel if other else mine_kernel,
+        out_shape=shapes,
+        compiler_params=params(),
+        name="project_other" if other else "project_mine",
         cost_estimate=pl.CostEstimate(
             flops=2 * half * PLANES * snps * width,
             bytes_accessed=4 * half * snps + 2 * snps * width + 4 * half * PLANES * width,
             transcendentals=0,
         ),
-    )(pick, words, basis)
+    )(words, basis)
+
+
+def merge_kernel(shift, mine, got, sums, more, send, keep, total):
+    half = send.shape[0]
+    bit = jnp.bitwise_and(jnp.right_shift(lax.axis_index("snp"), shift), 1)
+    for b in range(half):
+        for out, first in ((send, 1 - bit), (keep, bit)):
+            out[b] = mine[first * half + b] + got[first * half + b]
+    total[...] = sums[...] + more[...]
+
+
+def merge(mine, got, shift, sums, more):
+    half = (mine.shape[0] // 2,) + mine.shape[1:]
+    return pl.pallas_call(
+        functools.partial(merge_kernel, shift),
+        out_shape=[jax.ShapeDtypeStruct(half, jnp.float32)] * 2
+        + [jax.ShapeDtypeStruct(sums.shape, jnp.float32)],
+        compiler_params=params(),
+        name="merge",
+    )(mine, got, sums, more)
+
+
+def finish_kernel(samples, mine, got, sums, out):
+    center = jnp.sum(sums[...], axis=0, keepdims=True) / jnp.float32(samples)
+    value = (mine[...] + got[...]).reshape(out.shape) - center
+    out[...] = value.astype(jnp.bfloat16)
+
+
+def finish(mine, got, sums, samples):
+    rows, width = mine.size // mine.shape[-1], mine.shape[-1]
+    return pl.pallas_call(
+        functools.partial(finish_kernel, samples),
+        out_shape=jax.ShapeDtypeStruct((rows, width), jnp.bfloat16),
+        compiler_params=params(),
+        name="finish",
+    )(mine, got, sums)
 
 
 def bit_reverse(index, bits):
@@ -90,9 +148,15 @@
     return (total * scale).T
 
 
-def sent_kernel(scale, pick, words, scores, out):
-    value = back_project(words[...], scores, scale)
-    rows = value.shape[0]
+def chunk_value(scale, mask, piece, words, scores, rows):
+    index = piece if mask is None else jnp.bitwise_xor(lax.axis_index("samp"), mask)
+    span = pl.ds(pl.multiple_of(index * rows, rows), rows)
+    return back_project(words[:, span], scores, scale)
+
+
+def sent_kernel(scale, mask, words, scores, out):
+    rows = out.shape[0] - 16
+    value = chunk_value(scale, mask, 0, words, scores, rows)
     top = jnp.maximum(jnp.max(jnp.abs(value), axis=0, keepdims=True), 1e-30)
     level = jnp.ceil(STEPS * jnp.log2(top / TOP)) + 1.0
     unit = jnp.exp2(level * (1.0 / STEPS))
@@ -101,62 +165,50 @@
     out[rows:] = jnp.broadcast_to(level, (16, level.shape[1])).astype(jnp.int32).astype(jnp.int16)
 
 
-def kept_kernel(scale, pick, words, scores, out):
-    out[...] = back_project(words[...], scores, scale)
-
-
-def chunk_of_y(words, scores, pick, rows, scale, sent):
-    count, snps = words.shape
+def kept_kernel(scale, mask, piece, words, scores, out):
+    out[...] = chunk_value(scale, mask, piece, words, scores, out.shape[0])
+
+
+def chunk_of_y(words, scores, rows, scale, mask, piece=0):
     width = scores.shape[-1]
+    sent = mask is not None and mask > 0
     shape = (rows + 16, width) if sent else (rows, width)
     dtype = jnp.int16 if sent else jnp.float32
-    return pl.pallas_call(
-        functools.partial(sent_kernel if sent else kept_kernel, scale),
-        grid_spec=pltpu.PrefetchScalarGridSpec(
-            num_scalar_prefetch=1,
-            grid=(1,),
-            in_specs=[
-                pl.BlockSpec((count, rows), lambda i, pick: (0, pick[0])),
-                pl.BlockSpec(scores.shape, lambda i, pick: (0, 0, 0, 0)),
-            ],
-            out_specs=pl.BlockSpec(shape, lambda i, pick: (0, 0)),
-        ),
+    kernel = functools.partial(sent_kernel, scale, mask)
+    if not sent:
+        kernel = functools.partial(kept_kernel, scale, mask, piece)
+    return pl.pallas_call(
+        kernel,
         out_shape=jax.ShapeDtypeStruct(shape, dtype),
         compiler_params=params(),
         name="chunk_sent" if sent else "chunk_kept",
         cost_estimate=pl.CostEstimate(
-            flops=2 * count * PLANES * rows * width,
-            bytes_accessed=4 * count * rows + 2 * scores.size + 4 * rows * width,
+            flops=2 * words.shape[0] * PLANES * rows * width,
+            bytes_accessed=4 * words.shape[0] * rows + 2 * scores.size + 4 * rows * width,
             transcendentals=0,
         ),
-    )(pick, words, scores)
-
-
-def collect_kernel(scale, *refs):
-    kept, out, gram = refs[0], refs[-2], refs[-1]
-    rows = kept.shape[0]
-    total = kept[...]
-    for ref in refs[1:-2]:
-        level = ref[rows : rows + 16].astype(jnp.int32).astype(jnp.float32)[:1]
-        unit = jnp.exp2(level * (1.0 / STEPS))
-        total = total + ref[:rows].astype(jnp.int32).astype(jnp.float32) * unit
-    out[...] = total
-    gram[...] = scale * lax.dot_general(
-        total, total, (((0,), (0,)), ((), ())), precision=HIGH, preferred_element_type=jnp.float32
-    )
-
-
-def collect(kept, received, scale):
-    width = kept.shape[1]
-    return pl.pallas_call(
-        functools.partial(collect_kernel, scale),
-        out_shape=[
-            jax.ShapeDtypeStruct(kept.shape, jnp.float32),
-            jax.ShapeDtypeStruct((width, width), jnp.float32),
-        ],
-        compiler_params=params(),
-        name="collect",
-    )(kept, *received)
+    )(words, scores)
+
+
+def decoded(coded, rows):
+    level = coded[rows : rows + 16].astype(jnp.int32).astype(jnp.float32)[:1]
+    return coded[:rows].astype(jnp.int32).astype(jnp.float32) * jnp.exp2(level * (1.0 / STEPS))
+
+
+def add_kernel(kept, coded, out):
+    out[...] = kept[...] + decoded(coded, kept.shape[0])
+
+
+def add_chunk(kept, coded):
+    return pl.pallas_call(
+        add_kernel,
+        out_shape=jax.ShapeDtypeStruct(kept.shape, jnp.float32),
+        compiler_params=params(),
+        name="add_chunk",
+        cost_estimate=pl.CostEstimate(
+            flops=4 * kept.size, bytes_accessed=10 * kept.size, transcendentals=0
+        ),
+    )(kept, coded)
 
 
 def pieces(x):
@@ -165,6 +217,62 @@
     mid = rest.astype(jnp.bfloat16)
     low = (rest - mid.astype(jnp.float32)).astype(jnp.bfloat16)
     return high, mid, low
+
+def gram_blocks(total):
+    high, mid, low = pieces(total)
+    rows = (((0,), (0,)), ((), ()))
+    product = functools.partial(
+        lax.dot_general, dimension_numbers=rows, preferred_element_type=jnp.float32
+    )
+    small = product(high, mid) + product(high, low)
+    whole = product(high, high) + (product(mid, mid) + (small + small.T))
+    return whole[:LANES, :LANES], whole[:LANES, LANES:], whole[LANES:, LANES:]
+
+
+def collect_kernel(scale, *refs):
+    kept, out, copy, gram = refs[0], refs[-3], refs[-2], refs[-1]
+    total = kept[...]
+    for ref in refs[1:-3]:
+        total = total + decoded(ref, kept.shape[0])
+    out[...] = total
+    copy[...] = total
+    first, corner, second = (scale * block for block in gram_blocks(total))
+
+    row = lax.broadcasted_iota(jnp.int32, first.shape, 0)
+    column = lax.broadcasted_iota(jnp.int32, first.shape, 1)
+    gram[:LANES] = jnp.where(row <= column, first, second)
+    gram[LANES : 2 * LANES] = corner
+    gram[2 * LANES :] = jnp.zeros((PAD, LANES), jnp.float32)
+    gram[2 * LANES : 2 * LANES + 1] = jnp.sum(
+        jnp.where(row == column, second, 0.0), axis=0, keepdims=True
+    )
+
+
+def unpack_gram(packed, table):
+    mixed = packed[:LANES]
+    turned = mixed.T
+    row = lax.broadcasted_iota(jnp.int32, mixed.shape, 0)
+    column = lax.broadcasted_iota(jnp.int32, mixed.shape, 1)
+    table[:LANES, :LANES] = jnp.where(row <= column, mixed, turned)
+    second = jnp.where(row > column, mixed, turned)
+    table[LANES:, LANES:] = jnp.where(row == column, packed[2 * LANES : 2 * LANES + 1], second)
+    table[:LANES, LANES:] = packed[LANES : 2 * LANES]
+    table[LANES:, :LANES] = jnp.zeros((LANES, LANES), jnp.float32)
+
+
+def collect(kept, received, scale):
+    width = kept.shape[1]
+    return pl.pallas_call(
+        functools.partial(collect_kernel, scale),
+        out_shape=[
+            jax.ShapeDtypeStruct(kept.shape, jnp.float32),
+            jax.ShapeDtypeStruct(kept.shape, jnp.float32),
+            jax.ShapeDtypeStruct((width + PAD, LANES), jnp.float32),
+        ],
+        compiler_params=params(),
+        name="collect",
+    )(kept, *received)
+
 
 def factor(table, r_out):
     width = table.shape[0]
@@ -242,7 +350,7 @@
             table[end:, :] = keep - change[end - begin :]
 
 def basis_kernel(gram, y, r_out, q_out, table):
-    table[...] = gram[...]
+    unpack_gram(gram, table)
     factor(table, r_out)
     q_out[...] = lax.dot_general(
         y[...],
@@ -254,7 +362,7 @@
 
 
 def orthonormalize(gram, y):
-    width = gram.shape[0]
+    width = y.shape[1]
     return pl.pallas_call(
         basis_kernel,
         out_shape=[
@@ -268,7 +376,7 @@
 
 
 def swap(array, axis, mask):
-    size = lax.axis_size(axis)
+    size = math.prod(lax.axis_size(name) for name in (axis if isinstance(axis, tuple) else (axis,)))
     return lax.ppermute(array, axis, [(i, i ^ mask) for i in range(size)])
 
 
@@ -279,22 +387,19 @@
     return mine, swap(other, axis, mask)
 
 
+def both(mine, got, first):
+    return jnp.concatenate([jnp.where(first, mine, got), jnp.where(first, got, mine)], axis=0)
+
+
 def gram_total(gram):
-    width = gram.shape[0]
-    n_snp, n_samp = lax.axis_size("snp"), lax.axis_size("samp")
-    if n_snp != 4 or n_samp != 4:
+    rows, width = gram.shape
+    if lax.axis_size("snp") != 4 or lax.axis_size("samp") != 4:
         return lax.psum(gram, ("samp", "snp"))
-    mine, got = halve(gram.reshape(2, width // 2, width), "snp", 1)
+    mine, got = halve(gram.reshape(2, rows // 2, width), "snp", 1)
     part = mine + got
-    mine, got = halve(part.reshape(2, width // 4, width), "snp", 2)
-    part = mine + got
-    part = ((part + swap(part, "samp", 1)) + (swap(part, "samp", 2) + swap(part, "samp", 3)))
-    x_bit = (lax.axis_index("snp") // 2) == 0
-    c_bit = (lax.axis_index("snp") % 2) == 0
-    got = swap(part, "snp", 2)
-    part = jnp.concatenate([jnp.where(x_bit, part, got), jnp.where(x_bit, got, part)], axis=0)
-    got = swap(part, "snp", 1)
-    return jnp.concatenate([jnp.where(c_bit, part, got), jnp.where(c_bit, got, part)], axis=0)
+    part = part + swap(part, "snp", 2)
+    part = (part + swap(part, "samp", 1)) + (swap(part, "samp", 2) + swap(part, "samp", 3))
+    return both(part, swap(part, "snp", 1), jnp.bitwise_and(lax.axis_index("snp"), 1) == 0)
 
 
 def per_device(genotypes, basis_cols):
@@ -306,49 +411,48 @@
     inv_root = float(1.0 / samples**0.5)
     blocks = n_snp // 2
     depth = words // n_snp
-    me = lax.axis_index("snp")
-    low = (me & 1).astype(jnp.int32)
-
-    other, other_sums = project(genotypes, basis_cols, (1 - low)[None], blocks)
+
+    other, sums = project(genotypes, basis_cols, blocks, True)
+    if n_samp <= 4:
+        more = swap(sums, "samp", 1)
+    else:
+        more = lax.psum(sums, "samp") - sums
     got = swap(other, "snp", 1)
-    mine, mine_sums = project(genotypes, basis_cols, low[None], blocks)
-    part = mine + got
-    sums = mine_sums + other_sums
+    (mine,) = project(genotypes, basis_cols, blocks, False)
     for b in range(1, bits):
-        shape = (2, part.shape[0] // 2) + part.shape[1:]
-        keep, got = halve(part.reshape(shape), "snp", 1 << b)
-        part = keep + got
-    if n_snp * n_samp <= 16:
-        every = jnp.broadcast_to(sums[None], (n_snp * n_samp,) + sums.shape)
-        center = lax.all_to_all(every, ("samp", "snp"), 0, 0, tiled=True).sum(axis=(0, 1))
-    else:
-        center = lax.psum(sums, ("samp", "snp")).sum(axis=0)
-    center = center / jnp.float32(samples)
-    rows = (part.reshape(PLANES * depth, width) - center[None, :]).astype(jnp.bfloat16)
+        send, mine, sums = merge(mine, got, b, sums, more)
+        got = swap(send, "snp", 1 << b)
+        more = jnp.zeros_like(sums)
+    if n_samp <= 4:
+        for b in range(1, n_samp.bit_length() - 1):
+            sums = sums + swap(sums, "samp", 1 << b)
+    for b in range(bits):
+        sums = sums + swap(sums, "snp", 1 << b)
+    rows = finish(mine, got, sums, samples)
     scores = lax.all_gather(rows, "snp").reshape(n_snp, PLANES, depth, width)
 
     chunk = snps // n_samp
-    z = lax.axis_index("samp").astype(jnp.int32)
     total_snps = snps * n_snp
     if n_samp <= 4 and chunk % 128 == 0:
         received = []
         for mask in range(n_samp - 1, 0, -1):
-            coded = chunk_of_y(genotypes, scores, (z ^ mask)[None], chunk, inv_root, True)
+            coded = chunk_of_y(genotypes, scores, chunk, inv_root, mask)
             received.append(swap(coded, "samp", mask))
-        kept = chunk_of_y(genotypes, scores, z[None], chunk, inv_root, False)
-        y_local, gram = collect(kept, received, 1.0 / total_snps)
+        kept = chunk_of_y(genotypes, scores, chunk, inv_root, 0)
+        kept = add_chunk(kept, received[0])
+        y_local, y_again, gram = collect(kept, received[1:], 1.0 / total_snps)
     else:
         tile = 512 if snps % 512 == 0 else snps
         parts = [
-            chunk_of_y(genotypes, scores, jnp.full((1,), i, jnp.int32), tile, inv_root, False)
+            chunk_of_y(genotypes, scores, tile, inv_root, None, i)
             for i in range(snps // tile)
         ]
         y_local = lax.psum_scatter(
             jnp.concatenate(parts, axis=0), "samp", scatter_dimension=0, tiled=True
         )
-        y_local, gram = collect(y_local, [], 1.0 / total_snps)
+        y_local, y_again, gram = collect(y_local, [], 1.0 / total_snps)
     gram_sum = gram_total(gram)
-    r_factor, q_next = orthonormalize(gram_sum, y_local)
+    r_factor, q_next = orthonormalize(gram_sum, y_again)
     layout = (1, 1, y_local.shape[0], width)
     return (y_local.reshape(layout), r_factor, q_next.reshape(layout))
 

time: 101 us -> 87.3 us (0.86)
  waiting for transfers between devices: 45.3 us -> 38.3 us
  other arithmetic: 2.47 us -> 0.07 us
  starting transfers between devices: 20.1 us -> 18 us
  local copies, waits for them, and re-layouts: 4.41 us -> 2.82 us
    all_to_all x1 -> x0, starting transfers between devices: 7.02 us -> none  [per_device(): lax.all_to_all(every, ('samp', 'snp'), 0, 0, tiled=True).sum(axis=(0, 1))]
    ppermute x12 -> x15, starting transfers between devices: 13.1 us -> 18 us  [swap(): return lax.ppermute(array, axis, [(i, i ^ mask) for i in range(size)])]
    all_to_all x1 -> x0, waiting for transfers between devices: 3.79 us -> none  [per_device(): lax.all_to_all(every, ('samp', 'snp'), 0, 0, tiled=True).sum(axis=(0, 1))]
    ppermute x12 -> x15, waiting for transfers between devices: 41.5 us -> 38.3 us  [swap(): return lax.ppermute(array, axis, [(i, i ^ mask) for i in range(size)])]
    add x3 -> x4, other arithmetic: 2.29 us -> 0.02 us  [the longest x1 0.01 us: gram_total(): part = part + swap(part, 'snp', 2)]
    unnamed x10 -> x6, local copies, waits for them, and re-layouts: 3.7 us -> 2.82 us
    pallas_call x6 -> x9, Pallas kernels: 8.31 us -> 7.62 us  [the longest x4 3.98 us: chunk_of_y(): pl.pallas_call(kernel, out_shape=jax.ShapeDtypeStruct(shape, dtype), comp...]
  transfers between devices with their start and end apart: 13 -> 15, of which waited for: 10 -> 11; matrix products, arithmetic and copies ran while one was open for 2% -> 0% of each run, Pallas kernels for 2% -> 4%
where the time goes in v3:
time: 87.3 us; the launch traced here: 87 us
  waiting for transfers between devices  38.3 us (44%)
  Pallas kernels  18.7 us (21%)
  starting transfers between devices  18 us (21%)
  blocking collectives  8.4 us (10%)
  local copies, waits for them, and re-layouts  2.82 us (3%)
    ppermute x15, waiting for transfers between devices, swap(): return lax.ppermute(array, axis, [(i, i ^ mask) for i in range(size)])  38.3 us
    ppermute x15, starting transfers between devices, swap(): return lax.ppermute(array, axis, [(i, i ^ mask) for i in range(size)])  18 us
    pallas_call x1, Pallas kernels, orthonormalize(): pl.pallas_call(basis_kernel, out_shape=[jax.ShapeDtypeStruct((width, widt...  8.99 us
    all_gather x1, blocking collectives, per_device(): scores = lax.all_gather(rows, 'snp').reshape(n_snp, PLANES, depth, width)  8.4 us
    pallas_call x4, Pallas kernels, chunk_of_y(): pl.pallas_call(kernel, out_shape=jax.ShapeDtypeStruct(shape, dtype), comp...  3.98 us
    unnamed x6, local copies, waits for them, and re-layouts  2.82 us
    pallas_call x2, Pallas kernels, project(): pl.pallas_call(other_kernel if other else mine_kernel, out_shape=shapes,...  2.46 us
    pallas_call x1, Pallas kernels, collect(): pl.pallas_call(functools.partial(collect_kernel, scale), out_shape=[jax.S...  2.07 us
  transfers between devices with their start and end apart: 15, of which 11 were waited for; matrix products, arithmetic and copies ran while one was open for 0% of the time, Pallas kernels for 4%

profile of v3, /device:TPU:0, one launch (start us, length us, event | category | flops | bytes accessed | tf_op | source)
XLA Modules:
  0.0 87.0 jit_solution(8742770454768403434)
XLA Ops:
  0.6 0.0 copy-start
  0.6 1.6 %copy-done = s32[256,2048]{1,0:T(8,128)S(1)} copy-done((s32[256,2048]{1,0:T(8,128)S(1)}, s32[256,2048]{1,0:T(8,128)}, u32[]{:S(2)}) %copy-start) | copy-done | bytes 2097176
  2.2 0.0 copy-start.2
  2.2 1.2 %copy-done.2 = bf16[2048,256]{1,0:T(8,128)(2,1)S(1)} copy-done((bf16[2048,256]{1,0:T(8,128)(2,1)S(1)}, bf16[2048,256]{1,0:T(8,128)(2,1)}, u32[]{:S(2)}) %copy-start.2) | copy-done | bytes 1048600
  3.4 1.5 %project_other.1 = (f32[2,6,64,256]{3,2,1,0:T(8,128)S(1)}, f32[8,256]{1,0:T(8,128)S(1)}) custom-call(s32[256,2048]{1,0:T(8,128)S(1)} %copy-done, bf16[2048,256]{1,0:T(8,128)(2,1)S(1)} %copy-done.2), custom_call_target="tpu_custom_call" | custom-call | flops 805306368 | bytes 2883584 | tf_op jit(solution)/shard_map/project_other/pallas_call | solution.py:82
  4.9 0.5 collective-permute-start
  5.4 2.7 %collective-permute-start.1 = (f32[8,256]{1,0:T(8,128)S(1)}, f32[8,256]{1,0:T(8,128)S(1)}, u32[]{:S(2)}, u32[]{:S(2)}) collective-permute-start(f32[8,256]{1,0:T(8,128)S(1)} %get-tuple-element.14.sums), channel_id=1, source_target_pairs={{0,4},{4,0},{8,12},{12,8},{1,5},{5,1},{9,13},{13,9},{2,6},{6,2},{1... | collective-permute-start | bytes 24584 | tf_op jit(solution)/shard_map/ppermute | solution.py:380
  8.1 1.0 %project_mine.1.mine = f32[2,6,64,256]{3,2,1,0:T(8,128)S(1)} custom-call(s32[256,2048]{1,0:T(8,128)S(1)} %copy-done, bf16[2048,256]{1,0:T(8,128)(2,1)S(1)} %copy-done.2), custom_call_target="tpu_custom_call" | custom-call | flops 805306368 | bytes 2883584 | tf_op jit(solution)/shard_map/project_mine/pallas_call | solution.py:82
  9.1 0.0 copy-start.1
  9.1 0.6 collective-permute-done.1.more
  9.7 0.0 collective-permute-done.got
  9.7 0.1 merge.1
  9.8 2.0 %collective-permute-start.2 = (f32[1,6,64,256]{3,2,1,0:T(8,128)S(1)}, f32[1,6,64,256]{3,2,1,0:T(8,128)S(1)}, u32[]{:S(2)}, u32[]{:S(2)}) collective-permute-start(f32[1,6,64,256]{3,2,1,0:T(8,128)S(1)} %get-tuple-element.16), channel_id=1, source_target_pairs={{0,2},{1,3},{2,0},{3,1},{4,6},{5,7},{6,4},{7,5},{8,10},{9,11},{10,... | collective-permute-start | bytes 1179656 | tf_op jit(solution)/shard_map/ppermute | solution.py:380
  11.8 2.6 %collective-permute-start.3 = (f32[8,256]{1,0:T(8,128)S(1)}, f32[8,256]{1,0:T(8,128)S(1)}, u32[]{:S(2)}, u32[]{:S(2)}) collective-permute-start(f32[8,256]{1,0:T(8,128)S(1)} %get-tuple-element.17), channel_id=1, source_target_pairs={{0,8},{4,12},{8,0},{12,4},{1,9},{5,13},{9,1},{13,5},{2,10},{6,14},... | collective-permute-start | bytes 24584 | tf_op jit(solution)/shard_map/ppermute | solution.py:380
  14.4 2.0 %collective-permute-done.3 = f32[8,256]{1,0:T(8,128)S(1)} collective-permute-done((f32[8,256]{1,0:T(8,128)S(1)}, f32[8,256]{1,0:T(8,128)S(1)}, u32[]{:S(2)}, u32[]{:S(2)}) %collective-permute-start.3) | collective-permute-done | bytes 8224 | tf_op jit(solution)/shard_map/ppermute | solution.py:380
  16.4 0.0 collective-permute-start.4
  16.4 1.2 %collective-permute-done.4 = f32[8,256]{1,0:T(8,128)S(1)} collective-permute-done((f32[8,256]{1,0:T(8,128)S(1)}, f32[8,256]{1,0:T(8,128)S(1)}, u32[]{:S(2)}, u32[]{:S(2)}) %collective-permute-start.4) | collective-permute-done | bytes 8224 | tf_op jit(solution)/shard_map/ppermute | solution.py:380
  17.6 0.2 collective-permute-start.5
  17.8 3.4 %collective-permute-done.5 = f32[8,256]{1,0:T(8,128)S(1)} collective-permute-done((f32[8,256]{1,0:T(8,128)S(1)}, f32[8,256]{1,0:T(8,128)S(1)}, u32[]{:S(2)}, u32[]{:S(2)}) %collective-permute-start.5) | collective-permute-done | bytes 8224 | tf_op jit(solution)/shard_map/ppermute | solution.py:380
  21.2 0.0 collective-permute-done.2.got
  21.2 0.1 finish.1
  21.3 8.4 %all-gather = bf16[1536,256]{1,0:T(8,128)(2,1)S(1)} all-gather(bf16[384,256]{1,0:T(8,128)(2,1)S(1)} %finish.1), channel_id=2, replica_groups=mesh['grp'=2,'samp'=4,'snp'=4] {'snp'}, dimensions={0}, use_global_device_ids=true | all-gather | bytes 983040 | tf_op jit(solution)/shard_map/all_gather | solution.py:432
  29.7 0.0 copy-done.1
  29.7 1.6 %chunk_sent.3 = s16[528,256]{1,0:T(8,128)(2,1)} custom-call(s32[256,2048]{1,0:T(8,128)S(1)} %copy-done.1, bf16[4,6,64,256]{3,2,1,0:T(8,128)(2,1)S(1)} %bitcast.8), custom_call_target="tpu_custom_call" | custom-call | flops 402653184 | bytes 1835008 | tf_op jit(solution)/shard_map/chunk_sent/pallas_call | solution.py:180
  31.2 0.8 chunk_sent.4
  32.1 3.7 %collective-permute-start.6 = (s16[528,256]{1,0:T(8,128)(2,1)}, s16[528,256]{1,0:T(8,128)(2,1)}, u32[]{:S(2)}, u32[]{:S(2)}) collective-permute-start(s16[528,256]{1,0:T(8,128)(2,1)} %chunk_sent.3), channel_id=1, source_target_pairs={{0,12},{4,8},{8,4},{12,0},{1,13},{5,9},{9,5},{13,1},{2,14},{6,10},... | collective-permute-start | bytes 811016 | tf_op jit(solution)/shard_map/ppermute | solution.py:380
  35.8 0.8 chunk_sent.5
  36.6 0.1 collective-permute-start.7
  36.7 0.8 collective-permute-start.8
  37.5 0.8 chunk_kept.1.kept
  38.2 5.5 %collective-permute-done.6.coded = s16[528,256]{1,0:T(8,128)(2,1)} collective-permute-done((s16[528,256]{1,0:T(8,128)(2,1)}, s16[528,256]{1,0:T(8,128)(2,1)}, u32[]{:S(2)}, u32[]{:S(2)}) %collective-permute-start.6) | collective-permute-done | bytes 270368 | tf_op jit(solution)/shard_map/ppermute | solution.py:380
  43.7 1.0 %add_chunk.1.refs_0_ = f32[512,256]{1,0:T(8,128)S(1)} custom-call(f32[512,256]{1,0:T(8,128)S(1)} %chunk_kept.1.kept, s16[528,256]{1,0:T(8,128)(2,1)} %collective-permute-done.6.coded), custom_call_target="tpu_custom_call" | custom-call | flops 524288 | bytes 1310720 | tf_op jit(solution)/shard_map/add_chunk/pallas_call | solution.py:203
  44.7 14.9 %collective-permute-done.7.refs_1_ = s16[528,256]{1,0:T(8,128)(2,1)} collective-permute-done((s16[528,256]{1,0:T(8,128)(2,1)S(1)}, s16[528,256]{1,0:T(8,128)(2,1)}, u32[]{:S(2)}, u32[]{:S(2)}) %collective-permute-start.7) | collective-permute-done | bytes 270368 | tf_op jit(solution)/shard_map/ppermute | solution.py:380
  59.6 0.0 collective-permute-done.8.refs_2_
  59.6 2.1 %collect.1 = (f32[512,256]{1,0:T(8,128)}, f32[512,256]{1,0:T(8,128)S(1)}, f32[288,128]{1,0:T(8,128)S(1)}) custom-call(f32[512,256]{1,0:T(8,128)S(1)} %add_chunk.1.refs_0_, s16[528,256]{1,0:T(8,128)(2,1)} %collective-permute-done.7.refs_1_, s16[528,256]{1,0:T(8,128)(2,1)} %collective-permute-done.8.refs_2_), custom_call_target="tpu_custom_call" | custom-call | tf_op jit(solution)/shard_map/collect/pallas_call | solution.py:265
  61.7 0.0 collective-permute-start.9
  61.7 1.3 %collective-permute-done.9 = f32[144,128]{1,0:T(8,128)S(1)} collective-permute-done((f32[144,128]{1,0:T(8,128)S(1)}, f32[144,128]{1,0:T(8,128)S(1)}, u32[]{:S(2)}, u32[]{:S(2)}) %collective-permute-start.9) | collective-permute-done | bytes 73760 | tf_op jit(solution)/shard_map/ppermute | solution.py:380
  63.0 1.0 %collective-permute-start.10 = (f32[144,128]{1,0:T(8,128)S(1)}, f32[144,128]{1,0:T(8,128)S(1)}, u32[]{:S(2)}, u32[]{:S(2)}) collective-permute-start(f32[144,128]{1,0:T(8,128)S(1)} %bitcast_add_fusion), channel_id=1, source_target_pairs={{0,2},{1,3},{2,0},{3,1},{4,6},{5,7},{6,4},{7,5},{8,10},{9,11},{10,... | collective-permute-start | bytes 221192 | tf_op jit(solution)/shard_map/ppermute | solution.py:380
  63.9 3.4 %collective-permute-done.10 = f32[144,128]{1,0:T(8,128)S(1)} collective-permute-done((f32[144,128]{1,0:T(8,128)S(1)}, f32[144,128]{1,0:T(8,128)S(1)}, u32[]{:S(2)}, u32[]{:S(2)}) %collective-permute-start.10) | collective-permute-done | bytes 73760 | tf_op jit(solution)/shard_map/ppermute | solution.py:380
  67.4 0.1 collective-permute-start.11
  67.5 3.0 %collective-permute-start.12 = (f32[144,128]{1,0:T(8,128)S(1)}, f32[144,128]{1,0:T(8,128)S(1)}, u32[]{:S(2)}, u32[]{:S(2)}) collective-permute-start(f32[144,128]{1,0:T(8,128)S(1)} %add.39), channel_id=1, source_target_pairs={{0,8},{4,12},{8,0},{12,4},{1,9},{5,13},{9,1},{13,5},{2,10},{6,14},... | collective-permute-start | bytes 221192 | tf_op jit(solution)/shard_map/ppermute | solution.py:380
  70.5 1.3 %collective-permute-start.13 = (f32[144,128]{1,0:T(8,128)S(1)}, f32[144,128]{1,0:T(8,128)S(1)}, u32[]{:S(2)}, u32[]{:S(2)}) collective-permute-start(f32[144,128]{1,0:T(8,128)S(1)} %add.39), channel_id=1, source_target_pairs={{0,12},{4,8},{8,4},{12,0},{1,13},{5,9},{9,5},{13,1},{2,14},{6,10},... | collective-permute-start | bytes 221192 | tf_op jit(solution)/shard_map/ppermute | solution.py:380
  71.8 0.0 collective-permute-done.11
  71.8 3.2 %collective-permute-done.12 = f32[144,128]{1,0:T(8,128)S(1)} collective-permute-done((f32[144,128]{1,0:T(8,128)S(1)}, f32[144,128]{1,0:T(8,128)S(1)}, u32[]{:S(2)}, u32[]{:S(2)}) %collective-permute-start.12) | collective-permute-done | bytes 73760 | tf_op jit(solution)/shard_map/ppermute | solution.py:380
  75.1 1.6 %collective-permute-done.13 = f32[144,128]{1,0:T(8,128)S(1)} collective-permute-done((f32[144,128]{1,0:T(8,128)S(1)}, f32[144,128]{1,0:T(8,128)S(1)}, u32[]{:S(2)}, u32[]{:S(2)}) %collective-permute-start.13) | collective-permute-done | bytes 73760 | tf_op jit(solution)/shard_map/ppermute | solution.py:380
  76.7 0.1 collective-permute-start.14
  76.8 1.2 %collective-permute-done.14 = f32[144,128]{1,0:T(8,128)S(1)} collective-permute-done((f32[144,128]{1,0:T(8,128)S(1)}, f32[144,128]{1,0:T(8,128)S(1)}, u32[]{:S(2)}, u32[]{:S(2)}) %collective-permute-start.14) | collective-permute-done | bytes 73760 | tf_op jit(solution)/shard_map/ppermute | solution.py:380
  78.1 9.0 %orthonormalize.1 = (f32[256,256]{1,0:T(8,128)}, f32[512,256]{1,0:T(8,128)}) custom-call(f32[288,128]{1,0:T(8,128)S(1)} %pad_maximum_fusion.gram, f32[512,256]{1,0:T(8,128)S(1)} %get-tuple-element.20.y), custom_call_target="tpu_custom_call" | custom-call | tf_op jit(solution)/shard_map/orthonormalize/pallas_call | solution.py:366
  (9 shorter events, 0.1 us)
Async XLA Ops:
  0.6 1.6 %copy-start = (s32[256,2048]{1,0:T(8,128)S(1)}, s32[256,2048]{1,0:T(8,128)}, u32[]{:S(2)}) copy-start(s32[256,2048]{1,0:T(8,128)} %words.11) | copy-start | bytes 6291460
  2.2 1.2 %copy-start.2 = (bf16[2048,256]{1,0:T(8,128)(2,1)S(1)}, bf16[2048,256]{1,0:T(8,128)(2,1)}, u32[]{:S(2)}) copy-start(bf16[2048,256]{1,0:T(8,128)(2,1)} %basis.3) | copy-start | bytes 3145732
  4.9 4.8 %collective-permute-start = (f32[2,6,64,256]{3,2,1,0:T(8,128)S(1)}, f32[2,6,64,256]{3,2,1,0:T(8,128)S(1)}, u32[]{:S(2)}, u32[]{:S(2)}) collective-permute-start(f32[2,6,64,256]{3,2,1,0:T(8,128)S(1)} %get-tuple-element.13), channel_id=1, source_target_pairs={{0,1},{1,0},{2,3},{3,2},{4,5},{5,4},{6,7},{7,6},{8,9},{9,8},{10,11... | collective-permute-start | bytes 2359304 | tf_op jit(solution)/shard_map/ppermute | solution.py:380
  5.4 4.3 %collective-permute-start.1 = (f32[8,256]{1,0:T(8,128)S(1)}, f32[8,256]{1,0:T(8,128)S(1)}, u32[]{:S(2)}, u32[]{:S(2)}) collective-permute-start(f32[8,256]{1,0:T(8,128)S(1)} %get-tuple-element.14.sums), channel_id=1, source_target_pairs={{0,4},{4,0},{8,12},{12,8},{1,5},{5,1},{9,13},{13,9},{2,6},{6,2},{1... | collective-permute-start | bytes 24584 | tf_op jit(solution)/shard_map/ppermute | solution.py:380
  9.1 20.6 %copy-start.1 = (s32[256,2048]{1,0:T(8,128)S(1)}, s32[256,2048]{1,0:T(8,128)}, u32[]{:S(2)}) copy-start(s32[256,2048]{1,0:T(8,128)} %words.11) | copy-start | bytes 6291460
  9.8 11.4 %collective-permute-start.2 = (f32[1,6,64,256]{3,2,1,0:T(8,128)S(1)}, f32[1,6,64,256]{3,2,1,0:T(8,128)S(1)}, u32[]{:S(2)}, u32[]{:S(2)}) collective-permute-start(f32[1,6,64,256]{3,2,1,0:T(8,128)S(1)} %get-tuple-element.16), channel_id=1, source_target_pairs={{0,2},{1,3},{2,0},{3,1},{4,6},{5,7},{6,4},{7,5},{8,10},{9,11},{10,... | collective-permute-start | bytes 1179656 | tf_op jit(solution)/shard_map/ppermute | solution.py:380
  11.8 4.5 %collective-permute-start.3 = (f32[8,256]{1,0:T(8,128)S(1)}, f32[8,256]{1,0:T(8,128)S(1)}, u32[]{:S(2)}, u32[]{:S(2)}) collective-permute-start(f32[8,256]{1,0:T(8,128)S(1)} %get-tuple-element.17), channel_id=1, source_target_pairs={{0,8},{4,12},{8,0},{12,4},{1,9},{5,13},{9,1},{13,5},{2,10},{6,14},... | collective-permute-start | bytes 24584 | tf_op jit(solution)/shard_map/ppermute | solution.py:380
  16.4 1.2 %collective-permute-start.4 = (f32[8,256]{1,0:T(8,128)S(1)}, f32[8,256]{1,0:T(8,128)S(1)}, u32[]{:S(2)}, u32[]{:S(2)}) collective-permute-start(f32[8,256]{1,0:T(8,128)S(1)} %add.33), channel_id=1, source_target_pairs={{0,1},{1,0},{2,3},{3,2},{4,5},{5,4},{6,7},{7,6},{8,9},{9,8},{10,11... | collective-permute-start | bytes 24584 | tf_op jit(solution)/shard_map/ppermute | solution.py:380
  17.6 3.7 %collective-permute-start.5 = (f32[8,256]{1,0:T(8,128)S(1)}, f32[8,256]{1,0:T(8,128)S(1)}, u32[]{:S(2)}, u32[]{:S(2)}) collective-permute-start(f32[8,256]{1,0:T(8,128)S(1)} %add.34), channel_id=1, source_target_pairs={{0,2},{1,3},{2,0},{3,1},{4,6},{5,7},{6,4},{7,5},{8,10},{9,11},{10,... | collective-permute-start | bytes 24584 | tf_op jit(solution)/shard_map/ppermute | solution.py:380
  32.1 11.6 %collective-permute-start.6 = (s16[528,256]{1,0:T(8,128)(2,1)}, s16[528,256]{1,0:T(8,128)(2,1)}, u32[]{:S(2)}, u32[]{:S(2)}) collective-permute-start(s16[528,256]{1,0:T(8,128)(2,1)} %chunk_sent.3), channel_id=1, source_target_pairs={{0,12},{4,8},{8,4},{12,0},{1,13},{5,9},{9,5},{13,1},{2,14},{6,10},... | collective-permute-start | bytes 811016 | tf_op jit(solution)/shard_map/ppermute | solution.py:380
  36.6 23.0 %collective-permute-start.7 = (s16[528,256]{1,0:T(8,128)(2,1)S(1)}, s16[528,256]{1,0:T(8,128)(2,1)}, u32[]{:S(2)}, u32[]{:S(2)}) collective-permute-start(s16[528,256]{1,0:T(8,128)(2,1)S(1)} %chunk_sent.4), channel_id=1, source_target_pairs={{0,8},{4,12},{8,0},{12,4},{1,9},{5,13},{9,1},{13,5},{2,10},{6,14},... | collective-permute-start | bytes 811016 | tf_op jit(solution)/shard_map/ppermute | solution.py:380
  36.7 22.9 %collective-permute-start.8 = (s16[528,256]{1,0:T(8,128)(2,1)S(1)}, s16[528,256]{1,0:T(8,128)(2,1)}, u32[]{:S(2)}, u32[]{:S(2)}) collective-permute-start(s16[528,256]{1,0:T(8,128)(2,1)S(1)} %chunk_sent.5), channel_id=1, source_target_pairs={{0,4},{4,0},{8,12},{12,8},{1,5},{5,1},{9,13},{13,9},{2,6},{6,2},{1... | collective-permute-start | bytes 811016 | tf_op jit(solution)/shard_map/ppermute | solution.py:380
  61.7 1.3 %collective-permute-start.9 = (f32[144,128]{1,0:T(8,128)S(1)}, f32[144,128]{1,0:T(8,128)S(1)}, u32[]{:S(2)}, u32[]{:S(2)}) collective-permute-start(f32[144,128]{1,0:T(8,128)S(1)} %dynamic-slice_bitcast_fusion), channel_id=1, source_target_pairs={{0,1},{1,0},{2,3},{3,2},{4,5},{5,4},{6,7},{7,6},{8,9},{9,8},{10,11... | collective-permute-start | bytes 221192 | tf_op jit(solution)/shard_map/ppermute | solution.py:380
  63.0 4.4 %collective-permute-start.10 = (f32[144,128]{1,0:T(8,128)S(1)}, f32[144,128]{1,0:T(8,128)S(1)}, u32[]{:S(2)}, u32[]{:S(2)}) collective-permute-start(f32[144,128]{1,0:T(8,128)S(1)} %bitcast_add_fusion), channel_id=1, source_target_pairs={{0,2},{1,3},{2,0},{3,1},{4,6},{5,7},{6,4},{7,5},{8,10},{9,11},{10,... | collective-permute-start | bytes 221192 | tf_op jit(solution)/shard_map/ppermute | solution.py:380
  67.4 4.5 %collective-permute-start.11 = (f32[144,128]{1,0:T(8,128)S(1)}, f32[144,128]{1,0:T(8,128)S(1)}, u32[]{:S(2)}, u32[]{:S(2)}) collective-permute-start(f32[144,128]{1,0:T(8,128)S(1)} %add.39), channel_id=1, source_target_pairs={{0,4},{4,0},{8,12},{12,8},{1,5},{5,1},{9,13},{13,9},{2,6},{6,2},{1... | collective-permute-start | bytes 221192 | tf_op jit(solution)/shard_map/ppermute | solution.py:380
  67.5 7.6 %collective-permute-start.12 = (f32[144,128]{1,0:T(8,128)S(1)}, f32[144,128]{1,0:T(8,128)S(1)}, u32[]{:S(2)}, u32[]{:S(2)}) collective-permute-start(f32[144,128]{1,0:T(8,128)S(1)} %add.39), channel_id=1, source_target_pairs={{0,8},{4,12},{8,0},{12,4},{1,9},{5,13},{9,1},{13,5},{2,10},{6,14},... | collective-permute-start | bytes 221192 | tf_op jit(solution)/shard_map/ppermute | solution.py:380
  70.5 6.2 %collective-permute-start.13 = (f32[144,128]{1,0:T(8,128)S(1)}, f32[144,128]{1,0:T(8,128)S(1)}, u32[]{:S(2)}, u32[]{:S(2)}) collective-permute-start(f32[144,128]{1,0:T(8,128)S(1)} %add.39), channel_id=1, source_target_pairs={{0,12},{4,8},{8,4},{12,0},{1,13},{5,9},{9,5},{13,1},{2,14},{6,10},... | collective-permute-start | bytes 221192 | tf_op jit(solution)/shard_map/ppermute | solution.py:380
  76.7 1.3 %collective-permute-start.14 = (f32[144,128]{1,0:T(8,128)S(1)}, f32[144,128]{1,0:T(8,128)S(1)}, u32[]{:S(2)}, u32[]{:S(2)}) collective-permute-start(f32[144,128]{1,0:T(8,128)S(1)} %add_add_fusion), channel_id=1, source_target_pairs={{0,1},{1,0},{2,3},{3,2},{4,5},{5,4},{6,7},{7,6},{8,9},{9,8},{10,11... | collective-permute-start | bytes 221192 | tf_op jit(solution)/shard_map/ppermute | solution.py:380

commit v4 on v3

--- a/solution.py
+++ b/solution.py
@@ -30,12 +30,9 @@
 
 def half_rows(words, basis, out, place):
     half = words.shape[0] // 2
-    blocks, _, depth, _ = out.shape
     part = words[pl.ds(pl.multiple_of(place * half, half), half)]
     for t, plane in enumerate(planes_of(part)):
-        product = jnp.dot(plane, basis[...], preferred_element_type=jnp.float32)
-        for b in range(blocks):
-            out[b, t] = product[b * depth : (b + 1) * depth]
+        out[t] = jnp.dot(plane, basis[...], preferred_element_type=jnp.float32)
 
 
 def low_bit():
@@ -72,11 +69,11 @@
     half_rows(words, basis, out, low_bit())
 
 
-def project(words, basis, blocks, other):
+def project(words, basis, other):
     count, snps = words.shape
     width = basis.shape[1]
     half = count // 2
-    shapes = [jax.ShapeDtypeStruct((blocks, PLANES, half // blocks, width), jnp.float32)]
+    shapes = [jax.ShapeDtypeStruct((PLANES, half, width), jnp.float32)]
     if other:
         shapes.append(jax.ShapeDtypeStruct((8, width), jnp.float32))
     return pl.pallas_call(
@@ -92,55 +89,45 @@
     )(words, basis)
 
 
-def merge_kernel(shift, mine, got, sums, more, send, keep, total):
-    half = send.shape[0]
-    bit = jnp.bitwise_and(jnp.right_shift(lax.axis_index("snp"), shift), 1)
-    for b in range(half):
-        for out, first in ((send, 1 - bit), (keep, bit)):
-            out[b] = mine[first * half + b] + got[first * half + b]
-    total[...] = sums[...] + more[...]
-
-
-def merge(mine, got, shift, sums, more):
-    half = (mine.shape[0] // 2,) + mine.shape[1:]
-    return pl.pallas_call(
-        functools.partial(merge_kernel, shift),
-        out_shape=[jax.ShapeDtypeStruct(half, jnp.float32)] * 2
+def merge_kernel(mine, got, sums, more, *outs):
+    span = outs[0].shape[-1]
+    for i, out in enumerate(outs[:-1]):
+        columns = slice(i * span, (i + 1) * span)
+        out[...] = mine[:, :, columns] + got[:, :, columns]
+    outs[-1][...] = sums[...] + more[...]
+
+
+def merge(mine, got, sums, more, groups):
+    shape = mine.shape[:2] + (mine.shape[2] // groups,)
+    return pl.pallas_call(
+        merge_kernel,
+        out_shape=[jax.ShapeDtypeStruct(shape, jnp.float32)] * groups
         + [jax.ShapeDtypeStruct(sums.shape, jnp.float32)],
         compiler_params=params(),
         name="merge",
     )(mine, got, sums, more)
 
 
-def finish_kernel(samples, mine, got, sums, out):
-    center = jnp.sum(sums[...], axis=0, keepdims=True) / jnp.float32(samples)
-    value = (mine[...] + got[...]).reshape(out.shape) - center
-    out[...] = value.astype(jnp.bfloat16)
-
-
-def finish(mine, got, sums, samples):
-    rows, width = mine.size // mine.shape[-1], mine.shape[-1]
-    return pl.pallas_call(
-        functools.partial(finish_kernel, samples),
-        out_shape=jax.ShapeDtypeStruct((rows, width), jnp.bfloat16),
+def finish_kernel(samples, group, mine, got, sums, out):
+    span = out.shape[-1]
+    columns = sums[:, group * span : (group + 1) * span]
+    center = jnp.sum(columns, axis=0, keepdims=True) / jnp.float32(samples)
+    out[...] = (mine[...] + got[...] - center[None]).astype(jnp.bfloat16)
+
+
+def finish(mine, got, sums, samples, group):
+    return pl.pallas_call(
+        functools.partial(finish_kernel, samples, group),
+        out_shape=jax.ShapeDtypeStruct(mine.shape, jnp.bfloat16),
         compiler_params=params(),
         name="finish",
     )(mine, got, sums)
 
 
-def bit_reverse(index, bits):
-    out = 0
-    for b in range(bits):
-        out |= ((index >> b) & 1) << (bits - 1 - b)
-    return out
-
-
-def back_project(words, scores, scale):
-    blocks = scores.shape[0]
-    bits = blocks.bit_length() - 1
+def back_project(words, mine, other, scale):
     total = None
     for t, plane in enumerate(planes_of(words)):
-        rows = jnp.concatenate([scores[bit_reverse(b, bits), t] for b in range(blocks)], axis=0)
+        rows = jnp.concatenate([mine[t], other[t]], axis=0)
         term = lax.dot_general(
             rows, plane, (((0,), (0,)), ((), ())), preferred_element_type=jnp.float32
         )
@@ -148,15 +135,19 @@
     return (total * scale).T
 
 
-def chunk_value(scale, mask, piece, words, scores, rows):
+def chunk_value(scale, mask, piece, words, mine, other, rows):
     index = piece if mask is None else jnp.bitwise_xor(lax.axis_index("samp"), mask)
     span = pl.ds(pl.multiple_of(index * rows, rows), rows)
-    return back_project(words[:, span], scores, scale)
-
-
-def sent_kernel(scale, mask, words, scores, out):
-    rows = out.shape[0] - 16
-    value = chunk_value(scale, mask, 0, words, scores, rows)
+    half = words.shape[0] // 2
+    first, second = (
+        words[pl.ds(pl.multiple_of(place * half, half), half), span]
+        for place in (low_bit(), 1 - low_bit())
+    )
+    return back_project(jnp.concatenate([first, second], axis=0), mine, other, scale)
+
+
+def encode(value, out):
+    rows = value.shape[0]
     top = jnp.maximum(jnp.max(jnp.abs(value), axis=0, keepdims=True), 1e-30)
     level = jnp.ceil(STEPS * jnp.log2(top / TOP)) + 1.0
     unit = jnp.exp2(level * (1.0 / STEPS))
@@ -165,29 +156,43 @@
     out[rows:] = jnp.broadcast_to(level, (16, level.shape[1])).astype(jnp.int32).astype(jnp.int16)
 
 
-def kept_kernel(scale, mask, piece, words, scores, out):
-    out[...] = chunk_value(scale, mask, piece, words, scores, out.shape[0])
-
-
-def chunk_of_y(words, scores, rows, scale, mask, piece=0):
-    width = scores.shape[-1]
-    sent = mask is not None and mask > 0
-    shape = (rows + 16, width) if sent else (rows, width)
-    dtype = jnp.int16 if sent else jnp.float32
-    kernel = functools.partial(sent_kernel, scale, mask)
-    if not sent:
-        kernel = functools.partial(kept_kernel, scale, mask, piece)
+def chunks_kernel(scale, masks, rows, words, mine, other, *outs):
+    for mask, out in zip(masks, outs):
+        value = chunk_value(scale, mask, 0, words, mine, other, rows)
+        if mask:
+            encode(value, out)
+        else:
+            out[...] = value
+
+
+def piece_kernel(scale, piece, words, mine, other, out):
+    out[...] = chunk_value(scale, None, piece, words, mine, other, out.shape[0])
+
+
+def chunks_of_y(words, scores, rows, scale, masks=None, piece=None):
+    width = scores[0].shape[-1]
+    if masks is None:
+        kernel = functools.partial(piece_kernel, scale, piece)
+        shapes = [jax.ShapeDtypeStruct((rows, width), jnp.float32)]
+    else:
+        kernel = functools.partial(chunks_kernel, scale, masks, rows)
+        shapes = [
+            jax.ShapeDtypeStruct((rows + 16, width), jnp.int16)
+            if mask
+            else jax.ShapeDtypeStruct((rows, width), jnp.float32)
+            for mask in masks
+        ]
     return pl.pallas_call(
         kernel,
-        out_shape=jax.ShapeDtypeStruct(shape, dtype),
-        compiler_params=params(),
-        name="chunk_sent" if sent else "chunk_kept",
+        out_shape=shapes,
+        compiler_params=params(),
+        name="chunks",
         cost_estimate=pl.CostEstimate(
-            flops=2 * words.shape[0] * PLANES * rows * width,
-            bytes_accessed=4 * words.shape[0] * rows + 2 * scores.size + 4 * rows * width,
+            flops=2 * words.shape[0] * PLANES * rows * width * len(shapes),
+            bytes_accessed=(4 * words.shape[0] + 4 * width) * rows * len(shapes),
             transcendentals=0,
         ),
-    )(words, scores)
+    )(words, *scores)
 
 
 def decoded(coded, rows):
@@ -195,20 +200,23 @@
     return coded[:rows].astype(jnp.int32).astype(jnp.float32) * jnp.exp2(level * (1.0 / STEPS))
 
 
-def add_kernel(kept, coded, out):
-    out[...] = kept[...] + decoded(coded, kept.shape[0])
-
-
-def add_chunk(kept, coded):
+def add_kernel(kept, *refs):
+    total = kept[...]
+    for ref in refs[:-1]:
+        total = total + decoded(ref, kept.shape[0])
+    refs[-1][...] = total
+
+
+def add_chunks(kept, received):
     return pl.pallas_call(
         add_kernel,
         out_shape=jax.ShapeDtypeStruct(kept.shape, jnp.float32),
         compiler_params=params(),
-        name="add_chunk",
+        name="add_chunks",
         cost_estimate=pl.CostEstimate(
             flops=4 * kept.size, bytes_accessed=10 * kept.size, transcendentals=0
         ),
-    )(kept, coded)
+    )(kept, *received)
 
 
 def pieces(x):
@@ -229,11 +237,12 @@
     return whole[:LANES, :LANES], whole[:LANES, LANES:], whole[LANES:, LANES:]
 
 
-def collect_kernel(scale, *refs):
-    kept, out, copy, gram = refs[0], refs[-3], refs[-2], refs[-1]
-    total = kept[...]
-    for ref in refs[1:-3]:
-        total = total + decoded(ref, kept.shape[0])
+def collect_kernel(scale, done, kept, *refs):
+    out, copy, gram = refs[-3:]
+    last = kept[...]
+    for ref in refs[:-3]:
+        last = last + decoded(ref, kept.shape[0])
+    total = jnp.concatenate([done[...], last], axis=1)
     out[...] = total
     copy[...] = total
     first, corner, second = (scale * block for block in gram_blocks(total))
@@ -260,18 +269,18 @@
     table[LANES:, :LANES] = jnp.zeros((LANES, LANES), jnp.float32)
 
 
-def collect(kept, received, scale):
-    width = kept.shape[1]
+def collect(done, kept, received, scale):
+    rows, width = kept.shape[0], done.shape[1] + kept.shape[1]
     return pl.pallas_call(
         functools.partial(collect_kernel, scale),
         out_shape=[
-            jax.ShapeDtypeStruct(kept.shape, jnp.float32),
-            jax.ShapeDtypeStruct(kept.shape, jnp.float32),
+            jax.ShapeDtypeStruct((rows, width), jnp.float32),
+            jax.ShapeDtypeStruct((rows, width), jnp.float32),
             jax.ShapeDtypeStruct((width + PAD, LANES), jnp.float32),
         ],
         compiler_params=params(),
         name="collect",
-    )(kept, *received)
+    )(done, kept, *received)
 
 
 def factor(table, r_out):
@@ -380,13 +389,6 @@
     return lax.ppermute(array, axis, [(i, i ^ mask) for i in range(size)])
 
 
-def halve(array, axis, mask):
-    bit = (lax.axis_index(axis) & mask) // mask
-    mine = lax.dynamic_index_in_dim(array, bit, 0, keepdims=False)
-    other = lax.dynamic_index_in_dim(array, 1 - bit, 0, keepdims=False)
-    return mine, swap(other, axis, mask)
-
-
 def both(mine, got, first):
     return jnp.concatenate([jnp.where(first, mine, got), jnp.where(first, got, mine)], axis=0)
 
@@ -395,11 +397,13 @@
     rows, width = gram.shape
     if lax.axis_size("snp") != 4 or lax.axis_size("samp") != 4:
         return lax.psum(gram, ("samp", "snp"))
-    mine, got = halve(gram.reshape(2, rows // 2, width), "snp", 1)
-    part = mine + got
+    bit = jnp.bitwise_and(lax.axis_index("snp"), 1)
+    halves = gram.reshape(2, rows // 2, width)
+    mine, other = (lax.dynamic_index_in_dim(halves, b, 0, keepdims=False) for b in (bit, 1 - bit))
+    part = mine + swap(other, "snp", 1)
     part = part + swap(part, "snp", 2)
     part = (part + swap(part, "samp", 1)) + (swap(part, "samp", 2) + swap(part, "samp", 3))
-    return both(part, swap(part, "snp", 1), jnp.bitwise_and(lax.axis_index("snp"), 1) == 0)
+    return both(part, swap(part, "snp", 1), bit == 0)
 
 
 def per_device(genotypes, basis_cols):
@@ -409,48 +413,53 @@
     width = basis_cols.shape[1]
     samples = words * PLANES * n_samp
     inv_root = float(1.0 / samples**0.5)
-    blocks = n_snp // 2
-    depth = words // n_snp
-
-    other, sums = project(genotypes, basis_cols, blocks, True)
+    chunk = snps // n_samp
+    direct = n_samp <= 4 and chunk % LANES == 0
+
+    other, sums = project(genotypes, basis_cols, True)
+    got = swap(other, "snp", 1)
+    if n_snp <= 4:
+        more = sum(swap(sums, "snp", mask) for mask in range(1, n_snp))
+    else:
+        more = lax.psum(sums, "snp") - sums
+    (mine,) = project(genotypes, basis_cols, False)
+    *parts, sums = merge(mine, got, sums, more, 2)
     if n_samp <= 4:
-        more = swap(sums, "samp", 1)
+        for b in range(n_samp.bit_length() - 1):
+            sums = sums + swap(sums, "samp", 1 << b)
     else:
-        more = lax.psum(sums, "samp") - sums
-    got = swap(other, "snp", 1)
-    (mine,) = project(genotypes, basis_cols, blocks, False)
-    for b in range(1, bits):
-        send, mine, sums = merge(mine, got, b, sums, more)
-        got = swap(send, "snp", 1 << b)
-        more = jnp.zeros_like(sums)
-    if n_samp <= 4:
-        for b in range(1, n_samp.bit_length() - 1):
-            sums = sums + swap(sums, "samp", 1 << b)
-    for b in range(bits):
-        sums = sums + swap(sums, "snp", 1 << b)
-    rows = finish(mine, got, sums, samples)
-    scores = lax.all_gather(rows, "snp").reshape(n_snp, PLANES, depth, width)
-
-    chunk = snps // n_samp
-    total_snps = snps * n_snp
-    if n_samp <= 4 and chunk % 128 == 0:
-        received = []
-        for mask in range(n_samp - 1, 0, -1):
-            coded = chunk_of_y(genotypes, scores, chunk, inv_root, mask)
-            received.append(swap(coded, "samp", mask))
-        kept = chunk_of_y(genotypes, scores, chunk, inv_root, 0)
-        kept = add_chunk(kept, received[0])
-        y_local, y_again, gram = collect(kept, received[1:], 1.0 / total_snps)
-    else:
-        tile = 512 if snps % 512 == 0 else snps
-        parts = [
-            chunk_of_y(genotypes, scores, tile, inv_root, None, i)
-            for i in range(snps // tile)
-        ]
-        y_local = lax.psum_scatter(
-            jnp.concatenate(parts, axis=0), "samp", scatter_dimension=0, tiled=True
-        )
-        y_local, y_again, gram = collect(y_local, [], 1.0 / total_snps)
+        sums = lax.psum(sums, "samp")
+
+    kept, received = [], []
+    got, sent = None, None
+    for group, part in enumerate(parts):
+        if got is not None:
+            part, _, _ = lax.optimization_barrier((part, got, sums))
+        for b in range(1, bits - 1):
+            part = part + swap(part, "snp", 1 << b)
+        got = swap(part, "snp", 1 << (bits - 1))
+        ready = got
+        if sent is not None:
+            ready, _ = lax.optimization_barrier((got, sent[0]))
+        rows = finish(part, ready, sums, samples, group)
+        scores = (rows, swap(rows, "snp", 1))
+        if direct:
+            masks = (2, 1, 3)
+            *coded, own = chunks_of_y(genotypes, scores, chunk, inv_root, masks + (0,))
+            kept.append(own)
+            received.append([swap(c, "samp", mask) for c, mask in zip(coded, masks)])
+            sent = received[-1]
+        else:
+            tile = 4 * LANES if snps % (4 * LANES) == 0 else snps
+            tiles = [
+                chunks_of_y(genotypes, scores, tile, inv_root, piece=i)[0]
+                for i in range(snps // tile)
+            ]
+            whole = jnp.concatenate(tiles, axis=0)
+            kept.append(lax.psum_scatter(whole, "samp", scatter_dimension=0, tiled=True))
+            received.append([])
+    done = add_chunks(kept[0], received[0]) if direct else kept[0]
+    y_local, y_again, gram = collect(done, kept[1], received[1], 1.0 / (snps * n_snp))
     gram_sum = gram_total(gram)
     r_factor, q_next = orthonormalize(gram_sum, y_again)
     layout = (1, 1, y_local.shape[0], width)

time: 87.3 us -> 83.4 us (0.955)
  blocking collectives: 8.4 us -> 0 us
  starting transfers between devices: 18 us -> 25.2 us
  Pallas kernels: 18.7 us -> 17.2 us
  waiting for transfers between devices: 38.3 us -> 37.2 us
    all_gather x1 -> x0, blocking collectives: 8.4 us -> none  [per_device(): scores = lax.all_gather(rows, 'snp').reshape(n_snp, PLANES, depth, width)]
    ppermute x15 -> x22, starting transfers between devices: 18 us -> 25.2 us  [swap(): return lax.ppermute(array, axis, [(i, i ^ mask) for i in range(size)])]
    ppermute x15 -> x22, waiting for transfers between devices: 38.3 us -> 37.2 us  [swap(): return lax.ppermute(array, axis, [(i, i ^ mask) for i in range(size)])]
    pallas_call x1, Pallas kernels: 2.07 us -> 1.02 us  [collect(): pl.pallas_call(functools.partial(collect_kernel, scale), out_shape=[jax.S...]
    pallas_call x7 -> x6, Pallas kernels: 5.17 us -> 4.75 us  [the longest x2 4.39 us: chunks_of_y(): pl.pallas_call(kernel, out_shape=shapes, compiler_params=params(), name='...]
  transfers between devices with their start and end apart: 15 -> 22, of which waited for: 11 -> 17; matrix products, arithmetic and copies ran while one was open for 0% -> 0% of each run, Pallas kernels for 4% -> 7%
where the time goes in v4:
time: 83.4 us; the launch traced here: 83.3 us
  waiting for transfers between devices  37.2 us (45%)
  starting transfers between devices  25.2 us (30%)
  Pallas kernels  17.2 us (21%)
  local copies, waits for them, and re-layouts  2.82 us (3%)
    ppermute x22, waiting for transfers between devices, swap(): return lax.ppermute(array, axis, [(i, i ^ mask) for i in range(size)])  37.2 us
    ppermute x22, starting transfers between devices, swap(): return lax.ppermute(array, axis, [(i, i ^ mask) for i in range(size)])  25.2 us
    pallas_call x1, Pallas kernels, orthonormalize(): pl.pallas_call(basis_kernel, out_shape=[jax.ShapeDtypeStruct((width, widt...  8.99 us
    pallas_call x2, Pallas kernels, chunks_of_y(): pl.pallas_call(kernel, out_shape=shapes, compiler_params=params(), name='...  4.39 us
    unnamed x6, local copies, waits for them, and re-layouts  2.82 us
    pallas_call x2, Pallas kernels, project(): pl.pallas_call(other_kernel if other else mine_kernel, out_shape=shapes,...  2.46 us
  transfers between devices with their start and end apart: 22, of which 17 were waited for; matrix products, arithmetic and copies ran while one was open for 0% of the time, Pallas kernels for 7%

profile of v4, /device:TPU:0, one launch (start us, length us, event | category | flops | bytes accessed | tf_op | source)
XLA Modules:
  0.0 83.3 jit_solution(699699757885232336)
XLA Ops:
  0.6 1.6 %copy-done = s32[256,2048]{1,0:T(8,128)S(1)} copy-done((s32[256,2048]{1,0:T(8,128)S(1)}, s32[256,2048]{1,0:T(8,128)}, u32[]{:S(2)}) %copy-start) | copy-done | bytes 2097176
  2.2 1.2 %copy-done.2 = bf16[2048,256]{1,0:T(8,128)(2,1)S(1)} copy-done((bf16[2048,256]{1,0:T(8,128)(2,1)S(1)}, bf16[2048,256]{1,0:T(8,128)(2,1)}, u32[]{:S(2)}) %copy-start.2) | copy-done | bytes 1048600
  3.4 1.5 %project_other.1 = (f32[6,128,256]{2,1,0:T(8,128)S(1)}, f32[8,256]{1,0:T(8,128)S(1)}) custom-call(s32[256,2048]{1,0:T(8,128)S(1)} %copy-done, bf16[2048,256]{1,0:T(8,128)(2,1)S(1)} %copy-done.2), custom_call_target="tpu_custom_call" | custom-call | flops 805306368 | bytes 2883584 | tf_op jit(solution)/shard_map/project_other/pallas_call | solution.py:79
  4.9 0.5 collective-permute-start
  5.5 0.1 collective-permute-start.1
  5.5 2.9 %collective-permute-start.2 = (f32[8,256]{1,0:T(8,128)S(1)}, f32[8,256]{1,0:T(8,128)S(1)}, u32[]{:S(2)}, u32[]{:S(2)}) collective-permute-start(f32[8,256]{1,0:T(8,128)S(1)} %get-tuple-element.24.sums), channel_id=1, source_target_pairs={{0,2},{1,3},{2,0},{3,1},{4,6},{5,7},{6,4},{7,5},{8,10},{9,11},{10,... | collective-permute-start | bytes 24584 | tf_op jit(solution)/shard_map/ppermute | solution.py:389
  8.5 1.0 %project_mine.1.mine = f32[6,128,256]{2,1,0:T(8,128)S(1)} custom-call(s32[256,2048]{1,0:T(8,128)S(1)} %copy-done, bf16[2048,256]{1,0:T(8,128)(2,1)S(1)} %copy-done.2), custom_call_target="tpu_custom_call" | custom-call | flops 805306368 | bytes 2883584 | tf_op jit(solution)/shard_map/project_mine/pallas_call | solution.py:79
  9.5 0.6 collective-permute-done.2
  10.1 1.5 %collective-permute-done.3 = f32[8,256]{1,0:T(8,128)S(1)} collective-permute-done((f32[8,256]{1,0:T(8,128)S(1)}, f32[8,256]{1,0:T(8,128)S(1)}, u32[]{:S(2)}, u32[]{:S(2)}) %collective-permute-start.3) | collective-permute-done | bytes 8224 | tf_op jit(solution)/shard_map/ppermute | solution.py:389
  11.6 0.1 merge.1
  11.7 0.6 collective-permute-start.4
  12.3 1.6 %collective-permute-start.5 = (f32[8,256]{1,0:T(8,128)S(1)}, f32[8,256]{1,0:T(8,128)S(1)}, u32[]{:S(2)}, u32[]{:S(2)}) collective-permute-start(f32[8,256]{1,0:T(8,128)S(1)} %get-tuple-element.26), channel_id=1, source_target_pairs={{0,4},{4,0},{8,12},{12,8},{1,5},{5,1},{9,13},{13,9},{2,6},{6,2},{1... | collective-permute-start | bytes 24584 | tf_op jit(solution)/shard_map/ppermute | solution.py:389
  13.9 2.0 %collective-permute-done.5 = f32[8,256]{1,0:T(8,128)S(1)} collective-permute-done((f32[8,256]{1,0:T(8,128)S(1)}, f32[8,256]{1,0:T(8,128)S(1)}, u32[]{:S(2)}, u32[]{:S(2)}) %collective-permute-start.5) | collective-permute-done | bytes 8224 | tf_op jit(solution)/shard_map/ppermute | solution.py:389
  15.9 2.6 %collective-permute-start.6 = (f32[8,256]{1,0:T(8,128)S(1)}, f32[8,256]{1,0:T(8,128)S(1)}, u32[]{:S(2)}, u32[]{:S(2)}) collective-permute-start(f32[8,256]{1,0:T(8,128)S(1)} %add.37), channel_id=1, source_target_pairs={{0,8},{4,12},{8,0},{12,4},{1,9},{5,13},{9,1},{13,5},{2,10},{6,14},... | collective-permute-start | bytes 24584 | tf_op jit(solution)/shard_map/ppermute | solution.py:389
  18.6 1.9 %collective-permute-done.6 = f32[8,256]{1,0:T(8,128)S(1)} collective-permute-done((f32[8,256]{1,0:T(8,128)S(1)}, f32[8,256]{1,0:T(8,128)S(1)}, u32[]{:S(2)}, u32[]{:S(2)}) %collective-permute-start.6) | collective-permute-done | bytes 8224 | tf_op jit(solution)/shard_map/ppermute | solution.py:389
  20.5 2.4 %collective-permute-done.4.got = f32[6,128,128]{2,1,0:T(8,128)S(1)} collective-permute-done((f32[6,128,128]{2,1,0:T(8,128)S(1)}, f32[6,128,128]{2,1,0:T(8,128)S(1)}, u32[]{:S(2)}, u32[]{:S(2)}) %collective-permute-start.4) | collective-permute-done | bytes 393248 | tf_op jit(solution)/shard_map/ppermute | solution.py:389
  22.9 0.1 finish.2.mine
  23.0 0.1 collective-permute-start.7
  23.0 0.6 collective-permute-start.11
  23.6 0.8 collective-permute-done.7.other
  24.5 2.2 %chunks.2 = (s16[528,128]{1,0:T(8,128)(2,1)S(1)}, s16[528,128]{1,0:T(8,128)(2,1)S(1)}, s16[528,128]{1,0:T(8,128)(2,1)S(1)}, f32[512,128]{1,0:T(8,128)S(1)}) custom-call(s32[256,2048]{1,0:T(8,128)S(1)} %copy-done.1, bf16[6,128,128]{2,1,0:T(8,128)(2,1)S(1)} %finish.2.mine, bf16[6,128,128]{2,1,0:T(8,128)(2,1)S(1)} %collective-permute-done.7.other), custom_call_target="tpu_custom_call" | custom-call | flops 805306368 | bytes 3145728 | tf_op jit(solution)/shard_map/chunks/pallas_call | solution.py:185
  26.7 2.7 %collective-permute-start.8 = (s16[528,128]{1,0:T(8,128)(2,1)S(1)}, s16[528,128]{1,0:T(8,128)(2,1)S(1)}, u32[]{:S(2)}, u32[]{:S(2)}) collective-permute-start(s16[528,128]{1,0:T(8,128)(2,1)S(1)} %get-tuple-element.28), channel_id=1, source_target_pairs={{0,8},{4,12},{8,0},{12,4},{1,9},{5,13},{9,1},{13,5},{2,10},{6,14},... | collective-permute-start | bytes 405512 | tf_op jit(solution)/shard_map/ppermute | solution.py:389
  29.3 6.8 %collective-permute-done.8.refs_0_ = s16[528,128]{1,0:T(8,128)(2,1)S(1)} collective-permute-done((s16[528,128]{1,0:T(8,128)(2,1)S(1)}, s16[528,128]{1,0:T(8,128)(2,1)S(1)}, u32[]{:S(2)}, u32[]{:S(2)}) %collective-permute-start.8) | collective-permute-done | bytes 135200 | tf_op jit(solution)/shard_map/ppermute | solution.py:389
  36.2 0.1 finish.3.mine
  36.2 0.1 collective-permute-start.12
  36.3 3.5 %collective-permute-start.10 = (s16[528,128]{1,0:T(8,128)(2,1)S(1)}, s16[528,128]{1,0:T(8,128)(2,1)S(1)}, u32[]{:S(2)}, u32[]{:S(2)}) collective-permute-start(s16[528,128]{1,0:T(8,128)(2,1)S(1)} %get-tuple-element.30), channel_id=1, source_target_pairs={{0,12},{4,8},{8,4},{12,0},{1,13},{5,9},{9,5},{13,1},{2,14},{6,10},... | collective-permute-start | bytes 405512 | tf_op jit(solution)/shard_map/ppermute | solution.py:389
  39.9 2.2 %chunks.3 = (s16[528,128]{1,0:T(8,128)(2,1)S(1)}, s16[528,128]{1,0:T(8,128)(2,1)S(1)}, s16[528,128]{1,0:T(8,128)(2,1)S(1)}, f32[512,128]{1,0:T(8,128)S(1)}) custom-call(s32[256,2048]{1,0:T(8,128)S(1)} %copy-done.1, bf16[6,128,128]{2,1,0:T(8,128)(2,1)S(1)} %finish.3.mine, bf16[6,128,128]{2,1,0:T(8,128)(2,1)S(1)} %collective-permute-done.12.other), custom_call_target="tpu_custom_call" | custom-call | flops 805306368 | bytes 3145728 | tf_op jit(solution)/shard_map/chunks/pallas_call | solution.py:185
  42.1 1.0 %collective-permute-start.13 = (s16[528,128]{1,0:T(8,128)(2,1)S(1)}, s16[528,128]{1,0:T(8,128)(2,1)S(1)}, u32[]{:S(2)}, u32[]{:S(2)}) collective-permute-start(s16[528,128]{1,0:T(8,128)(2,1)S(1)} %get-tuple-element.35), channel_id=1, source_target_pairs={{0,8},{4,12},{8,0},{12,4},{1,9},{5,13},{9,1},{13,5},{2,10},{6,14},... | collective-permute-start | bytes 405512 | tf_op jit(solution)/shard_map/ppermute | solution.py:389
  43.0 1.2 %collective-permute-start.14 = (s16[528,128]{1,0:T(8,128)(2,1)S(1)}, s16[528,128]{1,0:T(8,128)(2,1)S(1)}, u32[]{:S(2)}, u32[]{:S(2)}) collective-permute-start(s16[528,128]{1,0:T(8,128)(2,1)S(1)} %get-tuple-element.36), channel_id=1, source_target_pairs={{0,4},{4,0},{8,12},{12,8},{1,5},{5,1},{9,13},{13,9},{2,6},{6,2},{1... | collective-permute-start | bytes 405512 | tf_op jit(solution)/shard_map/ppermute | solution.py:389
  44.2 2.3 %collective-permute-start.15 = (s16[528,128]{1,0:T(8,128)(2,1)S(1)}, s16[528,128]{1,0:T(8,128)(2,1)S(1)}, u32[]{:S(2)}, u32[]{:S(2)}) collective-permute-start(s16[528,128]{1,0:T(8,128)(2,1)S(1)} %get-tuple-element.37), channel_id=1, source_target_pairs={{0,12},{4,8},{8,4},{12,0},{1,13},{5,9},{9,5},{13,1},{2,14},{6,10},... | collective-permute-start | bytes 405512 | tf_op jit(solution)/shard_map/ppermute | solution.py:389
  46.5 2.0 %collective-permute-done.9.refs_1_ = s16[528,128]{1,0:T(8,128)(2,1)S(1)} collective-permute-done((s16[528,128]{1,0:T(8,128)(2,1)S(1)}, s16[528,128]{1,0:T(8,128)(2,1)S(1)}, u32[]{:S(2)}, u32[]{:S(2)}) %collective-permute-start.9) | collective-permute-done | bytes 135200 | tf_op jit(solution)/shard_map/ppermute | solution.py:389
  48.5 0.1 add_chunks.1.done
  48.6 4.3 %collective-permute-done.13.refs_0_ = s16[528,128]{1,0:T(8,128)(2,1)S(1)} collective-permute-done((s16[528,128]{1,0:T(8,128)(2,1)S(1)}, s16[528,128]{1,0:T(8,128)(2,1)S(1)}, u32[]{:S(2)}, u32[]{:S(2)}) %collective-permute-start.13) | collective-permute-done | bytes 135200 | tf_op jit(solution)/shard_map/ppermute | solution.py:389
  52.9 1.0 %collective-permute-done.14.refs_1_ = s16[528,128]{1,0:T(8,128)(2,1)S(1)} collective-permute-done((s16[528,128]{1,0:T(8,128)(2,1)S(1)}, s16[528,128]{1,0:T(8,128)(2,1)S(1)}, u32[]{:S(2)}, u32[]{:S(2)}) %collective-permute-start.14) | collective-permute-done | bytes 135200 | tf_op jit(solution)/shard_map/ppermute | solution.py:389
  53.9 2.0 %collective-permute-done.15.refs_2_ = s16[528,128]{1,0:T(8,128)(2,1)S(1)} collective-permute-done((s16[528,128]{1,0:T(8,128)(2,1)S(1)}, s16[528,128]{1,0:T(8,128)(2,1)S(1)}, u32[]{:S(2)}, u32[]{:S(2)}) %collective-permute-start.15) | collective-permute-done | bytes 135200 | tf_op jit(solution)/shard_map/ppermute | solution.py:389
  55.9 1.0 %collect.1 = (f32[512,256]{1,0:T(8,128)}, f32[512,256]{1,0:T(8,128)S(1)}, f32[288,128]{1,0:T(8,128)S(1)}) custom-call(f32[512,128]{1,0:T(8,128)S(1)} %add_chunks.1.done, f32[512,128]{1,0:T(8,128)S(1)} %get-tuple-element.34.kept, s16[528,128]{1,0:T(8,128)(2,1)S(1)} %collective-permute-done.13.refs_0_, s16[528,128]{1,0:T(8,128)(2,1)S(1)} %collective-permute-done.14.refs_1_, ...), custom_call_target="tpu_custom_call" | custom-call | tf_op jit(solution)/shard_map/collect/pallas_call | solution.py:274
  56.9 1.3 %collective-permute-done.16 = f32[144,128]{1,0:T(8,128)S(1)} collective-permute-done((f32[144,128]{1,0:T(8,128)S(1)}, f32[144,128]{1,0:T(8,128)S(1)}, u32[]{:S(2)}, u32[]{:S(2)}) %collective-permute-start.16) | collective-permute-done | bytes 73760 | tf_op jit(solution)/shard_map/ppermute | solution.py:389
  58.2 0.8 collective-permute-start.17
  59.0 3.7 %collective-permute-done.17 = f32[144,128]{1,0:T(8,128)S(1)} collective-permute-done((f32[144,128]{1,0:T(8,128)S(1)}, f32[144,128]{1,0:T(8,128)S(1)}, u32[]{:S(2)}, u32[]{:S(2)}) %collective-permute-start.17) | collective-permute-done | bytes 73760 | tf_op jit(solution)/shard_map/ppermute | solution.py:389
  62.6 2.2 %collective-permute-start.18 = (f32[144,128]{1,0:T(8,128)S(1)}, f32[144,128]{1,0:T(8,128)S(1)}, u32[]{:S(2)}, u32[]{:S(2)}) collective-permute-start(f32[144,128]{1,0:T(8,128)S(1)} %add.42), channel_id=1, source_target_pairs={{0,4},{4,0},{8,12},{12,8},{1,5},{5,1},{9,13},{13,9},{2,6},{6,2},{1... | collective-permute-start | bytes 221192 | tf_op jit(solution)/shard_map/ppermute | solution.py:389
  64.8 1.8 %collective-permute-start.19 = (f32[144,128]{1,0:T(8,128)S(1)}, f32[144,128]{1,0:T(8,128)S(1)}, u32[]{:S(2)}, u32[]{:S(2)}) collective-permute-start(f32[144,128]{1,0:T(8,128)S(1)} %add.42), channel_id=1, source_target_pairs={{0,8},{4,12},{8,0},{12,4},{1,9},{5,13},{9,1},{13,5},{2,10},{6,14},... | collective-permute-start | bytes 221192 | tf_op jit(solution)/shard_map/ppermute | solution.py:389
  66.6 0.6 collective-permute-start.20
  67.2 0.1 collective-permute-done.18
  67.4 4.2 %collective-permute-done.19 = f32[144,128]{1,0:T(8,128)S(1)} collective-permute-done((f32[144,128]{1,0:T(8,128)S(1)}, f32[144,128]{1,0:T(8,128)S(1)}, u32[]{:S(2)}, u32[]{:S(2)}) %collective-permute-start.19) | collective-permute-done | bytes 73760 | tf_op jit(solution)/shard_map/ppermute | solution.py:389
  71.6 1.3 %collective-permute-done.20 = f32[144,128]{1,0:T(8,128)S(1)} collective-permute-done((f32[144,128]{1,0:T(8,128)S(1)}, f32[144,128]{1,0:T(8,128)S(1)}, u32[]{:S(2)}, u32[]{:S(2)}) %collective-permute-start.20) | collective-permute-done | bytes 73760 | tf_op jit(solution)/shard_map/ppermute | solution.py:389
  72.9 0.1 collective-permute-start.21
  73.0 1.2 %collective-permute-done.21 = f32[144,128]{1,0:T(8,128)S(1)} collective-permute-done((f32[144,128]{1,0:T(8,128)S(1)}, f32[144,128]{1,0:T(8,128)S(1)}, u32[]{:S(2)}, u32[]{:S(2)}) %collective-permute-start.21) | collective-permute-done | bytes 73760 | tf_op jit(solution)/shard_map/ppermute | solution.py:389
  74.3 9.0 %orthonormalize.1 = (f32[256,256]{1,0:T(8,128)}, f32[512,256]{1,0:T(8,128)}) custom-call(f32[288,128]{1,0:T(8,128)S(1)} %pad_maximum_fusion.gram, f32[512,256]{1,0:T(8,128)S(1)} %get-tuple-element.40.y), custom_call_target="tpu_custom_call" | custom-call | tf_op jit(solution)/shard_map/orthonormalize/pallas_call | solution.py:375
  (21 shorter events, 0.1 us)
Async XLA Ops:
  0.6 1.6 %copy-start = (s32[256,2048]{1,0:T(8,128)S(1)}, s32[256,2048]{1,0:T(8,128)}, u32[]{:S(2)}) copy-start(s32[256,2048]{1,0:T(8,128)} %words.7) | copy-start | bytes 6291460
  2.2 1.2 %copy-start.2 = (bf16[2048,256]{1,0:T(8,128)(2,1)S(1)}, bf16[2048,256]{1,0:T(8,128)(2,1)}, u32[]{:S(2)}) copy-start(bf16[2048,256]{1,0:T(8,128)(2,1)} %basis.3) | copy-start | bytes 3145732
  4.9 6.7 %collective-permute-start = (f32[6,128,256]{2,1,0:T(8,128)S(1)}, f32[6,128,256]{2,1,0:T(8,128)S(1)}, u32[]{:S(2)}, u32[]{:S(2)}) collective-permute-start(f32[6,128,256]{2,1,0:T(8,128)S(1)} %get-tuple-element.23), channel_id=1, source_target_pairs={{0,1},{1,0},{2,3},{3,2},{4,5},{5,4},{6,7},{7,6},{8,9},{9,8},{10,11... | collective-permute-start | bytes 2359304 | tf_op jit(solution)/shard_map/ppermute | solution.py:389
  5.5 4.0 %collective-permute-start.1 = (f32[8,256]{1,0:T(8,128)S(1)}, f32[8,256]{1,0:T(8,128)S(1)}, u32[]{:S(2)}, u32[]{:S(2)}) collective-permute-start(f32[8,256]{1,0:T(8,128)S(1)} %get-tuple-element.24.sums), channel_id=1, source_target_pairs={{0,1},{1,0},{2,3},{3,2},{4,5},{5,4},{6,7},{7,6},{8,9},{9,8},{10,11... | collective-permute-start | bytes 24584 | tf_op jit(solution)/shard_map/ppermute | solution.py:389
  5.5 4.5 %collective-permute-start.2 = (f32[8,256]{1,0:T(8,128)S(1)}, f32[8,256]{1,0:T(8,128)S(1)}, u32[]{:S(2)}, u32[]{:S(2)}) collective-permute-start(f32[8,256]{1,0:T(8,128)S(1)} %get-tuple-element.24.sums), channel_id=1, source_target_pairs={{0,2},{1,3},{2,0},{3,1},{4,6},{5,7},{6,4},{7,5},{8,10},{9,11},{10,... | collective-permute-start | bytes 24584 | tf_op jit(solution)/shard_map/ppermute | solution.py:389
  8.4 3.1 %collective-permute-start.3 = (f32[8,256]{1,0:T(8,128)S(1)}, f32[8,256]{1,0:T(8,128)S(1)}, u32[]{:S(2)}, u32[]{:S(2)}) collective-permute-start(f32[8,256]{1,0:T(8,128)S(1)} %get-tuple-element.24.sums), channel_id=1, source_target_pairs={{0,3},{1,2},{2,1},{3,0},{4,7},{5,6},{6,5},{7,4},{8,11},{9,10},{10,... | collective-permute-start | bytes 24584 | tf_op jit(solution)/shard_map/ppermute | solution.py:389
  9.4 15.0 %copy-start.1 = (s32[256,2048]{1,0:T(8,128)S(1)}, s32[256,2048]{1,0:T(8,128)}, u32[]{:S(2)}) copy-start(s32[256,2048]{1,0:T(8,128)} %words.7) | copy-start | bytes 6291460
  11.7 11.2 %collective-permute-start.4 = (f32[6,128,128]{2,1,0:T(8,128)S(1)}, f32[6,128,128]{2,1,0:T(8,128)S(1)}, u32[]{:S(2)}, u32[]{:S(2)}) collective-permute-start(f32[6,128,128]{2,1,0:T(8,128)S(1)} %get-tuple-element.25.mine), channel_id=1, source_target_pairs={{0,2},{1,3},{2,0},{3,1},{4,6},{5,7},{6,4},{7,5},{8,10},{9,11},{10,... | collective-permute-start | bytes 1179656 | tf_op jit(solution)/shard_map/ppermute | solution.py:389
  12.3 3.7 %collective-permute-start.5 = (f32[8,256]{1,0:T(8,128)S(1)}, f32[8,256]{1,0:T(8,128)S(1)}, u32[]{:S(2)}, u32[]{:S(2)}) collective-permute-start(f32[8,256]{1,0:T(8,128)S(1)} %get-tuple-element.26), channel_id=1, source_target_pairs={{0,4},{4,0},{8,12},{12,8},{1,5},{5,1},{9,13},{13,9},{2,6},{6,2},{1... | collective-permute-start | bytes 24584 | tf_op jit(solution)/shard_map/ppermute | solution.py:389
  15.9 4.5 %collective-permute-start.6 = (f32[8,256]{1,0:T(8,128)S(1)}, f32[8,256]{1,0:T(8,128)S(1)}, u32[]{:S(2)}, u32[]{:S(2)}) collective-permute-start(f32[8,256]{1,0:T(8,128)S(1)} %add.37), channel_id=1, source_target_pairs={{0,8},{4,12},{8,0},{12,4},{1,9},{5,13},{9,1},{13,5},{2,10},{6,14},... | collective-permute-start | bytes 24584 | tf_op jit(solution)/shard_map/ppermute | solution.py:389
  23.0 1.5 %collective-permute-start.7 = (bf16[6,128,128]{2,1,0:T(8,128)(2,1)S(1)}, bf16[6,128,128]{2,1,0:T(8,128)(2,1)S(1)}, u32[]{:S(2)}, u32[]{:S(2)}) collective-permute-start(bf16[6,128,128]{2,1,0:T(8,128)(2,1)S(1)} %finish.2.mine), channel_id=1, source_target_pairs={{0,1},{1,0},{2,3},{3,2},{4,5},{5,4},{6,7},{7,6},{8,9},{9,8},{10,11... | collective-permute-start | bytes 589832 | tf_op jit(solution)/shard_map/ppermute | solution.py:389
  23.0 13.1 %collective-permute-start.11 = (f32[6,128,128]{2,1,0:T(8,128)S(1)}, f32[6,128,128]{2,1,0:T(8,128)S(1)}, u32[]{:S(2)}, u32[]{:S(2)}) collective-permute-start(f32[6,128,128]{2,1,0:T(8,128)S(1)} %get-tuple-element.32.mine), channel_id=1, source_target_pairs={{0,2},{1,3},{2,0},{3,1},{4,6},{5,7},{6,4},{7,5},{8,10},{9,11},{10,... | collective-permute-start | bytes 1179656 | tf_op jit(solution)/shard_map/ppermute | solution.py:389
  26.7 9.5 %collective-permute-start.8 = (s16[528,128]{1,0:T(8,128)(2,1)S(1)}, s16[528,128]{1,0:T(8,128)(2,1)S(1)}, u32[]{:S(2)}, u32[]{:S(2)}) collective-permute-start(s16[528,128]{1,0:T(8,128)(2,1)S(1)} %get-tuple-element.28), channel_id=1, source_target_pairs={{0,8},{4,12},{8,0},{12,4},{1,9},{5,13},{9,1},{13,5},{2,10},{6,14},... | collective-permute-start | bytes 405512 | tf_op jit(solution)/shard_map/ppermute | solution.py:389
  36.2 3.6 %collective-permute-start.12 = (bf16[6,128,128]{2,1,0:T(8,128)(2,1)S(1)}, bf16[6,128,128]{2,1,0:T(8,128)(2,1)S(1)}, u32[]{:S(2)}, u32[]{:S(2)}) collective-permute-start(bf16[6,128,128]{2,1,0:T(8,128)(2,1)S(1)} %finish.3.mine), channel_id=1, source_target_pairs={{0,1},{1,0},{2,3},{3,2},{4,5},{5,4},{6,7},{7,6},{8,9},{9,8},{10,11... | collective-permute-start | bytes 589832 | tf_op jit(solution)/shard_map/ppermute | solution.py:389
  36.3 10.2 %collective-permute-start.10 = (s16[528,128]{1,0:T(8,128)(2,1)S(1)}, s16[528,128]{1,0:T(8,128)(2,1)S(1)}, u32[]{:S(2)}, u32[]{:S(2)}) collective-permute-start(s16[528,128]{1,0:T(8,128)(2,1)S(1)} %get-tuple-element.30), channel_id=1, source_target_pairs={{0,12},{4,8},{8,4},{12,0},{1,13},{5,9},{9,5},{13,1},{2,14},{6,10},... | collective-permute-start | bytes 405512 | tf_op jit(solution)/shard_map/ppermute | solution.py:389
  39.9 8.6 %collective-permute-start.9 = (s16[528,128]{1,0:T(8,128)(2,1)S(1)}, s16[528,128]{1,0:T(8,128)(2,1)S(1)}, u32[]{:S(2)}, u32[]{:S(2)}) collective-permute-start(s16[528,128]{1,0:T(8,128)(2,1)S(1)} %get-tuple-element.29), channel_id=1, source_target_pairs={{0,4},{4,0},{8,12},{12,8},{1,5},{5,1},{9,13},{13,9},{2,6},{6,2},{1... | collective-permute-start | bytes 405512 | tf_op jit(solution)/shard_map/ppermute | solution.py:389
  42.1 10.8 %collective-permute-start.13 = (s16[528,128]{1,0:T(8,128)(2,1)S(1)}, s16[528,128]{1,0:T(8,128)(2,1)S(1)}, u32[]{:S(2)}, u32[]{:S(2)}) collective-permute-start(s16[528,128]{1,0:T(8,128)(2,1)S(1)} %get-tuple-element.35), channel_id=1, source_target_pairs={{0,8},{4,12},{8,0},{12,4},{1,9},{5,13},{9,1},{13,5},{2,10},{6,14},... | collective-permute-start | bytes 405512 | tf_op jit(solution)/shard_map/ppermute | solution.py:389
  43.0 10.9 %collective-permute-start.14 = (s16[528,128]{1,0:T(8,128)(2,1)S(1)}, s16[528,128]{1,0:T(8,128)(2,1)S(1)}, u32[]{:S(2)}, u32[]{:S(2)}) collective-permute-start(s16[528,128]{1,0:T(8,128)(2,1)S(1)} %get-tuple-element.36), channel_id=1, source_target_pairs={{0,4},{4,0},{8,12},{12,8},{1,5},{5,1},{9,13},{13,9},{2,6},{6,2},{1... | collective-permute-start | bytes 405512 | tf_op jit(solution)/shard_map/ppermute | solution.py:389
  44.2 11.6 %collective-permute-start.15 = (s16[528,128]{1,0:T(8,128)(2,1)S(1)}, s16[528,128]{1,0:T(8,128)(2,1)S(1)}, u32[]{:S(2)}, u32[]{:S(2)}) collective-permute-start(s16[528,128]{1,0:T(8,128)(2,1)S(1)} %get-tuple-element.37), channel_id=1, source_target_pairs={{0,12},{4,8},{8,4},{12,0},{1,13},{5,9},{9,5},{13,1},{2,14},{6,10},... | collective-permute-start | bytes 405512 | tf_op jit(solution)/shard_map/ppermute | solution.py:389
  56.9 1.3 %collective-permute-start.16 = (f32[144,128]{1,0:T(8,128)S(1)}, f32[144,128]{1,0:T(8,128)S(1)}, u32[]{:S(2)}, u32[]{:S(2)}) collective-permute-start(f32[144,128]{1,0:T(8,128)S(1)} %dynamic-slice_bitcast_fusion), channel_id=1, source_target_pairs={{0,1},{1,0},{2,3},{3,2},{4,5},{5,4},{6,7},{7,6},{8,9},{9,8},{10,11... | collective-permute-start | bytes 221192 | tf_op jit(solution)/shard_map/ppermute | solution.py:389
  58.2 4.4 %collective-permute-start.17 = (f32[144,128]{1,0:T(8,128)S(1)}, f32[144,128]{1,0:T(8,128)S(1)}, u32[]{:S(2)}, u32[]{:S(2)}) collective-permute-start(f32[144,128]{1,0:T(8,128)S(1)} %bitcast_add_fusion), channel_id=1, source_target_pairs={{0,2},{1,3},{2,0},{3,1},{4,6},{5,7},{6,4},{7,5},{8,10},{9,11},{10,... | collective-permute-start | bytes 221192 | tf_op jit(solution)/shard_map/ppermute | solution.py:389
  62.6 4.7 %collective-permute-start.18 = (f32[144,128]{1,0:T(8,128)S(1)}, f32[144,128]{1,0:T(8,128)S(1)}, u32[]{:S(2)}, u32[]{:S(2)}) collective-permute-start(f32[144,128]{1,0:T(8,128)S(1)} %add.42), channel_id=1, source_target_pairs={{0,4},{4,0},{8,12},{12,8},{1,5},{5,1},{9,13},{13,9},{2,6},{6,2},{1... | collective-permute-start | bytes 221192 | tf_op jit(solution)/shard_map/ppermute | solution.py:389
  64.8 6.8 %collective-permute-start.19 = (f32[144,128]{1,0:T(8,128)S(1)}, f32[144,128]{1,0:T(8,128)S(1)}, u32[]{:S(2)}, u32[]{:S(2)}) collective-permute-start(f32[144,128]{1,0:T(8,128)S(1)} %add.42), channel_id=1, source_target_pairs={{0,8},{4,12},{8,0},{12,4},{1,9},{5,13},{9,1},{13,5},{2,10},{6,14},... | collective-permute-start | bytes 221192 | tf_op jit(solution)/shard_map/ppermute | solution.py:389
  66.6 6.3 %collective-permute-start.20 = (f32[144,128]{1,0:T(8,128)S(1)}, f32[144,128]{1,0:T(8,128)S(1)}, u32[]{:S(2)}, u32[]{:S(2)}) collective-permute-start(f32[144,128]{1,0:T(8,128)S(1)} %add.42), channel_id=1, source_target_pairs={{0,12},{4,8},{8,4},{12,0},{1,13},{5,9},{9,5},{13,1},{2,14},{6,10},... | collective-permute-start | bytes 221192 | tf_op jit(solution)/shard_map/ppermute | solution.py:389
  72.9 1.3 %collective-permute-start.21 = (f32[144,128]{1,0:T(8,128)S(1)}, f32[144,128]{1,0:T(8,128)S(1)}, u32[]{:S(2)}, u32[]{:S(2)}) collective-permute-start(f32[144,128]{1,0:T(8,128)S(1)} %add_add_fusion), channel_id=1, source_target_pairs={{0,1},{1,0},{2,3},{3,2},{4,5},{5,4},{6,7},{7,6},{8,9},{9,8},{10,11... | collective-permute-start | bytes 221192 | tf_op jit(solution)/shard_map/ppermute | solution.py:389

commit v5 on v4

--- a/solution.py
+++ b/solution.py
@@ -289,14 +289,12 @@
     lane = lax.broadcasted_iota(jnp.int32, (SUB, LANES), 1)
     sub = lax.broadcasted_iota(jnp.int32, (SUB, LANES), 0)
     spread = lambda x, k: jnp.broadcast_to(x[k : k + 1], (SUB, LANES))
+    groups = BLOCK // SUB
+    ahead = table[:BLOCK, :]
     for base in range(0, width, BLOCK):
         t, off = base // LANES, base % LANES
-        groups = BLOCK // SUB
         rows = [
-            [
-                table[base + SUB * q : base + SUB * (q + 1), LANES * i : LANES * (i + 1)]
-                for i in range(tiles)
-            ]
+            [ahead[SUB * q : SUB * (q + 1), LANES * i : LANES * (i + 1)] for i in range(tiles)]
             for q in range(groups)
         ]
         for p in range(groups):
@@ -316,22 +314,31 @@
             for q in range(p, groups):
                 rows[q][t] = jnp.where(inside, unit if q == p else 0.0, rows[q][t])
             pivots = jnp.ones((SUB, LANES), jnp.float32)
-            for k in range(SUB):
-                pivot = spread(cols[k][p], k)
-                inverse = 1.0 / pivot
-                pivots = jnp.where(sub == k, pivot, pivots)
-                step = [None] * groups
+            for k in range(0, SUB, 2):
+                one, two = cols[k], cols[k + 1]
+                corner, side, far = spread(one[p], k), spread(two[p], k), spread(two[p], k + 1)
+                lead = 1.0 / corner
+                whole_ = corner * far - side * side
+                both = 1.0 / whole_
+                slope = side * lead
+                second = jnp.where(sub == k + 1, whole_ * lead, pivots)
+                pivots = jnp.where(sub == k, corner, second)
+                step, more = [None] * groups, [None] * groups
                 for q in range(p, groups):
-                    step[q] = (jnp.where(sub > k, cols[k][q], 0.0) if q == p else cols[k][q]) * inverse
-                for m in range(k + 1, SUB):
-                    line = spread(cols[m][p], k)
+                    step[q] = (far * one[q] - side * two[q]) * both
+                    more[q] = (corner * two[q] - side * one[q]) * both
+                step[p] = jnp.where(sub > k + 1, step[p], jnp.where(sub == k + 1, slope, 0.0))
+                more[p] = jnp.where(sub > k + 1, more[p], 0.0)
+                for m in range(k + 2, SUB):
+                    line, next_ = spread(cols[m][p], k), spread(cols[m][p], k + 1)
                     for q in range(p, groups):
-                        cols[m][q] = cols[m][q] - step[q] * line
+                        cols[m][q] = cols[m][q] - step[q] * line - more[q] * next_
                 for i in range(tiles):
-                    line = spread(rows[p][i], k)
+                    line, next_ = spread(rows[p][i], k), spread(rows[p][i], k + 1)
                     for q in range(p, groups):
-                        rows[q][i] = rows[q][i] - step[q] * line
-                upper = upper - step[p] * spread(upper, k)
+                        rows[q][i] = rows[q][i] - step[q] * line - more[q] * next_
+                line, next_ = spread(upper, k), spread(upper, k + 1)
+                upper = upper - step[p] * line - more[p] * next_
             scale = lax.rsqrt(pivots)
             for i in range(tiles):
                 rows[p][i] = rows[p][i] * scale
@@ -349,14 +356,19 @@
         table[base : base + BLOCK, :] = jnp.where(column < base + BLOCK, whole, 0.0)
         end = base + BLOCK
         if end < width:
-            begin = end // LANES * LANES
             h, m, l = pieces(whole)
-            left = jnp.concatenate([h, h, h, m, m, l], axis=0)[:, begin:]
+            left = jnp.concatenate([h, h, h, m, m, l], axis=0).T
             right = jnp.concatenate([h, m, l, h, m, h], axis=0)
-            change = lax.dot_general(left, right, (((0,), (0,)), ((), ())), preferred_element_type=jnp.float32)
-            column = lax.broadcasted_iota(jnp.int32, (width - end, width), 1)
-            keep = jnp.where((column >= base) & (column < end), 0.0, table[end:, :])
-            table[end:, :] = keep - change[end - begin :]
+
+            def update(begin, stop):
+                change = jnp.dot(left[begin:stop], right, preferred_element_type=jnp.float32)
+                column = lax.broadcasted_iota(jnp.int32, (stop - begin, width), 1)
+                inside = (column >= base) & (column < end)
+                return jnp.where(inside, 0.0, table[begin:stop, :]) - change
+
+            ahead = update(end, end + BLOCK)
+            if end + BLOCK < width:
+                table[end + BLOCK :, :] = update(end + BLOCK, width)
 
 def basis_kernel(gram, y, r_out, q_out, table):
     unpack_gram(gram, table)
@@ -440,15 +452,17 @@
         got = swap(part, "snp", 1 << (bits - 1))
         ready = got
         if sent is not None:
-            ready, _ = lax.optimization_barrier((got, sent[0]))
+            ready, _ = lax.optimization_barrier((got, sent))
         rows = finish(part, ready, sums, samples, group)
         scores = (rows, swap(rows, "snp", 1))
         if direct:
             masks = (2, 1, 3)
-            *coded, own = chunks_of_y(genotypes, scores, chunk, inv_root, masks + (0,))
+            coded = list(chunks_of_y(genotypes, scores, chunk, inv_root, masks[:1]))
+            *others, own = chunks_of_y(genotypes, scores, chunk, inv_root, masks[1:] + (0,))
+            coded += others
             kept.append(own)
             received.append([swap(c, "samp", mask) for c, mask in zip(coded, masks)])
-            sent = received[-1]
+            sent = (received[-1][0], own)
         else:
             tile = 4 * LANES if snps % (4 * LANES) == 0 else snps
             tiles = [

time: 83.4 us -> 82 us (0.983)
  waiting for transfers between devices: 37.2 us -> 34.9 us
    ppermute x22, waiting for transfers between devices: 37.2 us -> 34.9 us  [swap(): return lax.ppermute(array, axis, [(i, i ^ mask) for i in range(size)])]
    pallas_call x2 -> x4, Pallas kernels: 4.39 us -> 4.92 us  [chunks_of_y(): pl.pallas_call(kernel, out_shape=shapes, compiler_params=params(), name='...]
where the time goes in v5:
time: 82 us; the launch traced here: 81.9 us
  waiting for transfers between devices  34.9 us (43%)
  starting transfers between devices  26 us (32%)
  Pallas kernels  17.2 us (21%)
  local copies, waits for them, and re-layouts  2.82 us (3%)
    ppermute x22, waiting for transfers between devices, swap(): return lax.ppermute(array, axis, [(i, i ^ mask) for i in range(size)])  34.9 us
    ppermute x22, starting transfers between devices, swap(): return lax.ppermute(array, axis, [(i, i ^ mask) for i in range(size)])  26 us
    pallas_call x1, Pallas kernels, orthonormalize(): pl.pallas_call(basis_kernel, out_shape=[jax.ShapeDtypeStruct((width, widt...  8.52 us
    pallas_call x4, Pallas kernels, chunks_of_y(): pl.pallas_call(kernel, out_shape=shapes, compiler_params=params(), name='...  4.92 us
    unnamed x6, local copies, waits for them, and re-layouts  2.82 us
    pallas_call x2, Pallas kernels, project(): pl.pallas_call(other_kernel if other else mine_kernel, out_shape=shapes,...  2.46 us
  transfers between devices with their start and end apart: 22, of which 17 were waited for; matrix products, arithmetic and copies ran while one was open for 0% of the time, Pallas kernels for 7%

profile of v5, /device:TPU:0, one launch (start us, length us, event | category | flops | bytes accessed | tf_op | source)
XLA Modules:
  0.0 81.9 jit_solution(7515730938341104607)
XLA Ops:
  0.6 1.6 %copy-done = s32[256,2048]{1,0:T(8,128)S(1)} copy-done((s32[256,2048]{1,0:T(8,128)S(1)}, s32[256,2048]{1,0:T(8,128)}, u32[]{:S(2)}) %copy-start) | copy-done | bytes 2097176
  2.2 1.2 %copy-done.2 = bf16[2048,256]{1,0:T(8,128)(2,1)S(1)} copy-done((bf16[2048,256]{1,0:T(8,128)(2,1)S(1)}, bf16[2048,256]{1,0:T(8,128)(2,1)}, u32[]{:S(2)}) %copy-start.2) | copy-done | bytes 1048600
  3.4 1.5 %project_other.1 = (f32[6,128,256]{2,1,0:T(8,128)S(1)}, f32[8,256]{1,0:T(8,128)S(1)}) custom-call(s32[256,2048]{1,0:T(8,128)S(1)} %copy-done, bf16[2048,256]{1,0:T(8,128)(2,1)S(1)} %copy-done.2), custom_call_target="tpu_custom_call" | custom-call | flops 805306368 | bytes 2883584 | tf_op jit(solution)/shard_map/project_other/pallas_call | solution.py:79
  4.9 0.5 collective-permute-start
  5.5 0.1 collective-permute-start.1
  5.5 2.9 %collective-permute-start.2 = (f32[8,256]{1,0:T(8,128)S(1)}, f32[8,256]{1,0:T(8,128)S(1)}, u32[]{:S(2)}, u32[]{:S(2)}) collective-permute-start(f32[8,256]{1,0:T(8,128)S(1)} %get-tuple-element.22.sums), channel_id=1, source_target_pairs={{0,2},{1,3},{2,0},{3,1},{4,6},{5,7},{6,4},{7,5},{8,10},{9,11},{10,... | collective-permute-start | bytes 24584 | tf_op jit(solution)/shard_map/ppermute | solution.py:401
  8.5 1.0 %project_mine.1.mine = f32[6,128,256]{2,1,0:T(8,128)S(1)} custom-call(s32[256,2048]{1,0:T(8,128)S(1)} %copy-done, bf16[2048,256]{1,0:T(8,128)(2,1)S(1)} %copy-done.2), custom_call_target="tpu_custom_call" | custom-call | flops 805306368 | bytes 2883584 | tf_op jit(solution)/shard_map/project_mine/pallas_call | solution.py:79
  9.5 0.6 collective-permute-done.2
  10.1 1.5 %collective-permute-done.3 = f32[8,256]{1,0:T(8,128)S(1)} collective-permute-done((f32[8,256]{1,0:T(8,128)S(1)}, f32[8,256]{1,0:T(8,128)S(1)}, u32[]{:S(2)}, u32[]{:S(2)}) %collective-permute-start.3) | collective-permute-done | bytes 8224 | tf_op jit(solution)/shard_map/ppermute | solution.py:401
  11.6 0.1 merge.1
  11.7 0.6 collective-permute-start.4
  12.3 1.6 %collective-permute-start.5 = (f32[8,256]{1,0:T(8,128)S(1)}, f32[8,256]{1,0:T(8,128)S(1)}, u32[]{:S(2)}, u32[]{:S(2)}) collective-permute-start(f32[8,256]{1,0:T(8,128)S(1)} %get-tuple-element.24), channel_id=1, source_target_pairs={{0,4},{4,0},{8,12},{12,8},{1,5},{5,1},{9,13},{13,9},{2,6},{6,2},{1... | collective-permute-start | bytes 24584 | tf_op jit(solution)/shard_map/ppermute | solution.py:401
  13.9 2.0 %collective-permute-done.5 = f32[8,256]{1,0:T(8,128)S(1)} collective-permute-done((f32[8,256]{1,0:T(8,128)S(1)}, f32[8,256]{1,0:T(8,128)S(1)}, u32[]{:S(2)}, u32[]{:S(2)}) %collective-permute-start.5) | collective-permute-done | bytes 8224 | tf_op jit(solution)/shard_map/ppermute | solution.py:401
  15.9 2.6 %collective-permute-start.6 = (f32[8,256]{1,0:T(8,128)S(1)}, f32[8,256]{1,0:T(8,128)S(1)}, u32[]{:S(2)}, u32[]{:S(2)}) collective-permute-start(f32[8,256]{1,0:T(8,128)S(1)} %add.37), channel_id=1, source_target_pairs={{0,8},{4,12},{8,0},{12,4},{1,9},{5,13},{9,1},{13,5},{2,10},{6,14},... | collective-permute-start | bytes 24584 | tf_op jit(solution)/shard_map/ppermute | solution.py:401
  18.6 1.9 %collective-permute-done.6 = f32[8,256]{1,0:T(8,128)S(1)} collective-permute-done((f32[8,256]{1,0:T(8,128)S(1)}, f32[8,256]{1,0:T(8,128)S(1)}, u32[]{:S(2)}, u32[]{:S(2)}) %collective-permute-start.6) | collective-permute-done | bytes 8224 | tf_op jit(solution)/shard_map/ppermute | solution.py:401
  20.5 2.4 %collective-permute-done.4.got = f32[6,128,128]{2,1,0:T(8,128)S(1)} collective-permute-done((f32[6,128,128]{2,1,0:T(8,128)S(1)}, f32[6,128,128]{2,1,0:T(8,128)S(1)}, u32[]{:S(2)}, u32[]{:S(2)}) %collective-permute-start.4) | collective-permute-done | bytes 393248 | tf_op jit(solution)/shard_map/ppermute | solution.py:401
  22.9 0.5 collective-permute-start.11
  23.5 0.1 collective-permute-start.7
  23.5 1.4 %collective-permute-done.7.other = bf16[6,128,128]{2,1,0:T(8,128)(2,1)S(1)} collective-permute-done((bf16[6,128,128]{2,1,0:T(8,128)(2,1)S(1)}, bf16[6,128,128]{2,1,0:T(8,128)(2,1)S(1)}, u32[]{:S(2)}, u32[]{:S(2)}) %collective-permute-start.7) | collective-permute-done | bytes 196640 | tf_op jit(solution)/shard_map/ppermute | solution.py:401
  25.0 0.8 chunks.5
  25.8 2.7 %collective-permute-start.8 = (s16[528,128]{1,0:T(8,128)(2,1)S(1)}, s16[528,128]{1,0:T(8,128)(2,1)S(1)}, u32[]{:S(2)}, u32[]{:S(2)}) collective-permute-start(s16[528,128]{1,0:T(8,128)(2,1)S(1)} %chunks.5), channel_id=1, source_target_pairs={{0,8},{4,12},{8,0},{12,4},{1,9},{5,13},{9,1},{13,5},{2,10},{6,14},... | collective-permute-start | bytes 405512 | tf_op jit(solution)/shard_map/ppermute | solution.py:401
  28.5 1.7 %chunks.4 = (s16[528,128]{1,0:T(8,128)(2,1)S(1)}, s16[528,128]{1,0:T(8,128)(2,1)S(1)}, f32[512,128]{1,0:T(8,128)S(1)}) custom-call(s32[256,2048]{1,0:T(8,128)S(1)} %copy-done.1, bf16[6,128,128]{2,1,0:T(8,128)(2,1)S(1)} %finish.2.mine, bf16[6,128,128]{2,1,0:T(8,128)(2,1)S(1)} %collective-permute-done.7.other), custom_call_target="tpu_custom_call" | custom-call | flops 603979776 | bytes 2359296 | tf_op jit(solution)/shard_map/chunks/pallas_call | solution.py:185
  30.1 5.1 %collective-permute-done.8.refs_0_ = s16[528,128]{1,0:T(8,128)(2,1)S(1)} collective-permute-done((s16[528,128]{1,0:T(8,128)(2,1)S(1)}, s16[528,128]{1,0:T(8,128)(2,1)S(1)}, u32[]{:S(2)}, u32[]{:S(2)}) %collective-permute-start.8) | collective-permute-done | bytes 135200 | tf_op jit(solution)/shard_map/ppermute | solution.py:401
  35.3 0.1 collective-permute-start.12
  35.4 3.6 %collective-permute-start.10 = (s16[528,128]{1,0:T(8,128)(2,1)S(1)}, s16[528,128]{1,0:T(8,128)(2,1)S(1)}, u32[]{:S(2)}, u32[]{:S(2)}) collective-permute-start(s16[528,128]{1,0:T(8,128)(2,1)S(1)} %get-tuple-element.27), channel_id=1, source_target_pairs={{0,12},{4,8},{8,4},{12,0},{1,13},{5,9},{9,5},{13,1},{2,14},{6,10},... | collective-permute-start | bytes 405512 | tf_op jit(solution)/shard_map/ppermute | solution.py:401
  39.0 0.8 chunks.7
  39.8 0.9 %collective-permute-start.13 = (s16[528,128]{1,0:T(8,128)(2,1)S(1)}, s16[528,128]{1,0:T(8,128)(2,1)S(1)}, u32[]{:S(2)}, u32[]{:S(2)}) collective-permute-start(s16[528,128]{1,0:T(8,128)(2,1)S(1)} %chunks.7), channel_id=1, source_target_pairs={{0,8},{4,12},{8,0},{12,4},{1,9},{5,13},{9,1},{13,5},{2,10},{6,14},... | collective-permute-start | bytes 405512 | tf_op jit(solution)/shard_map/ppermute | solution.py:401
  40.7 1.7 %chunks.6 = (s16[528,128]{1,0:T(8,128)(2,1)S(1)}, s16[528,128]{1,0:T(8,128)(2,1)S(1)}, f32[512,128]{1,0:T(8,128)S(1)}) custom-call(s32[256,2048]{1,0:T(8,128)S(1)} %copy-done.1, bf16[6,128,128]{2,1,0:T(8,128)(2,1)S(1)} %finish.3.mine, bf16[6,128,128]{2,1,0:T(8,128)(2,1)S(1)} %collective-permute-done.12.other), custom_call_target="tpu_custom_call" | custom-call | flops 603979776 | bytes 2359296 | tf_op jit(solution)/shard_map/chunks/pallas_call | solution.py:185
  42.4 1.3 %collective-permute-start.14 = (s16[528,128]{1,0:T(8,128)(2,1)S(1)}, s16[528,128]{1,0:T(8,128)(2,1)S(1)}, u32[]{:S(2)}, u32[]{:S(2)}) collective-permute-start(s16[528,128]{1,0:T(8,128)(2,1)S(1)} %get-tuple-element.32), channel_id=1, source_target_pairs={{0,4},{4,0},{8,12},{12,8},{1,5},{5,1},{9,13},{13,9},{2,6},{6,2},{1... | collective-permute-start | bytes 405512 | tf_op jit(solution)/shard_map/ppermute | solution.py:401
  43.7 2.4 %collective-permute-start.15 = (s16[528,128]{1,0:T(8,128)(2,1)S(1)}, s16[528,128]{1,0:T(8,128)(2,1)S(1)}, u32[]{:S(2)}, u32[]{:S(2)}) collective-permute-start(s16[528,128]{1,0:T(8,128)(2,1)S(1)} %get-tuple-element.33), channel_id=1, source_target_pairs={{0,12},{4,8},{8,4},{12,0},{1,13},{5,9},{9,5},{13,1},{2,14},{6,10},... | collective-permute-start | bytes 405512 | tf_op jit(solution)/shard_map/ppermute | solution.py:401
  46.1 2.0 %collective-permute-done.9.refs_1_ = s16[528,128]{1,0:T(8,128)(2,1)S(1)} collective-permute-done((s16[528,128]{1,0:T(8,128)(2,1)S(1)}, s16[528,128]{1,0:T(8,128)(2,1)S(1)}, u32[]{:S(2)}, u32[]{:S(2)}) %collective-permute-start.9) | collective-permute-done | bytes 135200 | tf_op jit(solution)/shard_map/ppermute | solution.py:401
  48.1 0.1 add_chunks.1.done
  48.2 2.5 %collective-permute-done.13.refs_0_ = s16[528,128]{1,0:T(8,128)(2,1)S(1)} collective-permute-done((s16[528,128]{1,0:T(8,128)(2,1)S(1)}, s16[528,128]{1,0:T(8,128)(2,1)S(1)}, u32[]{:S(2)}, u32[]{:S(2)}) %collective-permute-start.13) | collective-permute-done | bytes 135200 | tf_op jit(solution)/shard_map/ppermute | solution.py:401
  50.7 1.8 %collective-permute-done.14.refs_1_ = s16[528,128]{1,0:T(8,128)(2,1)S(1)} collective-permute-done((s16[528,128]{1,0:T(8,128)(2,1)S(1)}, s16[528,128]{1,0:T(8,128)(2,1)S(1)}, u32[]{:S(2)}, u32[]{:S(2)}) %collective-permute-start.14) | collective-permute-done | bytes 135200 | tf_op jit(solution)/shard_map/ppermute | solution.py:401
  52.5 2.5 %collective-permute-done.15.refs_2_ = s16[528,128]{1,0:T(8,128)(2,1)S(1)} collective-permute-done((s16[528,128]{1,0:T(8,128)(2,1)S(1)}, s16[528,128]{1,0:T(8,128)(2,1)S(1)}, u32[]{:S(2)}, u32[]{:S(2)}) %collective-permute-start.15) | collective-permute-done | bytes 135200 | tf_op jit(solution)/shard_map/ppermute | solution.py:401
  55.0 1.0 %collect.1 = (f32[512,256]{1,0:T(8,128)}, f32[512,256]{1,0:T(8,128)S(1)}, f32[288,128]{1,0:T(8,128)S(1)}) custom-call(f32[512,128]{1,0:T(8,128)S(1)} %add_chunks.1.done, f32[512,128]{1,0:T(8,128)S(1)} %get-tuple-element.31.kept, s16[528,128]{1,0:T(8,128)(2,1)S(1)} %collective-permute-done.13.refs_0_, s16[528,128]{1,0:T(8,128)(2,1)S(1)} %collective-permute-done.14.refs_1_, ...), custom_call_target="tpu_custom_call" | custom-call | tf_op jit(solution)/shard_map/collect/pallas_call | solution.py:274
  56.0 1.3 %collective-permute-done.16 = f32[144,128]{1,0:T(8,128)S(1)} collective-permute-done((f32[144,128]{1,0:T(8,128)S(1)}, f32[144,128]{1,0:T(8,128)S(1)}, u32[]{:S(2)}, u32[]{:S(2)}) %collective-permute-start.16) | collective-permute-done | bytes 73760 | tf_op jit(solution)/shard_map/ppermute | solution.py:401
  57.3 1.6 %collective-permute-start.17 = (f32[144,128]{1,0:T(8,128)S(1)}, f32[144,128]{1,0:T(8,128)S(1)}, u32[]{:S(2)}, u32[]{:S(2)}) collective-permute-start(f32[144,128]{1,0:T(8,128)S(1)} %bitcast_add_fusion), channel_id=1, source_target_pairs={{0,2},{1,3},{2,0},{3,1},{4,6},{5,7},{6,4},{7,5},{8,10},{9,11},{10,... | collective-permute-start | bytes 221192 | tf_op jit(solution)/shard_map/ppermute | solution.py:401
  58.8 2.9 %collective-permute-done.17 = f32[144,128]{1,0:T(8,128)S(1)} collective-permute-done((f32[144,128]{1,0:T(8,128)S(1)}, f32[144,128]{1,0:T(8,128)S(1)}, u32[]{:S(2)}, u32[]{:S(2)}) %collective-permute-start.17) | collective-permute-done | bytes 73760 | tf_op jit(solution)/shard_map/ppermute | solution.py:401
  61.7 1.7 %collective-permute-start.18 = (f32[144,128]{1,0:T(8,128)S(1)}, f32[144,128]{1,0:T(8,128)S(1)}, u32[]{:S(2)}, u32[]{:S(2)}) collective-permute-start(f32[144,128]{1,0:T(8,128)S(1)} %add.42), channel_id=1, source_target_pairs={{0,4},{4,0},{8,12},{12,8},{1,5},{5,1},{9,13},{13,9},{2,6},{6,2},{1... | collective-permute-start | bytes 221192 | tf_op jit(solution)/shard_map/ppermute | solution.py:401
  63.4 2.4 %collective-permute-start.19 = (f32[144,128]{1,0:T(8,128)S(1)}, f32[144,128]{1,0:T(8,128)S(1)}, u32[]{:S(2)}, u32[]{:S(2)}) collective-permute-start(f32[144,128]{1,0:T(8,128)S(1)} %add.42), channel_id=1, source_target_pairs={{0,8},{4,12},{8,0},{12,4},{1,9},{5,13},{9,1},{13,5},{2,10},{6,14},... | collective-permute-start | bytes 221192 | tf_op jit(solution)/shard_map/ppermute | solution.py:401
  65.8 0.4 collective-permute-start.20
  66.2 0.3 collective-permute-done.18
  66.5 3.9 %collective-permute-done.19 = f32[144,128]{1,0:T(8,128)S(1)} collective-permute-done((f32[144,128]{1,0:T(8,128)S(1)}, f32[144,128]{1,0:T(8,128)S(1)}, u32[]{:S(2)}, u32[]{:S(2)}) %collective-permute-start.19) | collective-permute-done | bytes 73760 | tf_op jit(solution)/shard_map/ppermute | solution.py:401
  70.4 1.6 %collective-permute-done.20 = f32[144,128]{1,0:T(8,128)S(1)} collective-permute-done((f32[144,128]{1,0:T(8,128)S(1)}, f32[144,128]{1,0:T(8,128)S(1)}, u32[]{:S(2)}, u32[]{:S(2)}) %collective-permute-start.20) | collective-permute-done | bytes 73760 | tf_op jit(solution)/shard_map/ppermute | solution.py:401
  72.0 0.1 collective-permute-start.21
  72.1 1.2 %collective-permute-done.21 = f32[144,128]{1,0:T(8,128)S(1)} collective-permute-done((f32[144,128]{1,0:T(8,128)S(1)}, f32[144,128]{1,0:T(8,128)S(1)}, u32[]{:S(2)}, u32[]{:S(2)}) %collective-permute-start.21) | collective-permute-done | bytes 73760 | tf_op jit(solution)/shard_map/ppermute | solution.py:401
  73.3 8.5 %orthonormalize.1 = (f32[256,256]{1,0:T(8,128)}, f32[512,256]{1,0:T(8,128)}) custom-call(f32[288,128]{1,0:T(8,128)S(1)} %pad_maximum_fusion.gram, f32[512,256]{1,0:T(8,128)S(1)} %get-tuple-element.36.y), custom_call_target="tpu_custom_call" | custom-call | tf_op jit(solution)/shard_map/orthonormalize/pallas_call | solution.py:387
  (23 shorter events, 0.2 us)
Async XLA Ops:
  0.6 1.6 %copy-start = (s32[256,2048]{1,0:T(8,128)S(1)}, s32[256,2048]{1,0:T(8,128)}, u32[]{:S(2)}) copy-start(s32[256,2048]{1,0:T(8,128)} %words.11) | copy-start | bytes 6291460
  2.2 1.2 %copy-start.2 = (bf16[2048,256]{1,0:T(8,128)(2,1)S(1)}, bf16[2048,256]{1,0:T(8,128)(2,1)}, u32[]{:S(2)}) copy-start(bf16[2048,256]{1,0:T(8,128)(2,1)} %basis.3) | copy-start | bytes 3145732
  4.9 6.7 %collective-permute-start = (f32[6,128,256]{2,1,0:T(8,128)S(1)}, f32[6,128,256]{2,1,0:T(8,128)S(1)}, u32[]{:S(2)}, u32[]{:S(2)}) collective-permute-start(f32[6,128,256]{2,1,0:T(8,128)S(1)} %get-tuple-element.21), channel_id=1, source_target_pairs={{0,1},{1,0},{2,3},{3,2},{4,5},{5,4},{6,7},{7,6},{8,9},{9,8},{10,11... | collective-permute-start | bytes 2359304 | tf_op jit(solution)/shard_map/ppermute | solution.py:401
  5.5 4.0 %collective-permute-start.1 = (f32[8,256]{1,0:T(8,128)S(1)}, f32[8,256]{1,0:T(8,128)S(1)}, u32[]{:S(2)}, u32[]{:S(2)}) collective-permute-start(f32[8,256]{1,0:T(8,128)S(1)} %get-tuple-element.22.sums), channel_id=1, source_target_pairs={{0,1},{1,0},{2,3},{3,2},{4,5},{5,4},{6,7},{7,6},{8,9},{9,8},{10,11... | collective-permute-start | bytes 24584 | tf_op jit(solution)/shard_map/ppermute | solution.py:401
  5.5 4.5 %collective-permute-start.2 = (f32[8,256]{1,0:T(8,128)S(1)}, f32[8,256]{1,0:T(8,128)S(1)}, u32[]{:S(2)}, u32[]{:S(2)}) collective-permute-start(f32[8,256]{1,0:T(8,128)S(1)} %get-tuple-element.22.sums), channel_id=1, source_target_pairs={{0,2},{1,3},{2,0},{3,1},{4,6},{5,7},{6,4},{7,5},{8,10},{9,11},{10,... | collective-permute-start | bytes 24584 | tf_op jit(solution)/shard_map/ppermute | solution.py:401
  8.4 3.1 %collective-permute-start.3 = (f32[8,256]{1,0:T(8,128)S(1)}, f32[8,256]{1,0:T(8,128)S(1)}, u32[]{:S(2)}, u32[]{:S(2)}) collective-permute-start(f32[8,256]{1,0:T(8,128)S(1)} %get-tuple-element.22.sums), channel_id=1, source_target_pairs={{0,3},{1,2},{2,1},{3,0},{4,7},{5,6},{6,5},{7,4},{8,11},{9,10},{10,... | collective-permute-start | bytes 24584 | tf_op jit(solution)/shard_map/ppermute | solution.py:401
  9.4 15.5 %copy-start.1 = (s32[256,2048]{1,0:T(8,128)S(1)}, s32[256,2048]{1,0:T(8,128)}, u32[]{:S(2)}) copy-start(s32[256,2048]{1,0:T(8,128)} %words.11) | copy-start | bytes 6291460
  11.7 11.2 %collective-permute-start.4 = (f32[6,128,128]{2,1,0:T(8,128)S(1)}, f32[6,128,128]{2,1,0:T(8,128)S(1)}, u32[]{:S(2)}, u32[]{:S(2)}) collective-permute-start(f32[6,128,128]{2,1,0:T(8,128)S(1)} %get-tuple-element.23.mine), channel_id=1, source_target_pairs={{0,2},{1,3},{2,0},{3,1},{4,6},{5,7},{6,4},{7,5},{8,10},{9,11},{10,... | collective-permute-start | bytes 1179656 | tf_op jit(solution)/shard_map/ppermute | solution.py:401
  12.3 3.7 %collective-permute-start.5 = (f32[8,256]{1,0:T(8,128)S(1)}, f32[8,256]{1,0:T(8,128)S(1)}, u32[]{:S(2)}, u32[]{:S(2)}) collective-permute-start(f32[8,256]{1,0:T(8,128)S(1)} %get-tuple-element.24), channel_id=1, source_target_pairs={{0,4},{4,0},{8,12},{12,8},{1,5},{5,1},{9,13},{13,9},{2,6},{6,2},{1... | collective-permute-start | bytes 24584 | tf_op jit(solution)/shard_map/ppermute | solution.py:401
  15.9 4.5 %collective-permute-start.6 = (f32[8,256]{1,0:T(8,128)S(1)}, f32[8,256]{1,0:T(8,128)S(1)}, u32[]{:S(2)}, u32[]{:S(2)}) collective-permute-start(f32[8,256]{1,0:T(8,128)S(1)} %add.37), channel_id=1, source_target_pairs={{0,8},{4,12},{8,0},{12,4},{1,9},{5,13},{9,1},{13,5},{2,10},{6,14},... | collective-permute-start | bytes 24584 | tf_op jit(solution)/shard_map/ppermute | solution.py:401
  22.9 12.4 %collective-permute-start.11 = (f32[6,128,128]{2,1,0:T(8,128)S(1)}, f32[6,128,128]{2,1,0:T(8,128)S(1)}, u32[]{:S(2)}, u32[]{:S(2)}) collective-permute-start(f32[6,128,128]{2,1,0:T(8,128)S(1)} %get-tuple-element.29.mine), channel_id=1, source_target_pairs={{0,2},{1,3},{2,0},{3,1},{4,6},{5,7},{6,4},{7,5},{8,10},{9,11},{10,... | collective-permute-start | bytes 1179656 | tf_op jit(solution)/shard_map/ppermute | solution.py:401
  23.5 1.5 %collective-permute-start.7 = (bf16[6,128,128]{2,1,0:T(8,128)(2,1)S(1)}, bf16[6,128,128]{2,1,0:T(8,128)(2,1)S(1)}, u32[]{:S(2)}, u32[]{:S(2)}) collective-permute-start(bf16[6,128,128]{2,1,0:T(8,128)(2,1)S(1)} %finish.2.mine), channel_id=1, source_target_pairs={{0,1},{1,0},{2,3},{3,2},{4,5},{5,4},{6,7},{7,6},{8,9},{9,8},{10,11... | collective-permute-start | bytes 589832 | tf_op jit(solution)/shard_map/ppermute | solution.py:401
  25.8 9.5 %collective-permute-start.8 = (s16[528,128]{1,0:T(8,128)(2,1)S(1)}, s16[528,128]{1,0:T(8,128)(2,1)S(1)}, u32[]{:S(2)}, u32[]{:S(2)}) collective-permute-start(s16[528,128]{1,0:T(8,128)(2,1)S(1)} %chunks.5), channel_id=1, source_target_pairs={{0,8},{4,12},{8,0},{12,4},{1,9},{5,13},{9,1},{13,5},{2,10},{6,14},... | collective-permute-start | bytes 405512 | tf_op jit(solution)/shard_map/ppermute | solution.py:401
  35.3 3.7 %collective-permute-start.12 = (bf16[6,128,128]{2,1,0:T(8,128)(2,1)S(1)}, bf16[6,128,128]{2,1,0:T(8,128)(2,1)S(1)}, u32[]{:S(2)}, u32[]{:S(2)}) collective-permute-start(bf16[6,128,128]{2,1,0:T(8,128)(2,1)S(1)} %finish.3.mine), channel_id=1, source_target_pairs={{0,1},{1,0},{2,3},{3,2},{4,5},{5,4},{6,7},{7,6},{8,9},{9,8},{10,11... | collective-permute-start | bytes 589832 | tf_op jit(solution)/shard_map/ppermute | solution.py:401
  35.4 10.7 %collective-permute-start.10 = (s16[528,128]{1,0:T(8,128)(2,1)S(1)}, s16[528,128]{1,0:T(8,128)(2,1)S(1)}, u32[]{:S(2)}, u32[]{:S(2)}) collective-permute-start(s16[528,128]{1,0:T(8,128)(2,1)S(1)} %get-tuple-element.27), channel_id=1, source_target_pairs={{0,12},{4,8},{8,4},{12,0},{1,13},{5,9},{9,5},{13,1},{2,14},{6,10},... | collective-permute-start | bytes 405512 | tf_op jit(solution)/shard_map/ppermute | solution.py:401
  39.0 9.1 %collective-permute-start.9 = (s16[528,128]{1,0:T(8,128)(2,1)S(1)}, s16[528,128]{1,0:T(8,128)(2,1)S(1)}, u32[]{:S(2)}, u32[]{:S(2)}) collective-permute-start(s16[528,128]{1,0:T(8,128)(2,1)S(1)} %get-tuple-element.26), channel_id=1, source_target_pairs={{0,4},{4,0},{8,12},{12,8},{1,5},{5,1},{9,13},{13,9},{2,6},{6,2},{1... | collective-permute-start | bytes 405512 | tf_op jit(solution)/shard_map/ppermute | solution.py:401
  39.8 10.9 %collective-permute-start.13 = (s16[528,128]{1,0:T(8,128)(2,1)S(1)}, s16[528,128]{1,0:T(8,128)(2,1)S(1)}, u32[]{:S(2)}, u32[]{:S(2)}) collective-permute-start(s16[528,128]{1,0:T(8,128)(2,1)S(1)} %chunks.7), channel_id=1, source_target_pairs={{0,8},{4,12},{8,0},{12,4},{1,9},{5,13},{9,1},{13,5},{2,10},{6,14},... | collective-permute-start | bytes 405512 | tf_op jit(solution)/shard_map/ppermute | solution.py:401
  42.4 10.1 %collective-permute-start.14 = (s16[528,128]{1,0:T(8,128)(2,1)S(1)}, s16[528,128]{1,0:T(8,128)(2,1)S(1)}, u32[]{:S(2)}, u32[]{:S(2)}) collective-permute-start(s16[528,128]{1,0:T(8,128)(2,1)S(1)} %get-tuple-element.32), channel_id=1, source_target_pairs={{0,4},{4,0},{8,12},{12,8},{1,5},{5,1},{9,13},{13,9},{2,6},{6,2},{1... | collective-permute-start | bytes 405512 | tf_op jit(solution)/shard_map/ppermute | solution.py:401
  43.7 11.3 %collective-permute-start.15 = (s16[528,128]{1,0:T(8,128)(2,1)S(1)}, s16[528,128]{1,0:T(8,128)(2,1)S(1)}, u32[]{:S(2)}, u32[]{:S(2)}) collective-permute-start(s16[528,128]{1,0:T(8,128)(2,1)S(1)} %get-tuple-element.33), channel_id=1, source_target_pairs={{0,12},{4,8},{8,4},{12,0},{1,13},{5,9},{9,5},{13,1},{2,14},{6,10},... | collective-permute-start | bytes 405512 | tf_op jit(solution)/shard_map/ppermute | solution.py:401
  56.0 1.3 %collective-permute-start.16 = (f32[144,128]{1,0:T(8,128)S(1)}, f32[144,128]{1,0:T(8,128)S(1)}, u32[]{:S(2)}, u32[]{:S(2)}) collective-permute-start(f32[144,128]{1,0:T(8,128)S(1)} %dynamic-slice_bitcast_fusion), channel_id=1, source_target_pairs={{0,1},{1,0},{2,3},{3,2},{4,5},{5,4},{6,7},{7,6},{8,9},{9,8},{10,11... | collective-permute-start | bytes 221192 | tf_op jit(solution)/shard_map/ppermute | solution.py:401
  57.3 4.4 %collective-permute-start.17 = (f32[144,128]{1,0:T(8,128)S(1)}, f32[144,128]{1,0:T(8,128)S(1)}, u32[]{:S(2)}, u32[]{:S(2)}) collective-permute-start(f32[144,128]{1,0:T(8,128)S(1)} %bitcast_add_fusion), channel_id=1, source_target_pairs={{0,2},{1,3},{2,0},{3,1},{4,6},{5,7},{6,4},{7,5},{8,10},{9,11},{10,... | collective-permute-start | bytes 221192 | tf_op jit(solution)/shard_map/ppermute | solution.py:401
  61.7 4.7 %collective-permute-start.18 = (f32[144,128]{1,0:T(8,128)S(1)}, f32[144,128]{1,0:T(8,128)S(1)}, u32[]{:S(2)}, u32[]{:S(2)}) collective-permute-start(f32[144,128]{1,0:T(8,128)S(1)} %add.42), channel_id=1, source_target_pairs={{0,4},{4,0},{8,12},{12,8},{1,5},{5,1},{9,13},{13,9},{2,6},{6,2},{1... | collective-permute-start | bytes 221192 | tf_op jit(solution)/shard_map/ppermute | solution.py:401
  63.4 7.0 %collective-permute-start.19 = (f32[144,128]{1,0:T(8,128)S(1)}, f32[144,128]{1,0:T(8,128)S(1)}, u32[]{:S(2)}, u32[]{:S(2)}) collective-permute-start(f32[144,128]{1,0:T(8,128)S(1)} %add.42), channel_id=1, source_target_pairs={{0,8},{4,12},{8,0},{12,4},{1,9},{5,13},{9,1},{13,5},{2,10},{6,14},... | collective-permute-start | bytes 221192 | tf_op jit(solution)/shard_map/ppermute | solution.py:401
  65.8 6.2 %collective-permute-start.20 = (f32[144,128]{1,0:T(8,128)S(1)}, f32[144,128]{1,0:T(8,128)S(1)}, u32[]{:S(2)}, u32[]{:S(2)}) collective-permute-start(f32[144,128]{1,0:T(8,128)S(1)} %add.42), channel_id=1, source_target_pairs={{0,12},{4,8},{8,4},{12,0},{1,13},{5,9},{9,5},{13,1},{2,14},{6,10},... | collective-permute-start | bytes 221192 | tf_op jit(solution)/shard_map/ppermute | solution.py:401
  72.0 1.3 %collective-permute-start.21 = (f32[144,128]{1,0:T(8,128)S(1)}, f32[144,128]{1,0:T(8,128)S(1)}, u32[]{:S(2)}, u32[]{:S(2)}) collective-permute-start(f32[144,128]{1,0:T(8,128)S(1)} %add_add_fusion), channel_id=1, source_target_pairs={{0,1},{1,0},{2,3},{3,2},{4,5},{5,4},{6,7},{7,6},{8,9},{9,8},{10,11... | collective-permute-start | bytes 221192 | tf_op jit(solution)/shard_map/ppermute | solution.py:401

commit v6 on v5

--- a/solution.py
+++ b/solution.py
@@ -414,7 +414,8 @@
     mine, other = (lax.dynamic_index_in_dim(halves, b, 0, keepdims=False) for b in (bit, 1 - bit))
     part = mine + swap(other, "snp", 1)
     part = part + swap(part, "snp", 2)
-    part = (part + swap(part, "samp", 1)) + (swap(part, "samp", 2) + swap(part, "samp", 3))
+    part = part + swap(part, "samp", 1)
+    part = part + swap(part, "samp", 2)
     return both(part, swap(part, "snp", 1), bit == 0)
 
 
@@ -426,16 +427,15 @@
     samples = words * PLANES * n_samp
     inv_root = float(1.0 / samples**0.5)
     chunk = snps // n_samp
-    direct = n_samp <= 4 and chunk % LANES == 0
+    direct = n_samp in (2, 4) and chunk % LANES == 0
 
     other, sums = project(genotypes, basis_cols, True)
     got = swap(other, "snp", 1)
-    if n_snp <= 4:
-        more = sum(swap(sums, "snp", mask) for mask in range(1, n_snp))
-    else:
-        more = lax.psum(sums, "snp") - sums
+    more = swap(sums, "snp", 1 << (bits - 1))
     (mine,) = project(genotypes, basis_cols, False)
     *parts, sums = merge(mine, got, sums, more, 2)
+    for b in range(bits - 1):
+        sums = sums + swap(sums, "snp", 1 << b)
     if n_samp <= 4:
         for b in range(n_samp.bit_length() - 1):
             sums = sums + swap(sums, "samp", 1 << b)
@@ -456,7 +456,7 @@
         rows = finish(part, ready, sums, samples, group)
         scores = (rows, swap(rows, "snp", 1))
         if direct:
-            masks = (2, 1, 3)
+            masks = (2, 3, 1) if n_samp == 4 else (1,)
             coded = list(chunks_of_y(genotypes, scores, chunk, inv_root, masks[:1]))
             *others, own = chunks_of_y(genotypes, scores, chunk, inv_root, masks[1:] + (0,))
             coded += others

time: 82 us -> 80.2 us (0.978)
  waiting for transfers between devices: 34.9 us -> 32.4 us
    ppermute x22 -> x20, waiting for transfers between devices: 34.9 us -> 32.4 us  [swap(): return lax.ppermute(array, axis, [(i, i ^ mask) for i in range(size)])]
    ppermute x22 -> x20, starting transfers between devices: 26 us -> 26.7 us  [swap(): return lax.ppermute(array, axis, [(i, i ^ mask) for i in range(size)])]
  transfers between devices with their start and end apart: 22 -> 20, of which waited for: 17 -> 14; matrix products, arithmetic and copies ran while one was open for 0% -> 0% of each run, Pallas kernels for 7% -> 8%
where the time goes in v6:
time: 80.2 us; the launch traced here: 80 us
  waiting for transfers between devices  32.4 us (40%)
  starting transfers between devices  26.7 us (33%)
  Pallas kernels  17.3 us (22%)
  local copies, waits for them, and re-layouts  2.82 us (4%)
    ppermute x20, waiting for transfers between devices, swap(): return lax.ppermute(array, axis, [(i, i ^ mask) for i in range(size)])  32.4 us
    ppermute x20, starting transfers between devices, swap(): return lax.ppermute(array, axis, [(i, i ^ mask) for i in range(size)])  26.7 us
    pallas_call x1, Pallas kernels, orthonormalize(): pl.pallas_call(basis_kernel, out_shape=[jax.ShapeDtypeStruct((width, widt...  8.53 us
    pallas_call x4, Pallas kernels, chunks_of_y(): pl.pallas_call(kernel, out_shape=shapes, compiler_params=params(), name='...  4.93 us
    unnamed x6, local copies, waits for them, and re-layouts  2.82 us
    pallas_call x2, Pallas kernels, project(): pl.pallas_call(other_kernel if other else mine_kernel, out_shape=shapes,...  2.46 us
  transfers between devices with their start and end apart: 20, of which 14 were waited for; matrix products, arithmetic and copies ran while one was open for 0% of the time, Pallas kernels for 8%

profile of v6, /device:TPU:0, one launch (start us, length us, event | category | flops | bytes accessed | tf_op | source)
XLA Modules:
  0.0 80.0 jit_solution(14242450718615298324)
XLA Ops:
  0.6 0.0 copy-start
  0.6 1.6 %copy-done = s32[256,2048]{1,0:T(8,128)S(1)} copy-done((s32[256,2048]{1,0:T(8,128)S(1)}, s32[256,2048]{1,0:T(8,128)}, u32[]{:S(2)}) %copy-start) | copy-done | bytes 2097176
  2.2 1.2 %copy-done.2 = bf16[2048,256]{1,0:T(8,128)(2,1)S(1)} copy-done((bf16[2048,256]{1,0:T(8,128)(2,1)S(1)}, bf16[2048,256]{1,0:T(8,128)(2,1)}, u32[]{:S(2)}) %copy-start.2) | copy-done | bytes 1048600
  3.4 1.5 %project_other.1 = (f32[6,128,256]{2,1,0:T(8,128)S(1)}, f32[8,256]{1,0:T(8,128)S(1)}) custom-call(s32[256,2048]{1,0:T(8,128)S(1)} %copy-done, bf16[2048,256]{1,0:T(8,128)(2,1)S(1)} %copy-done.2), custom_call_target="tpu_custom_call" | custom-call | flops 805306368 | bytes 2883584 | tf_op jit(solution)/shard_map/project_other/pallas_call | solution.py:79
  4.9 0.5 collective-permute-start
  5.5 2.6 %collective-permute-start.1 = (f32[8,256]{1,0:T(8,128)S(1)}, f32[8,256]{1,0:T(8,128)S(1)}, u32[]{:S(2)}, u32[]{:S(2)}) collective-permute-start(f32[8,256]{1,0:T(8,128)S(1)} %get-tuple-element.22.sums), channel_id=1, source_target_pairs={{0,2},{1,3},{2,0},{3,1},{4,6},{5,7},{6,4},{7,5},{8,10},{9,11},{10,... | collective-permute-start | bytes 24584 | tf_op jit(solution)/shard_map/ppermute | solution.py:401
  8.0 1.0 %project_mine.1.mine = f32[6,128,256]{2,1,0:T(8,128)S(1)} custom-call(s32[256,2048]{1,0:T(8,128)S(1)} %copy-done, bf16[2048,256]{1,0:T(8,128)(2,1)S(1)} %copy-done.2), custom_call_target="tpu_custom_call" | custom-call | flops 805306368 | bytes 2883584 | tf_op jit(solution)/shard_map/project_mine/pallas_call | solution.py:79
  9.0 0.0 copy-start.1
  9.0 0.6 collective-permute-done.1.more
  9.6 0.0 collective-permute-done.got
  9.7 0.1 merge.1
  9.8 2.1 %collective-permute-start.2 = (f32[6,128,128]{2,1,0:T(8,128)S(1)}, f32[6,128,128]{2,1,0:T(8,128)S(1)}, u32[]{:S(2)}, u32[]{:S(2)}) collective-permute-start(f32[6,128,128]{2,1,0:T(8,128)S(1)} %get-tuple-element.23.mine), channel_id=1, source_target_pairs={{0,2},{1,3},{2,0},{3,1},{4,6},{5,7},{6,4},{7,5},{8,10},{9,11},{10,... | collective-permute-start | bytes 1179656 | tf_op jit(solution)/shard_map/ppermute | solution.py:401
  11.8 1.2 %collective-permute-done.3 = f32[8,256]{1,0:T(8,128)S(1)} collective-permute-done((f32[8,256]{1,0:T(8,128)S(1)}, f32[8,256]{1,0:T(8,128)S(1)}, u32[]{:S(2)}, u32[]{:S(2)}) %collective-permute-start.3) | collective-permute-done | bytes 8224 | tf_op jit(solution)/shard_map/ppermute | solution.py:401
  13.0 1.6 %collective-permute-start.4 = (f32[8,256]{1,0:T(8,128)S(1)}, f32[8,256]{1,0:T(8,128)S(1)}, u32[]{:S(2)}, u32[]{:S(2)}) collective-permute-start(f32[8,256]{1,0:T(8,128)S(1)} %add.29), channel_id=1, source_target_pairs={{0,4},{4,0},{8,12},{12,8},{1,5},{5,1},{9,13},{13,9},{2,6},{6,2},{1... | collective-permute-start | bytes 24584 | tf_op jit(solution)/shard_map/ppermute | solution.py:401
  14.6 2.1 %collective-permute-done.4 = f32[8,256]{1,0:T(8,128)S(1)} collective-permute-done((f32[8,256]{1,0:T(8,128)S(1)}, f32[8,256]{1,0:T(8,128)S(1)}, u32[]{:S(2)}, u32[]{:S(2)}) %collective-permute-start.4) | collective-permute-done | bytes 8224 | tf_op jit(solution)/shard_map/ppermute | solution.py:401
  16.7 2.6 %collective-permute-start.5 = (f32[8,256]{1,0:T(8,128)S(1)}, f32[8,256]{1,0:T(8,128)S(1)}, u32[]{:S(2)}, u32[]{:S(2)}) collective-permute-start(f32[8,256]{1,0:T(8,128)S(1)} %add.30), channel_id=1, source_target_pairs={{0,8},{4,12},{8,0},{12,4},{1,9},{5,13},{9,1},{13,5},{2,10},{6,14},... | collective-permute-start | bytes 24584 | tf_op jit(solution)/shard_map/ppermute | solution.py:401
  19.3 2.0 %collective-permute-done.5 = f32[8,256]{1,0:T(8,128)S(1)} collective-permute-done((f32[8,256]{1,0:T(8,128)S(1)}, f32[8,256]{1,0:T(8,128)S(1)}, u32[]{:S(2)}, u32[]{:S(2)}) %collective-permute-start.5) | collective-permute-done | bytes 8224 | tf_op jit(solution)/shard_map/ppermute | solution.py:401
  21.2 0.0 collective-permute-done.2.got
  21.2 0.9 %collective-permute-start.10 = (f32[6,128,128]{2,1,0:T(8,128)S(1)}, f32[6,128,128]{2,1,0:T(8,128)S(1)}, u32[]{:S(2)}, u32[]{:S(2)}) collective-permute-start(f32[6,128,128]{2,1,0:T(8,128)S(1)} %get-tuple-element.29.mine), channel_id=1, source_target_pairs={{0,2},{1,3},{2,0},{3,1},{4,6},{5,7},{6,4},{7,5},{8,10},{9,11},{10,... | collective-permute-start | bytes 1179656 | tf_op jit(solution)/shard_map/ppermute | solution.py:401
  22.2 0.1 collective-permute-start.6
  22.3 1.4 %collective-permute-done.6.other = bf16[6,128,128]{2,1,0:T(8,128)(2,1)S(1)} collective-permute-done((bf16[6,128,128]{2,1,0:T(8,128)(2,1)S(1)}, bf16[6,128,128]{2,1,0:T(8,128)(2,1)S(1)}, u32[]{:S(2)}, u32[]{:S(2)}) %collective-permute-start.6) | collective-permute-done | bytes 196640 | tf_op jit(solution)/shard_map/ppermute | solution.py:401
  23.7 0.8 chunks.5
  24.5 2.6 %collective-permute-start.7 = (s16[528,128]{1,0:T(8,128)(2,1)S(1)}, s16[528,128]{1,0:T(8,128)(2,1)S(1)}, u32[]{:S(2)}, u32[]{:S(2)}) collective-permute-start(s16[528,128]{1,0:T(8,128)(2,1)S(1)} %chunks.5), channel_id=1, source_target_pairs={{0,8},{4,12},{8,0},{12,4},{1,9},{5,13},{9,1},{13,5},{2,10},{6,14},... | collective-permute-start | bytes 405512 | tf_op jit(solution)/shard_map/ppermute | solution.py:401
  27.2 1.7 %chunks.4 = (s16[528,128]{1,0:T(8,128)(2,1)S(1)}, s16[528,128]{1,0:T(8,128)(2,1)S(1)}, f32[512,128]{1,0:T(8,128)S(1)}) custom-call(s32[256,2048]{1,0:T(8,128)S(1)} %copy-done.1, bf16[6,128,128]{2,1,0:T(8,128)(2,1)S(1)} %finish.2.mine, bf16[6,128,128]{2,1,0:T(8,128)(2,1)S(1)} %collective-permute-done.6.other), custom_call_target="tpu_custom_call" | custom-call | flops 603979776 | bytes 2359296 | tf_op jit(solution)/shard_map/chunks/pallas_call | solution.py:185
  28.8 5.1 %collective-permute-done.7.refs_0_ = s16[528,128]{1,0:T(8,128)(2,1)S(1)} collective-permute-done((s16[528,128]{1,0:T(8,128)(2,1)S(1)}, s16[528,128]{1,0:T(8,128)(2,1)S(1)}, u32[]{:S(2)}, u32[]{:S(2)}) %collective-permute-start.7) | collective-permute-done | bytes 135200 | tf_op jit(solution)/shard_map/ppermute | solution.py:401
  34.0 0.0 collective-permute-done.10.got
  34.0 0.1 finish.3.mine
  34.1 0.1 collective-permute-start.11
  34.1 3.6 %collective-permute-start.8 = (s16[528,128]{1,0:T(8,128)(2,1)S(1)}, s16[528,128]{1,0:T(8,128)(2,1)S(1)}, u32[]{:S(2)}, u32[]{:S(2)}) collective-permute-start(s16[528,128]{1,0:T(8,128)(2,1)S(1)} %get-tuple-element.26), channel_id=1, source_target_pairs={{0,12},{4,8},{8,4},{12,0},{1,13},{5,9},{9,5},{13,1},{2,14},{6,10},... | collective-permute-start | bytes 405512 | tf_op jit(solution)/shard_map/ppermute | solution.py:401
  37.7 0.8 chunks.7
  38.5 1.0 %collective-permute-start.12 = (s16[528,128]{1,0:T(8,128)(2,1)S(1)}, s16[528,128]{1,0:T(8,128)(2,1)S(1)}, u32[]{:S(2)}, u32[]{:S(2)}) collective-permute-start(s16[528,128]{1,0:T(8,128)(2,1)S(1)} %chunks.7), channel_id=1, source_target_pairs={{0,8},{4,12},{8,0},{12,4},{1,9},{5,13},{9,1},{13,5},{2,10},{6,14},... | collective-permute-start | bytes 405512 | tf_op jit(solution)/shard_map/ppermute | solution.py:401
  39.5 1.7 %chunks.6 = (s16[528,128]{1,0:T(8,128)(2,1)S(1)}, s16[528,128]{1,0:T(8,128)(2,1)S(1)}, f32[512,128]{1,0:T(8,128)S(1)}) custom-call(s32[256,2048]{1,0:T(8,128)S(1)} %copy-done.1, bf16[6,128,128]{2,1,0:T(8,128)(2,1)S(1)} %finish.3.mine, bf16[6,128,128]{2,1,0:T(8,128)(2,1)S(1)} %collective-permute-done.11.other), custom_call_target="tpu_custom_call" | custom-call | flops 603979776 | bytes 2359296 | tf_op jit(solution)/shard_map/chunks/pallas_call | solution.py:185
  41.1 3.6 %collective-permute-start.13 = (s16[528,128]{1,0:T(8,128)(2,1)S(1)}, s16[528,128]{1,0:T(8,128)(2,1)S(1)}, u32[]{:S(2)}, u32[]{:S(2)}) collective-permute-start(s16[528,128]{1,0:T(8,128)(2,1)S(1)} %get-tuple-element.32), channel_id=1, source_target_pairs={{0,12},{4,8},{8,4},{12,0},{1,13},{5,9},{9,5},{13,1},{2,14},{6,10},... | collective-permute-start | bytes 405512 | tf_op jit(solution)/shard_map/ppermute | solution.py:401
  44.7 2.1 %collective-permute-done.9.refs_2_ = s16[528,128]{1,0:T(8,128)(2,1)S(1)} collective-permute-done((s16[528,128]{1,0:T(8,128)(2,1)S(1)}, s16[528,128]{1,0:T(8,128)(2,1)S(1)}, u32[]{:S(2)}, u32[]{:S(2)}) %collective-permute-start.9) | collective-permute-done | bytes 135200 | tf_op jit(solution)/shard_map/ppermute | solution.py:401
  46.9 0.1 add_chunks.1.done
  47.0 5.4 %collective-permute-done.12.refs_0_ = s16[528,128]{1,0:T(8,128)(2,1)S(1)} collective-permute-done((s16[528,128]{1,0:T(8,128)(2,1)S(1)}, s16[528,128]{1,0:T(8,128)(2,1)S(1)}, u32[]{:S(2)}, u32[]{:S(2)}) %collective-permute-start.12) | collective-permute-done | bytes 135200 | tf_op jit(solution)/shard_map/ppermute | solution.py:401
  52.3 1.3 %collective-permute-done.14.refs_2_ = s16[528,128]{1,0:T(8,128)(2,1)S(1)} collective-permute-done((s16[528,128]{1,0:T(8,128)(2,1)S(1)}, s16[528,128]{1,0:T(8,128)(2,1)S(1)}, u32[]{:S(2)}, u32[]{:S(2)}) %collective-permute-start.14) | collective-permute-done | bytes 135200 | tf_op jit(solution)/shard_map/ppermute | solution.py:401
  53.6 1.0 %collect.1 = (f32[512,256]{1,0:T(8,128)}, f32[512,256]{1,0:T(8,128)S(1)}, f32[288,128]{1,0:T(8,128)S(1)}) custom-call(f32[512,128]{1,0:T(8,128)S(1)} %add_chunks.1.done, f32[512,128]{1,0:T(8,128)S(1)} %get-tuple-element.31.kept, s16[528,128]{1,0:T(8,128)(2,1)S(1)} %collective-permute-done.12.refs_0_, s16[528,128]{1,0:T(8,128)(2,1)S(1)} %collective-permute-done.13.refs_1_, ...), custom_call_target="tpu_custom_call" | custom-call | tf_op jit(solution)/shard_map/collect/pallas_call | solution.py:274
  54.7 1.3 %collective-permute-done.15 = f32[144,128]{1,0:T(8,128)S(1)} collective-permute-done((f32[144,128]{1,0:T(8,128)S(1)}, f32[144,128]{1,0:T(8,128)S(1)}, u32[]{:S(2)}, u32[]{:S(2)}) %collective-permute-start.15) | collective-permute-done | bytes 73760 | tf_op jit(solution)/shard_map/ppermute | solution.py:401
  55.9 1.2 %collective-permute-start.16 = (f32[144,128]{1,0:T(8,128)S(1)}, f32[144,128]{1,0:T(8,128)S(1)}, u32[]{:S(2)}, u32[]{:S(2)}) collective-permute-start(f32[144,128]{1,0:T(8,128)S(1)} %bitcast_add_fusion), channel_id=1, source_target_pairs={{0,2},{1,3},{2,0},{3,1},{4,6},{5,7},{6,4},{7,5},{8,10},{9,11},{10,... | collective-permute-start | bytes 221192 | tf_op jit(solution)/shard_map/ppermute | solution.py:401
  57.1 3.3 %collective-permute-done.16 = f32[144,128]{1,0:T(8,128)S(1)} collective-permute-done((f32[144,128]{1,0:T(8,128)S(1)}, f32[144,128]{1,0:T(8,128)S(1)}, u32[]{:S(2)}, u32[]{:S(2)}) %collective-permute-start.16) | collective-permute-done | bytes 73760 | tf_op jit(solution)/shard_map/ppermute | solution.py:401
  60.4 1.8 %collective-permute-start.17 = (f32[144,128]{1,0:T(8,128)S(1)}, f32[144,128]{1,0:T(8,128)S(1)}, u32[]{:S(2)}, u32[]{:S(2)}) collective-permute-start(f32[144,128]{1,0:T(8,128)S(1)} %add.35), channel_id=1, source_target_pairs={{0,4},{4,0},{8,12},{12,8},{1,5},{5,1},{9,13},{13,9},{2,6},{6,2},{1... | collective-permute-start | bytes 221192 | tf_op jit(solution)/shard_map/ppermute | solution.py:401
  62.2 2.6 %collective-permute-done.17 = f32[144,128]{1,0:T(8,128)S(1)} collective-permute-done((f32[144,128]{1,0:T(8,128)S(1)}, f32[144,128]{1,0:T(8,128)S(1)}, u32[]{:S(2)}, u32[]{:S(2)}) %collective-permute-start.17) | collective-permute-done | bytes 73760 | tf_op jit(solution)/shard_map/ppermute | solution.py:401
  64.8 2.6 %collective-permute-start.18 = (f32[144,128]{1,0:T(8,128)S(1)}, f32[144,128]{1,0:T(8,128)S(1)}, u32[]{:S(2)}, u32[]{:S(2)}) collective-permute-start(f32[144,128]{1,0:T(8,128)S(1)} %add.36), channel_id=1, source_target_pairs={{0,8},{4,12},{8,0},{12,4},{1,9},{5,13},{9,1},{13,5},{2,10},{6,14},... | collective-permute-start | bytes 221192 | tf_op jit(solution)/shard_map/ppermute | solution.py:401
  67.4 2.7 %collective-permute-done.18 = f32[144,128]{1,0:T(8,128)S(1)} collective-permute-done((f32[144,128]{1,0:T(8,128)S(1)}, f32[144,128]{1,0:T(8,128)S(1)}, u32[]{:S(2)}, u32[]{:S(2)}) %collective-permute-start.18) | collective-permute-done | bytes 73760 | tf_op jit(solution)/shard_map/ppermute | solution.py:401
  70.1 0.1 collective-permute-start.19
  70.2 1.2 %collective-permute-done.19 = f32[144,128]{1,0:T(8,128)S(1)} collective-permute-done((f32[144,128]{1,0:T(8,128)S(1)}, f32[144,128]{1,0:T(8,128)S(1)}, u32[]{:S(2)}, u32[]{:S(2)}) %collective-permute-start.19) | collective-permute-done | bytes 73760 | tf_op jit(solution)/shard_map/ppermute | solution.py:401
  71.5 8.5 %orthonormalize.1 = (f32[256,256]{1,0:T(8,128)}, f32[512,256]{1,0:T(8,128)}) custom-call(f32[288,128]{1,0:T(8,128)S(1)} %pad_maximum_fusion.gram, f32[512,256]{1,0:T(8,128)S(1)} %get-tuple-element.36.y), custom_call_target="tpu_custom_call" | custom-call | tf_op jit(solution)/shard_map/orthonormalize/pallas_call | solution.py:387
  (20 shorter events, 0.1 us)
Async XLA Ops:
  0.6 1.6 %copy-start = (s32[256,2048]{1,0:T(8,128)S(1)}, s32[256,2048]{1,0:T(8,128)}, u32[]{:S(2)}) copy-start(s32[256,2048]{1,0:T(8,128)} %words.11) | copy-start | bytes 6291460
  2.2 1.2 %copy-start.2 = (bf16[2048,256]{1,0:T(8,128)(2,1)S(1)}, bf16[2048,256]{1,0:T(8,128)(2,1)}, u32[]{:S(2)}) copy-start(bf16[2048,256]{1,0:T(8,128)(2,1)} %basis.3) | copy-start | bytes 3145732
  4.9 4.7 %collective-permute-start = (f32[6,128,256]{2,1,0:T(8,128)S(1)}, f32[6,128,256]{2,1,0:T(8,128)S(1)}, u32[]{:S(2)}, u32[]{:S(2)}) collective-permute-start(f32[6,128,256]{2,1,0:T(8,128)S(1)} %get-tuple-element.21), channel_id=1, source_target_pairs={{0,1},{1,0},{2,3},{3,2},{4,5},{5,4},{6,7},{7,6},{8,9},{9,8},{10,11... | collective-permute-start | bytes 2359304 | tf_op jit(solution)/shard_map/ppermute | solution.py:401
  5.5 4.2 %collective-permute-start.1 = (f32[8,256]{1,0:T(8,128)S(1)}, f32[8,256]{1,0:T(8,128)S(1)}, u32[]{:S(2)}, u32[]{:S(2)}) collective-permute-start(f32[8,256]{1,0:T(8,128)S(1)} %get-tuple-element.22.sums), channel_id=1, source_target_pairs={{0,2},{1,3},{2,0},{3,1},{4,6},{5,7},{6,4},{7,5},{8,10},{9,11},{10,... | collective-permute-start | bytes 24584 | tf_op jit(solution)/shard_map/ppermute | solution.py:401
  9.0 14.7 %copy-start.1 = (s32[256,2048]{1,0:T(8,128)S(1)}, s32[256,2048]{1,0:T(8,128)}, u32[]{:S(2)}) copy-start(s32[256,2048]{1,0:T(8,128)} %words.11) | copy-start | bytes 6291460
  9.8 11.5 %collective-permute-start.2 = (f32[6,128,128]{2,1,0:T(8,128)S(1)}, f32[6,128,128]{2,1,0:T(8,128)S(1)}, u32[]{:S(2)}, u32[]{:S(2)}) collective-permute-start(f32[6,128,128]{2,1,0:T(8,128)S(1)} %get-tuple-element.23.mine), channel_id=1, source_target_pairs={{0,2},{1,3},{2,0},{3,1},{4,6},{5,7},{6,4},{7,5},{8,10},{9,11},{10,... | collective-permute-start | bytes 1179656 | tf_op jit(solution)/shard_map/ppermute | solution.py:401
  11.8 1.2 %collective-permute-start.3 = (f32[8,256]{1,0:T(8,128)S(1)}, f32[8,256]{1,0:T(8,128)S(1)}, u32[]{:S(2)}, u32[]{:S(2)}) collective-permute-start(f32[8,256]{1,0:T(8,128)S(1)} %get-tuple-element.24), channel_id=1, source_target_pairs={{0,1},{1,0},{2,3},{3,2},{4,5},{5,4},{6,7},{7,6},{8,9},{9,8},{10,11... | collective-permute-start | bytes 24584 | tf_op jit(solution)/shard_map/ppermute | solution.py:401
  13.0 3.7 %collective-permute-start.4 = (f32[8,256]{1,0:T(8,128)S(1)}, f32[8,256]{1,0:T(8,128)S(1)}, u32[]{:S(2)}, u32[]{:S(2)}) collective-permute-start(f32[8,256]{1,0:T(8,128)S(1)} %add.29), channel_id=1, source_target_pairs={{0,4},{4,0},{8,12},{12,8},{1,5},{5,1},{9,13},{13,9},{2,6},{6,2},{1... | collective-permute-start | bytes 24584 | tf_op jit(solution)/shard_map/ppermute | solution.py:401
  16.7 4.5 %collective-permute-start.5 = (f32[8,256]{1,0:T(8,128)S(1)}, f32[8,256]{1,0:T(8,128)S(1)}, u32[]{:S(2)}, u32[]{:S(2)}) collective-permute-start(f32[8,256]{1,0:T(8,128)S(1)} %add.30), channel_id=1, source_target_pairs={{0,8},{4,12},{8,0},{12,4},{1,9},{5,13},{9,1},{13,5},{2,10},{6,14},... | collective-permute-start | bytes 24584 | tf_op jit(solution)/shard_map/ppermute | solution.py:401
  21.2 12.8 %collective-permute-start.10 = (f32[6,128,128]{2,1,0:T(8,128)S(1)}, f32[6,128,128]{2,1,0:T(8,128)S(1)}, u32[]{:S(2)}, u32[]{:S(2)}) collective-permute-start(f32[6,128,128]{2,1,0:T(8,128)S(1)} %get-tuple-element.29.mine), channel_id=1, source_target_pairs={{0,2},{1,3},{2,0},{3,1},{4,6},{5,7},{6,4},{7,5},{8,10},{9,11},{10,... | collective-permute-start | bytes 1179656 | tf_op jit(solution)/shard_map/ppermute | solution.py:401
  22.2 1.5 %collective-permute-start.6 = (bf16[6,128,128]{2,1,0:T(8,128)(2,1)S(1)}, bf16[6,128,128]{2,1,0:T(8,128)(2,1)S(1)}, u32[]{:S(2)}, u32[]{:S(2)}) collective-permute-start(bf16[6,128,128]{2,1,0:T(8,128)(2,1)S(1)} %finish.2.mine), channel_id=1, source_target_pairs={{0,1},{1,0},{2,3},{3,2},{4,5},{5,4},{6,7},{7,6},{8,9},{9,8},{10,11... | collective-permute-start | bytes 589832 | tf_op jit(solution)/shard_map/ppermute | solution.py:401
  24.5 9.5 %collective-permute-start.7 = (s16[528,128]{1,0:T(8,128)(2,1)S(1)}, s16[528,128]{1,0:T(8,128)(2,1)S(1)}, u32[]{:S(2)}, u32[]{:S(2)}) collective-permute-start(s16[528,128]{1,0:T(8,128)(2,1)S(1)} %chunks.5), channel_id=1, source_target_pairs={{0,8},{4,12},{8,0},{12,4},{1,9},{5,13},{9,1},{13,5},{2,10},{6,14},... | collective-permute-start | bytes 405512 | tf_op jit(solution)/shard_map/ppermute | solution.py:401
  34.1 3.6 %collective-permute-start.11 = (bf16[6,128,128]{2,1,0:T(8,128)(2,1)S(1)}, bf16[6,128,128]{2,1,0:T(8,128)(2,1)S(1)}, u32[]{:S(2)}, u32[]{:S(2)}) collective-permute-start(bf16[6,128,128]{2,1,0:T(8,128)(2,1)S(1)} %finish.3.mine), channel_id=1, source_target_pairs={{0,1},{1,0},{2,3},{3,2},{4,5},{5,4},{6,7},{7,6},{8,9},{9,8},{10,11... | collective-permute-start | bytes 589832 | tf_op jit(solution)/shard_map/ppermute | solution.py:401
  34.1 10.6 %collective-permute-start.8 = (s16[528,128]{1,0:T(8,128)(2,1)S(1)}, s16[528,128]{1,0:T(8,128)(2,1)S(1)}, u32[]{:S(2)}, u32[]{:S(2)}) collective-permute-start(s16[528,128]{1,0:T(8,128)(2,1)S(1)} %get-tuple-element.26), channel_id=1, source_target_pairs={{0,12},{4,8},{8,4},{12,0},{1,13},{5,9},{9,5},{13,1},{2,14},{6,10},... | collective-permute-start | bytes 405512 | tf_op jit(solution)/shard_map/ppermute | solution.py:401
  37.7 9.2 %collective-permute-start.9 = (s16[528,128]{1,0:T(8,128)(2,1)S(1)}, s16[528,128]{1,0:T(8,128)(2,1)S(1)}, u32[]{:S(2)}, u32[]{:S(2)}) collective-permute-start(s16[528,128]{1,0:T(8,128)(2,1)S(1)} %get-tuple-element.27), channel_id=1, source_target_pairs={{0,4},{4,0},{8,12},{12,8},{1,5},{5,1},{9,13},{13,9},{2,6},{6,2},{1... | collective-permute-start | bytes 405512 | tf_op jit(solution)/shard_map/ppermute | solution.py:401
  38.5 13.8 %collective-permute-start.12 = (s16[528,128]{1,0:T(8,128)(2,1)S(1)}, s16[528,128]{1,0:T(8,128)(2,1)S(1)}, u32[]{:S(2)}, u32[]{:S(2)}) collective-permute-start(s16[528,128]{1,0:T(8,128)(2,1)S(1)} %chunks.7), channel_id=1, source_target_pairs={{0,8},{4,12},{8,0},{12,4},{1,9},{5,13},{9,1},{13,5},{2,10},{6,14},... | collective-permute-start | bytes 405512 | tf_op jit(solution)/shard_map/ppermute | solution.py:401
  41.1 11.2 %collective-permute-start.13 = (s16[528,128]{1,0:T(8,128)(2,1)S(1)}, s16[528,128]{1,0:T(8,128)(2,1)S(1)}, u32[]{:S(2)}, u32[]{:S(2)}) collective-permute-start(s16[528,128]{1,0:T(8,128)(2,1)S(1)} %get-tuple-element.32), channel_id=1, source_target_pairs={{0,12},{4,8},{8,4},{12,0},{1,13},{5,9},{9,5},{13,1},{2,14},{6,10},... | collective-permute-start | bytes 405512 | tf_op jit(solution)/shard_map/ppermute | solution.py:401
  44.7 8.9 %collective-permute-start.14 = (s16[528,128]{1,0:T(8,128)(2,1)S(1)}, s16[528,128]{1,0:T(8,128)(2,1)S(1)}, u32[]{:S(2)}, u32[]{:S(2)}) collective-permute-start(s16[528,128]{1,0:T(8,128)(2,1)S(1)} %get-tuple-element.33), channel_id=1, source_target_pairs={{0,4},{4,0},{8,12},{12,8},{1,5},{5,1},{9,13},{13,9},{2,6},{6,2},{1... | collective-permute-start | bytes 405512 | tf_op jit(solution)/shard_map/ppermute | solution.py:401
  54.7 1.3 %collective-permute-start.15 = (f32[144,128]{1,0:T(8,128)S(1)}, f32[144,128]{1,0:T(8,128)S(1)}, u32[]{:S(2)}, u32[]{:S(2)}) collective-permute-start(f32[144,128]{1,0:T(8,128)S(1)} %dynamic-slice_bitcast_fusion), channel_id=1, source_target_pairs={{0,1},{1,0},{2,3},{3,2},{4,5},{5,4},{6,7},{7,6},{8,9},{9,8},{10,11... | collective-permute-start | bytes 221192 | tf_op jit(solution)/shard_map/ppermute | solution.py:401
  55.9 4.4 %collective-permute-start.16 = (f32[144,128]{1,0:T(8,128)S(1)}, f32[144,128]{1,0:T(8,128)S(1)}, u32[]{:S(2)}, u32[]{:S(2)}) collective-permute-start(f32[144,128]{1,0:T(8,128)S(1)} %bitcast_add_fusion), channel_id=1, source_target_pairs={{0,2},{1,3},{2,0},{3,1},{4,6},{5,7},{6,4},{7,5},{8,10},{9,11},{10,... | collective-permute-start | bytes 221192 | tf_op jit(solution)/shard_map/ppermute | solution.py:401
  60.4 4.4 %collective-permute-start.17 = (f32[144,128]{1,0:T(8,128)S(1)}, f32[144,128]{1,0:T(8,128)S(1)}, u32[]{:S(2)}, u32[]{:S(2)}) collective-permute-start(f32[144,128]{1,0:T(8,128)S(1)} %add.35), channel_id=1, source_target_pairs={{0,4},{4,0},{8,12},{12,8},{1,5},{5,1},{9,13},{13,9},{2,6},{6,2},{1... | collective-permute-start | bytes 221192 | tf_op jit(solution)/shard_map/ppermute | solution.py:401
  64.8 5.3 %collective-permute-start.18 = (f32[144,128]{1,0:T(8,128)S(1)}, f32[144,128]{1,0:T(8,128)S(1)}, u32[]{:S(2)}, u32[]{:S(2)}) collective-permute-start(f32[144,128]{1,0:T(8,128)S(1)} %add.36), channel_id=1, source_target_pairs={{0,8},{4,12},{8,0},{12,4},{1,9},{5,13},{9,1},{13,5},{2,10},{6,14},... | collective-permute-start | bytes 221192 | tf_op jit(solution)/shard_map/ppermute | solution.py:401
  70.1 1.3 %collective-permute-start.19 = (f32[144,128]{1,0:T(8,128)S(1)}, f32[144,128]{1,0:T(8,128)S(1)}, u32[]{:S(2)}, u32[]{:S(2)}) collective-permute-start(f32[144,128]{1,0:T(8,128)S(1)} %add.37), channel_id=1, source_target_pairs={{0,1},{1,0},{2,3},{3,2},{4,5},{5,4},{6,7},{7,6},{8,9},{9,8},{10,11... | collective-permute-start | bytes 221192 | tf_op jit(solution)/shard_map/ppermute | solution.py:401

commit v7 on v6

--- a/solution.py
+++ b/solution.py
@@ -456,7 +456,7 @@
         rows = finish(part, ready, sums, samples, group)
         scores = (rows, swap(rows, "snp", 1))
         if direct:
-            masks = (2, 3, 1) if n_samp == 4 else (1,)
+            masks = ((2, 3, 1) if group else (3, 2, 1)) if n_samp == 4 else (1,)
             coded = list(chunks_of_y(genotypes, scores, chunk, inv_root, masks[:1]))
             *others, own = chunks_of_y(genotypes, scores, chunk, inv_root, masks[1:] + (0,))
             coded += others

time: 80.2 us -> 80 us (level)
  waiting for transfers between devices: 32.4 us -> 29.5 us
  starting transfers between devices: 26.7 us -> 29.4 us
    ppermute x20, waiting for transfers between devices: 32.4 us -> 29.5 us  [swap(): return lax.ppermute(array, axis, [(i, i ^ mask) for i in range(size)])]
    ppermute x20, starting transfers between devices: 26.7 us -> 29.4 us  [swap(): return lax.ppermute(array, axis, [(i, i ^ mask) for i in range(size)])]
  transfers between devices with their start and end apart: 20 -> 20, of which waited for: 14 -> 15; matrix products, arithmetic and copies ran while one was open for 0% -> 0% of each run, Pallas kernels for 8% -> 8%
where the time goes in v7:
time: 80 us; the launch traced here: 79.8 us
  waiting for transfers between devices  29.5 us (37%)
  starting transfers between devices  29.4 us (37%)
  Pallas kernels  17.2 us (22%)
  local copies, waits for them, and re-layouts  2.82 us (4%)
    ppermute x20, waiting for transfers between devices, swap(): return lax.ppermute(array, axis, [(i, i ^ mask) for i in range(size)])  29.5 us
    ppermute x20, starting transfers between devices, swap(): return lax.ppermute(array, axis, [(i, i ^ mask) for i in range(size)])  29.4 us
    pallas_call x1, Pallas kernels, orthonormalize(): pl.pallas_call(basis_kernel, out_shape=[jax.ShapeDtypeStruct((width, widt...  8.53 us
    pallas_call x4, Pallas kernels, chunks_of_y(): pl.pallas_call(kernel, out_shape=shapes, compiler_params=params(), name='...  4.92 us
    unnamed x6, local copies, waits for them, and re-layouts  2.82 us
    pallas_call x2, Pallas kernels, project(): pl.pallas_call(other_kernel if other else mine_kernel, out_shape=shapes,...  2.46 us
  transfers between devices with their start and end apart: 20, of which 15 were waited for; matrix products, arithmetic and copies ran while one was open for 0% of the time, Pallas kernels for 8%

profile of v7, /device:TPU:0, one launch (start us, length us, event | category | flops | bytes accessed | tf_op | source)
XLA Modules:
  0.0 79.8 jit_solution(17792516334343872808)
XLA Ops:
  0.6 0.0 copy-start
  0.6 1.6 %copy-done = s32[256,2048]{1,0:T(8,128)S(1)} copy-done((s32[256,2048]{1,0:T(8,128)S(1)}, s32[256,2048]{1,0:T(8,128)}, u32[]{:S(2)}) %copy-start) | copy-done | bytes 2097176
  2.2 1.2 %copy-done.2 = bf16[2048,256]{1,0:T(8,128)(2,1)S(1)} copy-done((bf16[2048,256]{1,0:T(8,128)(2,1)S(1)}, bf16[2048,256]{1,0:T(8,128)(2,1)}, u32[]{:S(2)}) %copy-start.2) | copy-done | bytes 1048600
  3.4 1.5 %project_other.1 = (f32[6,128,256]{2,1,0:T(8,128)S(1)}, f32[8,256]{1,0:T(8,128)S(1)}) custom-call(s32[256,2048]{1,0:T(8,128)S(1)} %copy-done, bf16[2048,256]{1,0:T(8,128)(2,1)S(1)} %copy-done.2), custom_call_target="tpu_custom_call" | custom-call | flops 805306368 | bytes 2883584 | tf_op jit(solution)/shard_map/project_other/pallas_call | solution.py:79
  4.9 0.5 collective-permute-start
  5.5 2.6 %collective-permute-start.1 = (f32[8,256]{1,0:T(8,128)S(1)}, f32[8,256]{1,0:T(8,128)S(1)}, u32[]{:S(2)}, u32[]{:S(2)}) collective-permute-start(f32[8,256]{1,0:T(8,128)S(1)} %get-tuple-element.22.sums), channel_id=1, source_target_pairs={{0,2},{1,3},{2,0},{3,1},{4,6},{5,7},{6,4},{7,5},{8,10},{9,11},{10,... | collective-permute-start | bytes 24584 | tf_op jit(solution)/shard_map/ppermute | solution.py:401
  8.0 1.0 %project_mine.1.mine = f32[6,128,256]{2,1,0:T(8,128)S(1)} custom-call(s32[256,2048]{1,0:T(8,128)S(1)} %copy-done, bf16[2048,256]{1,0:T(8,128)(2,1)S(1)} %copy-done.2), custom_call_target="tpu_custom_call" | custom-call | flops 805306368 | bytes 2883584 | tf_op jit(solution)/shard_map/project_mine/pallas_call | solution.py:79
  9.0 0.0 copy-start.1
  9.0 0.6 collective-permute-done.1.more
  9.7 0.1 merge.1
  9.8 2.1 %collective-permute-start.2 = (f32[6,128,128]{2,1,0:T(8,128)S(1)}, f32[6,128,128]{2,1,0:T(8,128)S(1)}, u32[]{:S(2)}, u32[]{:S(2)}) collective-permute-start(f32[6,128,128]{2,1,0:T(8,128)S(1)} %get-tuple-element.23.mine), channel_id=1, source_target_pairs={{0,2},{1,3},{2,0},{3,1},{4,6},{5,7},{6,4},{7,5},{8,10},{9,11},{10,... | collective-permute-start | bytes 1179656 | tf_op jit(solution)/shard_map/ppermute | solution.py:401
  11.8 0.0 collective-permute-start.3
  11.8 1.2 %collective-permute-done.3 = f32[8,256]{1,0:T(8,128)S(1)} collective-permute-done((f32[8,256]{1,0:T(8,128)S(1)}, f32[8,256]{1,0:T(8,128)S(1)}, u32[]{:S(2)}, u32[]{:S(2)}) %collective-permute-start.3) | collective-permute-done | bytes 8224 | tf_op jit(solution)/shard_map/ppermute | solution.py:401
  13.0 1.6 %collective-permute-start.4 = (f32[8,256]{1,0:T(8,128)S(1)}, f32[8,256]{1,0:T(8,128)S(1)}, u32[]{:S(2)}, u32[]{:S(2)}) collective-permute-start(f32[8,256]{1,0:T(8,128)S(1)} %add.29), channel_id=1, source_target_pairs={{0,4},{4,0},{8,12},{12,8},{1,5},{5,1},{9,13},{13,9},{2,6},{6,2},{1... | collective-permute-start | bytes 24584 | tf_op jit(solution)/shard_map/ppermute | solution.py:401
  14.6 2.1 %collective-permute-done.4 = f32[8,256]{1,0:T(8,128)S(1)} collective-permute-done((f32[8,256]{1,0:T(8,128)S(1)}, f32[8,256]{1,0:T(8,128)S(1)}, u32[]{:S(2)}, u32[]{:S(2)}) %collective-permute-start.4) | collective-permute-done | bytes 8224 | tf_op jit(solution)/shard_map/ppermute | solution.py:401
  16.7 2.6 %collective-permute-start.5 = (f32[8,256]{1,0:T(8,128)S(1)}, f32[8,256]{1,0:T(8,128)S(1)}, u32[]{:S(2)}, u32[]{:S(2)}) collective-permute-start(f32[8,256]{1,0:T(8,128)S(1)} %add.30), channel_id=1, source_target_pairs={{0,8},{4,12},{8,0},{12,4},{1,9},{5,13},{9,1},{13,5},{2,10},{6,14},... | collective-permute-start | bytes 24584 | tf_op jit(solution)/shard_map/ppermute | solution.py:401
  19.3 2.0 %collective-permute-done.5 = f32[8,256]{1,0:T(8,128)S(1)} collective-permute-done((f32[8,256]{1,0:T(8,128)S(1)}, f32[8,256]{1,0:T(8,128)S(1)}, u32[]{:S(2)}, u32[]{:S(2)}) %collective-permute-start.5) | collective-permute-done | bytes 8224 | tf_op jit(solution)/shard_map/ppermute | solution.py:401
  21.2 0.9 %collective-permute-start.10 = (f32[6,128,128]{2,1,0:T(8,128)S(1)}, f32[6,128,128]{2,1,0:T(8,128)S(1)}, u32[]{:S(2)}, u32[]{:S(2)}) collective-permute-start(f32[6,128,128]{2,1,0:T(8,128)S(1)} %get-tuple-element.29.mine), channel_id=1, source_target_pairs={{0,2},{1,3},{2,0},{3,1},{4,6},{5,7},{6,4},{7,5},{8,10},{9,11},{10,... | collective-permute-start | bytes 1179656 | tf_op jit(solution)/shard_map/ppermute | solution.py:401
  22.2 0.1 collective-permute-start.6
  22.3 1.4 %collective-permute-done.6.other = bf16[6,128,128]{2,1,0:T(8,128)(2,1)S(1)} collective-permute-done((bf16[6,128,128]{2,1,0:T(8,128)(2,1)S(1)}, bf16[6,128,128]{2,1,0:T(8,128)(2,1)S(1)}, u32[]{:S(2)}, u32[]{:S(2)}) %collective-permute-start.6) | collective-permute-done | bytes 196640 | tf_op jit(solution)/shard_map/ppermute | solution.py:401
  23.7 0.8 chunks.5
  24.5 3.7 %collective-permute-start.7 = (s16[528,128]{1,0:T(8,128)(2,1)S(1)}, s16[528,128]{1,0:T(8,128)(2,1)S(1)}, u32[]{:S(2)}, u32[]{:S(2)}) collective-permute-start(s16[528,128]{1,0:T(8,128)(2,1)S(1)} %chunks.5), channel_id=1, source_target_pairs={{0,12},{4,8},{8,4},{12,0},{1,13},{5,9},{9,5},{13,1},{2,14},{6,10},... | collective-permute-start | bytes 405512 | tf_op jit(solution)/shard_map/ppermute | solution.py:401
  28.2 1.7 %chunks.4 = (s16[528,128]{1,0:T(8,128)(2,1)S(1)}, s16[528,128]{1,0:T(8,128)(2,1)S(1)}, f32[512,128]{1,0:T(8,128)S(1)}) custom-call(s32[256,2048]{1,0:T(8,128)S(1)} %copy-done.1, bf16[6,128,128]{2,1,0:T(8,128)(2,1)S(1)} %finish.2.mine, bf16[6,128,128]{2,1,0:T(8,128)(2,1)S(1)} %collective-permute-done.6.other), custom_call_target="tpu_custom_call" | custom-call | flops 603979776 | bytes 2359296 | tf_op jit(solution)/shard_map/chunks/pallas_call | solution.py:185
  29.9 2.3 %collective-permute-done.7.refs_0_ = s16[528,128]{1,0:T(8,128)(2,1)S(1)} collective-permute-done((s16[528,128]{1,0:T(8,128)(2,1)S(1)}, s16[528,128]{1,0:T(8,128)(2,1)S(1)}, u32[]{:S(2)}, u32[]{:S(2)}) %collective-permute-start.7) | collective-permute-done | bytes 135200 | tf_op jit(solution)/shard_map/ppermute | solution.py:401
  32.2 0.1 finish.3.mine
  32.2 0.1 collective-permute-start.11
  32.3 3.6 %collective-permute-start.8 = (s16[528,128]{1,0:T(8,128)(2,1)S(1)}, s16[528,128]{1,0:T(8,128)(2,1)S(1)}, u32[]{:S(2)}, u32[]{:S(2)}) collective-permute-start(s16[528,128]{1,0:T(8,128)(2,1)S(1)} %get-tuple-element.26), channel_id=1, source_target_pairs={{0,8},{4,12},{8,0},{12,4},{1,9},{5,13},{9,1},{13,5},{2,10},{6,14},... | collective-permute-start | bytes 405512 | tf_op jit(solution)/shard_map/ppermute | solution.py:401
  35.9 0.6 collective-permute-start.9
  36.5 0.8 chunks.7
  37.3 1.4 %collective-permute-start.12 = (s16[528,128]{1,0:T(8,128)(2,1)S(1)}, s16[528,128]{1,0:T(8,128)(2,1)S(1)}, u32[]{:S(2)}, u32[]{:S(2)}) collective-permute-start(s16[528,128]{1,0:T(8,128)(2,1)S(1)} %chunks.7), channel_id=1, source_target_pairs={{0,8},{4,12},{8,0},{12,4},{1,9},{5,13},{9,1},{13,5},{2,10},{6,14},... | collective-permute-start | bytes 405512 | tf_op jit(solution)/shard_map/ppermute | solution.py:401
  38.7 1.7 %chunks.6 = (s16[528,128]{1,0:T(8,128)(2,1)S(1)}, s16[528,128]{1,0:T(8,128)(2,1)S(1)}, f32[512,128]{1,0:T(8,128)S(1)}) custom-call(s32[256,2048]{1,0:T(8,128)S(1)} %copy-done.1, bf16[6,128,128]{2,1,0:T(8,128)(2,1)S(1)} %finish.3.mine, bf16[6,128,128]{2,1,0:T(8,128)(2,1)S(1)} %collective-permute-done.11.other), custom_call_target="tpu_custom_call" | custom-call | flops 603979776 | bytes 2359296 | tf_op jit(solution)/shard_map/chunks/pallas_call | solution.py:185
  40.4 2.5 %collective-permute-start.13 = (s16[528,128]{1,0:T(8,128)(2,1)S(1)}, s16[528,128]{1,0:T(8,128)(2,1)S(1)}, u32[]{:S(2)}, u32[]{:S(2)}) collective-permute-start(s16[528,128]{1,0:T(8,128)(2,1)S(1)} %get-tuple-element.32), channel_id=1, source_target_pairs={{0,12},{4,8},{8,4},{12,0},{1,13},{5,9},{9,5},{13,1},{2,14},{6,10},... | collective-permute-start | bytes 405512 | tf_op jit(solution)/shard_map/ppermute | solution.py:401
  42.9 0.4 collective-permute-done.8.refs_1_
  43.3 0.8 %collective-permute-done.9.refs_2_ = s16[528,128]{1,0:T(8,128)(2,1)S(1)} collective-permute-done((s16[528,128]{1,0:T(8,128)(2,1)S(1)}, s16[528,128]{1,0:T(8,128)(2,1)S(1)}, u32[]{:S(2)}, u32[]{:S(2)}) %collective-permute-start.9) | collective-permute-done | bytes 135200 | tf_op jit(solution)/shard_map/ppermute | solution.py:401
  44.1 0.1 add_chunks.1.done
  44.3 7.8 %collective-permute-done.12.refs_0_ = s16[528,128]{1,0:T(8,128)(2,1)S(1)} collective-permute-done((s16[528,128]{1,0:T(8,128)(2,1)S(1)}, s16[528,128]{1,0:T(8,128)(2,1)S(1)}, u32[]{:S(2)}, u32[]{:S(2)}) %collective-permute-start.12) | collective-permute-done | bytes 135200 | tf_op jit(solution)/shard_map/ppermute | solution.py:401
  52.0 0.5 collective-permute-done.14.refs_2_
  52.5 1.0 %collect.1 = (f32[512,256]{1,0:T(8,128)}, f32[512,256]{1,0:T(8,128)S(1)}, f32[288,128]{1,0:T(8,128)S(1)}) custom-call(f32[512,128]{1,0:T(8,128)S(1)} %add_chunks.1.done, f32[512,128]{1,0:T(8,128)S(1)} %get-tuple-element.31.kept, s16[528,128]{1,0:T(8,128)(2,1)S(1)} %collective-permute-done.12.refs_0_, s16[528,128]{1,0:T(8,128)(2,1)S(1)} %collective-permute-done.13.refs_1_, ...), custom_call_target="tpu_custom_call" | custom-call | tf_op jit(solution)/shard_map/collect/pallas_call | solution.py:274
  53.6 1.3 %collective-permute-done.15 = f32[144,128]{1,0:T(8,128)S(1)} collective-permute-done((f32[144,128]{1,0:T(8,128)S(1)}, f32[144,128]{1,0:T(8,128)S(1)}, u32[]{:S(2)}, u32[]{:S(2)}) %collective-permute-start.15) | collective-permute-done | bytes 73760 | tf_op jit(solution)/shard_map/ppermute | solution.py:401
  54.8 1.2 %collective-permute-start.16 = (f32[144,128]{1,0:T(8,128)S(1)}, f32[144,128]{1,0:T(8,128)S(1)}, u32[]{:S(2)}, u32[]{:S(2)}) collective-permute-start(f32[144,128]{1,0:T(8,128)S(1)} %bitcast_add_fusion), channel_id=1, source_target_pairs={{0,2},{1,3},{2,0},{3,1},{4,6},{5,7},{6,4},{7,5},{8,10},{9,11},{10,... | collective-permute-start | bytes 221192 | tf_op jit(solution)/shard_map/ppermute | solution.py:401
  56.0 3.3 %collective-permute-done.16 = f32[144,128]{1,0:T(8,128)S(1)} collective-permute-done((f32[144,128]{1,0:T(8,128)S(1)}, f32[144,128]{1,0:T(8,128)S(1)}, u32[]{:S(2)}, u32[]{:S(2)}) %collective-permute-start.16) | collective-permute-done | bytes 73760 | tf_op jit(solution)/shard_map/ppermute | solution.py:401
  59.3 2.8 %collective-permute-start.17 = (f32[144,128]{1,0:T(8,128)S(1)}, f32[144,128]{1,0:T(8,128)S(1)}, u32[]{:S(2)}, u32[]{:S(2)}) collective-permute-start(f32[144,128]{1,0:T(8,128)S(1)} %add.35), channel_id=1, source_target_pairs={{0,4},{4,0},{8,12},{12,8},{1,5},{5,1},{9,13},{13,9},{2,6},{6,2},{1... | collective-permute-start | bytes 221192 | tf_op jit(solution)/shard_map/ppermute | solution.py:401
  62.0 2.3 %collective-permute-done.17 = f32[144,128]{1,0:T(8,128)S(1)} collective-permute-done((f32[144,128]{1,0:T(8,128)S(1)}, f32[144,128]{1,0:T(8,128)S(1)}, u32[]{:S(2)}, u32[]{:S(2)}) %collective-permute-start.17) | collective-permute-done | bytes 73760 | tf_op jit(solution)/shard_map/ppermute | solution.py:401
  64.4 3.2 %collective-permute-start.18 = (f32[144,128]{1,0:T(8,128)S(1)}, f32[144,128]{1,0:T(8,128)S(1)}, u32[]{:S(2)}, u32[]{:S(2)}) collective-permute-start(f32[144,128]{1,0:T(8,128)S(1)} %add.36), channel_id=1, source_target_pairs={{0,8},{4,12},{8,0},{12,4},{1,9},{5,13},{9,1},{13,5},{2,10},{6,14},... | collective-permute-start | bytes 221192 | tf_op jit(solution)/shard_map/ppermute | solution.py:401
  67.6 2.3 %collective-permute-done.18 = f32[144,128]{1,0:T(8,128)S(1)} collective-permute-done((f32[144,128]{1,0:T(8,128)S(1)}, f32[144,128]{1,0:T(8,128)S(1)}, u32[]{:S(2)}, u32[]{:S(2)}) %collective-permute-start.18) | collective-permute-done | bytes 73760 | tf_op jit(solution)/shard_map/ppermute | solution.py:401
  69.9 0.1 collective-permute-start.19
  70.0 1.2 %collective-permute-done.19 = f32[144,128]{1,0:T(8,128)S(1)} collective-permute-done((f32[144,128]{1,0:T(8,128)S(1)}, f32[144,128]{1,0:T(8,128)S(1)}, u32[]{:S(2)}, u32[]{:S(2)}) %collective-permute-start.19) | collective-permute-done | bytes 73760 | tf_op jit(solution)/shard_map/ppermute | solution.py:401
  71.3 8.5 %orthonormalize.1 = (f32[256,256]{1,0:T(8,128)}, f32[512,256]{1,0:T(8,128)}) custom-call(f32[288,128]{1,0:T(8,128)S(1)} %pad_maximum_fusion.gram, f32[512,256]{1,0:T(8,128)S(1)} %get-tuple-element.36.y), custom_call_target="tpu_custom_call" | custom-call | tf_op jit(solution)/shard_map/orthonormalize/pallas_call | solution.py:387
  (20 shorter events, 0.1 us)
Async XLA Ops:
  0.6 1.6 %copy-start = (s32[256,2048]{1,0:T(8,128)S(1)}, s32[256,2048]{1,0:T(8,128)}, u32[]{:S(2)}) copy-start(s32[256,2048]{1,0:T(8,128)} %words.11) | copy-start | bytes 6291460
  2.2 1.2 %copy-start.2 = (bf16[2048,256]{1,0:T(8,128)(2,1)S(1)}, bf16[2048,256]{1,0:T(8,128)(2,1)}, u32[]{:S(2)}) copy-start(bf16[2048,256]{1,0:T(8,128)(2,1)} %basis.3) | copy-start | bytes 3145732
  4.9 4.7 %collective-permute-start = (f32[6,128,256]{2,1,0:T(8,128)S(1)}, f32[6,128,256]{2,1,0:T(8,128)S(1)}, u32[]{:S(2)}, u32[]{:S(2)}) collective-permute-start(f32[6,128,256]{2,1,0:T(8,128)S(1)} %get-tuple-element.21), channel_id=1, source_target_pairs={{0,1},{1,0},{2,3},{3,2},{4,5},{5,4},{6,7},{7,6},{8,9},{9,8},{10,11... | collective-permute-start | bytes 2359304 | tf_op jit(solution)/shard_map/ppermute | solution.py:401
  5.5 4.2 %collective-permute-start.1 = (f32[8,256]{1,0:T(8,128)S(1)}, f32[8,256]{1,0:T(8,128)S(1)}, u32[]{:S(2)}, u32[]{:S(2)}) collective-permute-start(f32[8,256]{1,0:T(8,128)S(1)} %get-tuple-element.22.sums), channel_id=1, source_target_pairs={{0,2},{1,3},{2,0},{3,1},{4,6},{5,7},{6,4},{7,5},{8,10},{9,11},{10,... | collective-permute-start | bytes 24584 | tf_op jit(solution)/shard_map/ppermute | solution.py:401
  9.0 14.7 %copy-start.1 = (s32[256,2048]{1,0:T(8,128)S(1)}, s32[256,2048]{1,0:T(8,128)}, u32[]{:S(2)}) copy-start(s32[256,2048]{1,0:T(8,128)} %words.11) | copy-start | bytes 6291460
  9.8 11.5 %collective-permute-start.2 = (f32[6,128,128]{2,1,0:T(8,128)S(1)}, f32[6,128,128]{2,1,0:T(8,128)S(1)}, u32[]{:S(2)}, u32[]{:S(2)}) collective-permute-start(f32[6,128,128]{2,1,0:T(8,128)S(1)} %get-tuple-element.23.mine), channel_id=1, source_target_pairs={{0,2},{1,3},{2,0},{3,1},{4,6},{5,7},{6,4},{7,5},{8,10},{9,11},{10,... | collective-permute-start | bytes 1179656 | tf_op jit(solution)/shard_map/ppermute | solution.py:401
  11.8 1.2 %collective-permute-start.3 = (f32[8,256]{1,0:T(8,128)S(1)}, f32[8,256]{1,0:T(8,128)S(1)}, u32[]{:S(2)}, u32[]{:S(2)}) collective-permute-start(f32[8,256]{1,0:T(8,128)S(1)} %get-tuple-element.24), channel_id=1, source_target_pairs={{0,1},{1,0},{2,3},{3,2},{4,5},{5,4},{6,7},{7,6},{8,9},{9,8},{10,11... | collective-permute-start | bytes 24584 | tf_op jit(solution)/shard_map/ppermute | solution.py:401
  13.0 3.7 %collective-permute-start.4 = (f32[8,256]{1,0:T(8,128)S(1)}, f32[8,256]{1,0:T(8,128)S(1)}, u32[]{:S(2)}, u32[]{:S(2)}) collective-permute-start(f32[8,256]{1,0:T(8,128)S(1)} %add.29), channel_id=1, source_target_pairs={{0,4},{4,0},{8,12},{12,8},{1,5},{5,1},{9,13},{13,9},{2,6},{6,2},{1... | collective-permute-start | bytes 24584 | tf_op jit(solution)/shard_map/ppermute | solution.py:401
  16.7 4.5 %collective-permute-start.5 = (f32[8,256]{1,0:T(8,128)S(1)}, f32[8,256]{1,0:T(8,128)S(1)}, u32[]{:S(2)}, u32[]{:S(2)}) collective-permute-start(f32[8,256]{1,0:T(8,128)S(1)} %add.30), channel_id=1, source_target_pairs={{0,8},{4,12},{8,0},{12,4},{1,9},{5,13},{9,1},{13,5},{2,10},{6,14},... | collective-permute-start | bytes 24584 | tf_op jit(solution)/shard_map/ppermute | solution.py:401
  21.2 10.9 %collective-permute-start.10 = (f32[6,128,128]{2,1,0:T(8,128)S(1)}, f32[6,128,128]{2,1,0:T(8,128)S(1)}, u32[]{:S(2)}, u32[]{:S(2)}) collective-permute-start(f32[6,128,128]{2,1,0:T(8,128)S(1)} %get-tuple-element.29.mine), channel_id=1, source_target_pairs={{0,2},{1,3},{2,0},{3,1},{4,6},{5,7},{6,4},{7,5},{8,10},{9,11},{10,... | collective-permute-start | bytes 1179656 | tf_op jit(solution)/shard_map/ppermute | solution.py:401
  22.2 1.5 %collective-permute-start.6 = (bf16[6,128,128]{2,1,0:T(8,128)(2,1)S(1)}, bf16[6,128,128]{2,1,0:T(8,128)(2,1)S(1)}, u32[]{:S(2)}, u32[]{:S(2)}) collective-permute-start(bf16[6,128,128]{2,1,0:T(8,128)(2,1)S(1)} %finish.2.mine), channel_id=1, source_target_pairs={{0,1},{1,0},{2,3},{3,2},{4,5},{5,4},{6,7},{7,6},{8,9},{9,8},{10,11... | collective-permute-start | bytes 589832 | tf_op jit(solution)/shard_map/ppermute | solution.py:401
  24.5 7.7 %collective-permute-start.7 = (s16[528,128]{1,0:T(8,128)(2,1)S(1)}, s16[528,128]{1,0:T(8,128)(2,1)S(1)}, u32[]{:S(2)}, u32[]{:S(2)}) collective-permute-start(s16[528,128]{1,0:T(8,128)(2,1)S(1)} %chunks.5), channel_id=1, source_target_pairs={{0,12},{4,8},{8,4},{12,0},{1,13},{5,9},{9,5},{13,1},{2,14},{6,10},... | collective-permute-start | bytes 405512 | tf_op jit(solution)/shard_map/ppermute | solution.py:401
  32.2 4.3 %collective-permute-start.11 = (bf16[6,128,128]{2,1,0:T(8,128)(2,1)S(1)}, bf16[6,128,128]{2,1,0:T(8,128)(2,1)S(1)}, u32[]{:S(2)}, u32[]{:S(2)}) collective-permute-start(bf16[6,128,128]{2,1,0:T(8,128)(2,1)S(1)} %finish.3.mine), channel_id=1, source_target_pairs={{0,1},{1,0},{2,3},{3,2},{4,5},{5,4},{6,7},{7,6},{8,9},{9,8},{10,11... | collective-permute-start | bytes 589832 | tf_op jit(solution)/shard_map/ppermute | solution.py:401
  32.3 11.0 %collective-permute-start.8 = (s16[528,128]{1,0:T(8,128)(2,1)S(1)}, s16[528,128]{1,0:T(8,128)(2,1)S(1)}, u32[]{:S(2)}, u32[]{:S(2)}) collective-permute-start(s16[528,128]{1,0:T(8,128)(2,1)S(1)} %get-tuple-element.26), channel_id=1, source_target_pairs={{0,8},{4,12},{8,0},{12,4},{1,9},{5,13},{9,1},{13,5},{2,10},{6,14},... | collective-permute-start | bytes 405512 | tf_op jit(solution)/shard_map/ppermute | solution.py:401
  35.9 8.3 %collective-permute-start.9 = (s16[528,128]{1,0:T(8,128)(2,1)S(1)}, s16[528,128]{1,0:T(8,128)(2,1)S(1)}, u32[]{:S(2)}, u32[]{:S(2)}) collective-permute-start(s16[528,128]{1,0:T(8,128)(2,1)S(1)} %get-tuple-element.27), channel_id=1, source_target_pairs={{0,4},{4,0},{8,12},{12,8},{1,5},{5,1},{9,13},{13,9},{2,6},{6,2},{1... | collective-permute-start | bytes 405512 | tf_op jit(solution)/shard_map/ppermute | solution.py:401
  37.3 14.7 %collective-permute-start.12 = (s16[528,128]{1,0:T(8,128)(2,1)S(1)}, s16[528,128]{1,0:T(8,128)(2,1)S(1)}, u32[]{:S(2)}, u32[]{:S(2)}) collective-permute-start(s16[528,128]{1,0:T(8,128)(2,1)S(1)} %chunks.7), channel_id=1, source_target_pairs={{0,8},{4,12},{8,0},{12,4},{1,9},{5,13},{9,1},{13,5},{2,10},{6,14},... | collective-permute-start | bytes 405512 | tf_op jit(solution)/shard_map/ppermute | solution.py:401
  40.4 11.7 %collective-permute-start.13 = (s16[528,128]{1,0:T(8,128)(2,1)S(1)}, s16[528,128]{1,0:T(8,128)(2,1)S(1)}, u32[]{:S(2)}, u32[]{:S(2)}) collective-permute-start(s16[528,128]{1,0:T(8,128)(2,1)S(1)} %get-tuple-element.32), channel_id=1, source_target_pairs={{0,12},{4,8},{8,4},{12,0},{1,13},{5,9},{9,5},{13,1},{2,14},{6,10},... | collective-permute-start | bytes 405512 | tf_op jit(solution)/shard_map/ppermute | solution.py:401
  42.9 9.6 %collective-permute-start.14 = (s16[528,128]{1,0:T(8,128)(2,1)S(1)}, s16[528,128]{1,0:T(8,128)(2,1)S(1)}, u32[]{:S(2)}, u32[]{:S(2)}) collective-permute-start(s16[528,128]{1,0:T(8,128)(2,1)S(1)} %get-tuple-element.33), channel_id=1, source_target_pairs={{0,4},{4,0},{8,12},{12,8},{1,5},{5,1},{9,13},{13,9},{2,6},{6,2},{1... | collective-permute-start | bytes 405512 | tf_op jit(solution)/shard_map/ppermute | solution.py:401
  53.5 1.3 %collective-permute-start.15 = (f32[144,128]{1,0:T(8,128)S(1)}, f32[144,128]{1,0:T(8,128)S(1)}, u32[]{:S(2)}, u32[]{:S(2)}) collective-permute-start(f32[144,128]{1,0:T(8,128)S(1)} %dynamic-slice_bitcast_fusion), channel_id=1, source_target_pairs={{0,1},{1,0},{2,3},{3,2},{4,5},{5,4},{6,7},{7,6},{8,9},{9,8},{10,11... | collective-permute-start | bytes 221192 | tf_op jit(solution)/shard_map/ppermute | solution.py:401
  54.8 4.4 %collective-permute-start.16 = (f32[144,128]{1,0:T(8,128)S(1)}, f32[144,128]{1,0:T(8,128)S(1)}, u32[]{:S(2)}, u32[]{:S(2)}) collective-permute-start(f32[144,128]{1,0:T(8,128)S(1)} %bitcast_add_fusion), channel_id=1, source_target_pairs={{0,2},{1,3},{2,0},{3,1},{4,6},{5,7},{6,4},{7,5},{8,10},{9,11},{10,... | collective-permute-start | bytes 221192 | tf_op jit(solution)/shard_map/ppermute | solution.py:401
  59.3 5.1 %collective-permute-start.17 = (f32[144,128]{1,0:T(8,128)S(1)}, f32[144,128]{1,0:T(8,128)S(1)}, u32[]{:S(2)}, u32[]{:S(2)}) collective-permute-start(f32[144,128]{1,0:T(8,128)S(1)} %add.35), channel_id=1, source_target_pairs={{0,4},{4,0},{8,12},{12,8},{1,5},{5,1},{9,13},{13,9},{2,6},{6,2},{1... | collective-permute-start | bytes 221192 | tf_op jit(solution)/shard_map/ppermute | solution.py:401
  64.4 5.5 %collective-permute-start.18 = (f32[144,128]{1,0:T(8,128)S(1)}, f32[144,128]{1,0:T(8,128)S(1)}, u32[]{:S(2)}, u32[]{:S(2)}) collective-permute-start(f32[144,128]{1,0:T(8,128)S(1)} %add.36), channel_id=1, source_target_pairs={{0,8},{4,12},{8,0},{12,4},{1,9},{5,13},{9,1},{13,5},{2,10},{6,14},... | collective-permute-start | bytes 221192 | tf_op jit(solution)/shard_map/ppermute | solution.py:401
  69.9 1.3 %collective-permute-start.19 = (f32[144,128]{1,0:T(8,128)S(1)}, f32[144,128]{1,0:T(8,128)S(1)}, u32[]{:S(2)}, u32[]{:S(2)}) collective-permute-start(f32[144,128]{1,0:T(8,128)S(1)} %add.37), channel_id=1, source_target_pairs={{0,1},{1,0},{2,3},{3,2},{4,5},{5,4},{6,7},{7,6},{8,9},{9,8},{10,11... | collective-permute-start | bytes 221192 | tf_op jit(solution)/shard_map/ppermute | solution.py:401
